TPU v7x, 512 devices: a whole 4x8x8 slice. The times are simulated.
512 devices in a mesh: context: 32 (over z, y_lo, core), tensor: 16 (over x, y_hi).
Axes of the slice: x: 4, y: 8 (y_hi: 4, y_lo: 2; y = y_hi * 2 + y_lo), z: 8, core: 2. Of those that a mesh axis runs over, the one named last changes fastest.
Arguments:
- x_in: bfloat16 [8192, 8192], P('context', 'tensor'), may hold values from -6 to 6
- grad_out: bfloat16 [8192, 8192], P('context', 'tensor'), may hold values from -6 to 6
- step_size: float32 [128, 8192], P('tensor', 'context'), may hold values from 0 to 1, as said below
- log_decay: float32 [128, 8192], P('tensor', 'context'), may hold values from -1 to 0, as said below
- b_proj: bfloat16 [2048, 8192], P('tensor', 'context'), may hold values from -0.375 to 0.375
- c_proj: bfloat16 [2048, 8192], P('tensor', 'context'), may hold values from -0.375 to 0.375
- w_in: bfloat16 [8192, 4096], P('tensor'), may hold values from -0.125 to 0.125
Outputs:
- grad_input: bfloat16 [4096, 8192], P('tensor', 'context')
- grad_b: bfloat16 [2048, 8192], P('tensor', 'context')
- grad_c: bfloat16 [2048, 8192], P('tensor', 'context')
Inputs may be any that keep to these rules, and one draw needn't show every extreme that they name: `step_size`: every entry is positive. `log_decay`: every entry is below zero.
All inputs are finite; a program needn't handle non-finite values.
Results may differ from a plain program's by a relative error of at most 0.025.
Values may be sent and summed in bfloat16 or wider, within the bound.
No kernel may reach another device: no remote copies, remote signals or barrier semaphores. Data moves between devices by JAX's collectives and lax.ppermute only.
A program may use at most 128 MiB of HBM per device.

v0:
```python
import jax
import jax.numpy as jnp
from jax import lax
from jax.sharding import PartitionSpec as P


def partner(shard, axis, distance):
    return lax.ppermute(shard, axis, [(i, i ^ 1 << distance) for i in range(lax.axis_size(axis))])


def carried_in(shard, axis, combine, identity, reverse):
    length, mine = (lax.axis_size(axis), lax.axis_index(axis))
    everything = jax.tree.map(
        lambda part, kind: lax.all_gather(part.astype(kind), axis),
        shard,
        (jnp.bfloat16, jnp.bfloat16),
    )
    start = jax.tree.map(
        lambda part, zero: jnp.broadcast_to(jnp.asarray(zero, part.dtype), part.shape),
        shard,
        identity,
    )

    def step(k, before):
        at = length - 1 - k if reverse else k
        reached = at > mine if reverse else at < mine
        new = combine(
            before, jax.tree.map(lambda part, own: part[at].astype(own.dtype), everything, shard)
        )
        return jax.tree.map(lambda a, b: jnp.where(reached, a, b), new, before)

    return lax.fori_loop(0, length, step, start)


def chain_step(earlier, later):
    return (earlier[0] * later[1][:, None, None] + later[0], earlier[1] * later[1])


def per_device(x_in, grad_out, step_size, log_decay, b_proj, c_proj, w_in):
    tokens = x_in.shape[0]
    head_count = step_size.shape[0]
    head_width = x_in.shape[1] // head_count
    half_rows = b_proj.shape[0]
    highest = lax.Precision.HIGHEST
    parity = lax.axis_index("tensor") % 2
    leading = parity == 0
    other_b, other_c = partner((b_proj, c_proj), "tensor", 0)
    b_full = jnp.where(
        leading, jnp.concatenate([b_proj, other_b], 0), jnp.concatenate([other_b, b_proj], 0)
    )
    c_full = jnp.where(
        leading, jnp.concatenate([c_proj, other_c], 0), jnp.concatenate([other_c, c_proj], 0)
    )
    heads_x = x_in.reshape(tokens, head_count, head_width)
    heads_dy = grad_out.reshape(tokens, head_count, head_width)
    running = jnp.cumsum(log_decay, axis=1)
    to_end = jnp.exp(running[:, -1:] - running)
    from_start = jnp.exp(running)
    fwd_weight = step_size * to_end
    weighted_x = (fwd_weight.T[:, :, None] * heads_x).astype(jnp.bfloat16)
    finals = jnp.einsum("thp,nt->hpn", weighted_x, b_full, preferred_element_type=jnp.float32)
    weighted_dy = (from_start.T[:, :, None] * heads_dy).astype(jnp.bfloat16)
    reach = jnp.einsum("thp,nt->hpn", weighted_dy, c_full, preferred_element_type=jnp.float32)
    block_decay = jnp.exp(running[:, -1])
    neutral = (jnp.zeros_like(finals), jnp.ones_like(block_decay))
    state_in, _ = carried_in((finals, block_decay), "context", chain_step, neutral, False)
    grad_state, _ = carried_in((reach, block_decay), "context", chain_step, neutral, True)
    position = jnp.arange(tokens)
    causal = position[None, :] >= position[:, None]
    pair_decay = jnp.exp(
        jnp.where(causal[None], running[:, None, :] - running[:, :, None], -jnp.inf)
    )
    intersection = jnp.einsum("thp,shp->hts", heads_x, heads_dy, preferred_element_type=jnp.float32)
    mixing = (pair_decay * intersection * step_size[:, :, None]).astype(jnp.bfloat16)
    pair_score = jnp.einsum("nt,ns->ts", b_full, c_full, preferred_element_type=jnp.float32)
    kernel = (pair_decay * pair_score[None]).astype(jnp.bfloat16)
    local_dx = jnp.einsum("hts,shp->thp", kernel, heads_dy, preferred_element_type=jnp.float32)
    carried = jnp.einsum("nt,hpn->thp", b_full.astype(jnp.float32), grad_state, precision=highest)
    grad_x = (step_size.T[:, :, None] * (local_dx + to_end.T[:, :, None] * carried)).astype(
        jnp.bfloat16
    )
    grad_x = grad_x.reshape(tokens, head_count * head_width)
    b_local = jnp.einsum("hts,ns->nt", mixing, c_full, preferred_element_type=jnp.float32)
    b_carried = jnp.einsum(
        "thp,hpn->nt",
        fwd_weight.T[:, :, None] * heads_x.astype(jnp.float32),
        grad_state,
        precision=highest,
    )
    c_local = jnp.einsum("hts,nt->ns", mixing, b_full, preferred_element_type=jnp.float32)
    c_carried = jnp.einsum(
        "thp,hpn->nt",
        from_start.T[:, :, None] * heads_dy.astype(jnp.float32),
        state_in,
        precision=highest,
    )
    part_b = (b_local + b_carried).astype(jnp.bfloat16)
    part_c = (c_local + c_carried).astype(jnp.bfloat16)
    split_b = part_b.reshape(2, half_rows, tokens)
    split_c = part_c.reshape(2, half_rows, tokens)
    mine_b = jnp.where(leading, split_b[0], split_b[1])
    mine_c = jnp.where(leading, split_c[0], split_c[1])
    send_b = jnp.where(leading, split_b[1], split_b[0])
    send_c = jnp.where(leading, split_c[1], split_c[0])
    got_b, got_c = partner((send_b, send_c), "tensor", 0)
    grad_b = (mine_b.astype(jnp.float32) + got_b.astype(jnp.float32)).astype(jnp.bfloat16)
    grad_c = (mine_c.astype(jnp.float32) + got_c.astype(jnp.float32)).astype(jnp.bfloat16)
    grad_input = lax.psum_scatter(
        lax.dot_general(
            w_in, grad_x, (((0,), (1,)), ((), ())), preferred_element_type=jnp.float32
        ).astype(jnp.bfloat16),
        "tensor",
        scatter_dimension=0,
        tiled=True,
    )
    return (grad_input, grad_b, grad_c)


def solution(mesh):
    placed = (
        P("context", "tensor"),
        P("context", "tensor"),
        P("tensor", "context"),
        P("tensor", "context"),
        P("tensor", "context"),
        P("tensor", "context"),
        P("tensor", None),
    )
    return jax.shard_map(
        per_device,
        mesh=mesh,
        in_specs=placed,
        out_specs=(P("tensor", "context"), P("tensor", "context"), P("tensor", "context")),
        check_vma=False,
    )
```

profile of v0, /device:TPU:1, one launch (start us, length us, event | category | flops | bytes accessed | tf_op | source)
XLA Modules:
  0.0 280.3 jit_solution(15618783674866816149)
XLA Ops:
  7.2 5.0 %collective-permute-start.1 = (bf16[128,256]{1,0:T(8,128)(2,1)}, bf16[128,256]{1,0:T(8,128)(2,1)S(1)}, u32[]{:S(2)}, u32[]{:S(2)}) collective-permute-start(bf16[128,256]{1,0:T(8,128)(2,1)} %param.16), channel_id=1, source_target_pairs={{0,1},{1,0},{2,3},{3,2},{4,5},{5,4},{6,7},{7,6},{8,9},{9,8},{10,11... | collective-permute-start | bytes 196616 | tf_op jit(solution)/shard_map/ppermute | solution.py:8
  12.3 1.3 reduce-window.6
  14.9 1.9 convolution_convert_fusion.2
  16.9 3.6 %collective-permute-start = (bf16[128,256]{1,0:T(8,128)(2,1)}, bf16[128,256]{1,0:T(8,128)(2,1)S(1)}, u32[]{:S(2)}, u32[]{:S(2)}) collective-permute-start(bf16[128,256]{1,0:T(8,128)(2,1)} %param.15), channel_id=1, source_target_pairs={{0,1},{1,0},{2,3},{3,2},{4,5},{5,4},{6,7},{7,6},{8,9},{9,8},{10,11... | collective-permute-start | bytes 196616 | tf_op jit(solution)/shard_map/ppermute | solution.py:8
  24.1 1.3 dynamic-slice
  26.5 61.6 %all-reduce = bf16[256]{0:T(256)(128)(2,1)S(1)} all-reduce(bf16[256]{0:T(256)(128)(2,1)S(1)} %dynamic-update-slice), channel_id=2, replica_groups=mesh['context'=32,'tensor'=16] {'context'}, use_global_device_ids=true, to_apply=%add | all-reduce | flops 256 | bytes 1024
  89.6 9.6 %all-gather.6.cloned.1.call-done = bf16[256,64,256]{2,1,0:T(8,128)(2,1)} async-done(((bf16[8,64,256]{2,1,0:T(8,128)(2,1)}), bf16[256,64,256]{2,1,0:T(8,128)(2,1)}) %all-gather.6.cloned.1.call-update) | async-done | bytes 8388624 | tf_op jit(solution)/shard_map/all_gather | solution.py:14
  99.2 36.7 %while.30 = (s32[]{:T(128)}, f32[8,64,256]{2,1,0:T(8,128)S(1)}, s32[]{:T(128)}, bf16[32,8]{1,0:T(8,128)(2,1)S(1)}, bf16[32,8,64,256]{3,2,1,0:T(8,128)(2,1)}, /*index=5*/s32[]{:T(128)}, s32[]{:T(128)}, s32[]{:T(128)}, s32[]{:T(128)}) while((s32[]{:T(128)}, f32[8,64,256]{2,1,0:T(8,128)S(1)}, s32[]{:T(128)}, ...), condition=%wide.region_3.4_spmd.clone, body=%wide.region_2.3_spmd.clone.sunk | while | flops 655376 | bytes 1310975 | solution.py:32
  101.5 1.1 fusion.40
  103.8 1.1 fusion.40
  106.1 1.1 fusion.40
  108.4 1.1 fusion.40
  109.5 1.1 fusion.40
  111.8 1.1 fusion.40
  114.1 1.1 fusion.40
  116.4 1.1 fusion.40
  118.7 1.1 fusion.40
  121.0 1.1 fusion.40
  124.4 1.1 fusion.40
  125.6 1.1 fusion.40
  126.7 1.1 fusion.40
  130.2 1.1 fusion.40
  131.3 1.1 fusion.40
  133.6 1.1 fusion.40
  137.1 3.9 %collective-permute-start.2 = (bf16[128,256]{1,0:T(8,128)(2,1)S(1)}, bf16[128,256]{1,0:T(8,128)(2,1)S(1)}, u32[]{:S(2)}, u32[]{:S(2)}) collective-permute-start(bf16[128,256]{1,0:T(8,128)(2,1)S(1)} %broadcast_select_fusion.1), channel_id=1, source_target_pairs={{0,1},{1,0},{2,3},{3,2},{4,5},{5,4},{6,7},{7,6},{8,9},{9,8},{10,11... | collective-permute-start | bytes 196616 | tf_op jit(solution)/shard_map/ppermute | solution.py:8
  142.1 1.2 copy-done
  143.3 2.7 fusion.2
  146.0 30.1 %all-gather.8.cloned.1.call-done = bf16[256,64,256]{2,1,0:T(8,128)(2,1)} async-done(((bf16[8,64,256]{2,1,0:T(8,128)(2,1)}), bf16[256,64,256]{2,1,0:T(8,128)(2,1)}) %all-gather.8.cloned.1.call-update) | async-done | bytes 8388624 | tf_op jit(solution)/shard_map/all_gather | solution.py:14
  176.1 36.4 %while.31 = (s32[]{:T(128)}, f32[8,64,256]{2,1,0:T(8,128)S(1)}, s32[]{:T(128)}, bf16[32,8]{1,0:T(8,128)(2,1)S(1)}, bf16[32,8,64,256]{3,2,1,0:T(8,128)(2,1)}, /*index=5*/s32[]{:T(128)}, s32[]{:T(128)}) while((s32[]{:T(128)}, f32[8,64,256]{2,1,0:T(8,128)S(1)}, s32[]{:T(128)}, bf16[32,8]{1,0:T(8,128)(2,1)S(1)}, ...), condition=%wide.region_7.8_spmd.clone, body=%wide.region_6.7_spmd.clone.sunk | while | flops 655372 | bytes 1310913 | solution.py:32
  177.3 1.1 fusion.41
  178.4 1.1 fusion.41
  179.5 1.1 fusion.41
  180.7 1.1 fusion.41
  181.8 1.1 fusion.41
  183.0 1.1 fusion.41
  184.1 1.1 fusion.41
  185.2 1.1 fusion.41
  186.4 1.1 fusion.41
  187.5 1.1 fusion.41
  188.7 1.1 fusion.41
  189.8 1.1 fusion.41
  190.9 1.1 fusion.41
  192.1 1.1 fusion.41
  193.2 1.1 fusion.41
  194.4 1.1 fusion.41
  195.5 1.1 fusion.41
  196.6 1.1 fusion.41
  197.8 1.1 fusion.41
  198.9 1.1 fusion.41
  200.1 1.1 fusion.41
  201.2 1.1 fusion.41
  202.3 1.1 fusion.41
  203.5 1.1 fusion.41
  204.6 1.1 fusion.41
  205.8 1.1 fusion.41
  206.9 1.1 fusion.41
  208.1 1.1 fusion.41
  209.2 1.1 fusion.41
  210.3 1.1 fusion.41
  211.5 1.1 fusion.41
  213.8 3.9 %collective-permute-start.3 = (bf16[128,256]{1,0:T(8,128)(2,1)S(1)}, bf16[128,256]{1,0:T(8,128)(2,1)S(1)}, u32[]{:S(2)}, u32[]{:S(2)}) collective-permute-start(bf16[128,256]{1,0:T(8,128)(2,1)S(1)} %broadcast_select_fusion), channel_id=1, source_target_pairs={{0,1},{1,0},{2,3},{3,2},{4,5},{5,4},{6,7},{7,6},{8,9},{9,8},{10,11... | collective-permute-start | bytes 196616 | tf_op jit(solution)/shard_map/ppermute | solution.py:8
  218.4 5.0 %collective-permute-done.3 = bf16[128,256]{1,0:T(8,128)(2,1)S(1)} collective-permute-done((bf16[128,256]{1,0:T(8,128)(2,1)S(1)}, bf16[128,256]{1,0:T(8,128)(2,1)S(1)}, u32[]{:S(2)}, u32[]{:S(2)}) %collective-permute-start.3) | collective-permute-done | bytes 65568 | tf_op jit(solution)/shard_map/ppermute | solution.py:8
  224.0 48.0 %reduce-scatter.2.cloned.1.call-done = bf16[256,256]{0,1:T(8,128)(2,1)} async-done(((bf16[4096,256]{0,1:T(8,128)(2,1)}), bf16[256,256]{0,1:T(8,128)(2,1)}) %reduce-scatter.2.cloned.1.call-update) | async-done | bytes 131088 | tf_op jit(solution)/shard_map/reduce_scatter | solution.py:108
  272.1 1.7 copy.21
  (125 shorter events, 31.0 us)
Async XLA Ops:
  7.2 15.9 %copy-start.1 = (bf16[128,256]{1,0:T(8,128)(2,1)S(1)}, bf16[128,256]{1,0:T(8,128)(2,1)}, u32[]{:S(2)}) copy-start(bf16[128,256]{1,0:T(8,128)(2,1)} %param.15) | copy-start | bytes 196612
  7.2 81.1 %copy-start.2 = (f32[8,256]{1,0:T(8,128)S(1)}, f32[8,256]{1,0:T(8,128)}, u32[]{:S(2)}) copy-start(f32[8,256]{1,0:T(8,128)} %param.13) | copy-start | bytes 24580
  7.2 92.0 %all-gather.6.cloned.1.call-start = ((), (), s32[]{:S(2)}) async-start(), calls=%async_computation.2 | async-start | bytes 8650752 | tf_op jit(solution)/shard_map/all_gather | solution.py:14
  7.2 7.7 %collective-permute-start.1 = (bf16[128,256]{1,0:T(8,128)(2,1)}, bf16[128,256]{1,0:T(8,128)(2,1)S(1)}, u32[]{:S(2)}, u32[]{:S(2)}) collective-permute-start(bf16[128,256]{1,0:T(8,128)(2,1)} %param.16), channel_id=1, source_target_pairs={{0,1},{1,0},{2,3},{3,2},{4,5},{5,4},{6,7},{7,6},{8,9},{9,8},{10,11... | collective-permute-start | bytes 196616 | tf_op jit(solution)/shard_map/ppermute | solution.py:8
  16.9 159.3 %all-gather.8.cloned.1.call-start = ((), (), s32[]{:S(2)}) async-start(), calls=%async_computation.3 | async-start | bytes 8650752 | tf_op jit(solution)/shard_map/all_gather | solution.py:14
  16.9 6.1 %collective-permute-start = (bf16[128,256]{1,0:T(8,128)(2,1)}, bf16[128,256]{1,0:T(8,128)(2,1)S(1)}, u32[]{:S(2)}, u32[]{:S(2)}) collective-permute-start(bf16[128,256]{1,0:T(8,128)(2,1)} %param.15), channel_id=1, source_target_pairs={{0,1},{1,0},{2,3},{3,2},{4,5},{5,4},{6,7},{7,6},{8,9},{9,8},{10,11... | collective-permute-start | bytes 196616 | tf_op jit(solution)/shard_map/ppermute | solution.py:8
  24.0 65.3 %copy-start.3 = (bf16[128,256]{1,0:T(8,128)(2,1)S(1)}, bf16[128,256]{1,0:T(8,128)(2,1)}, u32[]{:S(2)}) copy-start(bf16[128,256]{1,0:T(8,128)(2,1)} %param.16) | copy-start | bytes 196612
  24.0 248.1 %reduce-scatter.2.cloned.1.call-start = ((), (), s32[]{:S(2)}) async-start(), calls=%async_computation.1 | async-start | bytes 2228224 | tf_op jit(solution)/shard_map/reduce_scatter | solution.py:108
  137.1 80.6 %collective-permute-start.2 = (bf16[128,256]{1,0:T(8,128)(2,1)S(1)}, bf16[128,256]{1,0:T(8,128)(2,1)S(1)}, u32[]{:S(2)}, u32[]{:S(2)}) collective-permute-start(bf16[128,256]{1,0:T(8,128)(2,1)S(1)} %broadcast_select_fusion.1), channel_id=1, source_target_pairs={{0,1},{1,0},{2,3},{3,2},{4,5},{5,4},{6,7},{7,6},{8,9},{9,8},{10,11... | collective-permute-start | bytes 196616 | tf_op jit(solution)/shard_map/ppermute | solution.py:8
  141.0 2.3 copy-start
  213.8 9.6 %collective-permute-start.3 = (bf16[128,256]{1,0:T(8,128)(2,1)S(1)}, bf16[128,256]{1,0:T(8,128)(2,1)S(1)}, u32[]{:S(2)}, u32[]{:S(2)}) collective-permute-start(bf16[128,256]{1,0:T(8,128)(2,1)S(1)} %broadcast_select_fusion), channel_id=1, source_target_pairs={{0,1},{1,0},{2,3},{3,2},{4,5},{5,4},{6,7},{7,6},{8,9},{9,8},{10,11... | collective-permute-start | bytes 196616 | tf_op jit(solution)/shard_map/ppermute | solution.py:8
Sparse Core Ops, SparseCore 0:
  17.0 82.1 all-gather.5
  101.3 74.7 all-gather.7
  180.3 91.7 reduce-scatter.1
where the time goes:
time: 283 us; the launch traced here: 280 us
  waiting for transfers between devices  93.3 us (33%)
  other arithmetic  74.5 us (26%)
  blocking collectives  61.6 us (22%)
  starting transfers between devices  16.5 us (6%)
  between operations  14.6 us (5%)
  matrix products  10.3 us (4%)
  local copies, waits for them, and re-layouts  6.98 us (2%)
    select_n x64, other arithmetic, step(): return jax.tree.map(lambda a, b: jnp.where(reached, a, b), new, before)  70.1 us
    unnamed x1, blocking collectives  61.6 us
    reduce_scatter x1, waiting for transfers between devices, per_device(): lax.psum_scatter(lax.dot_general(w_in, grad_x, (((0,), (1,)), ((), ())),...  48 us
    all_gather x2, waiting for transfers between devices, carried_in(): lax.all_gather(part.astype(kind), axis)  39.7 us
    ppermute x4, starting transfers between devices, partner(): lax.ppermute(shard, axis, [(i, i ^ 1 << distance) for i in range(lax.axis...  16.4 us
    unnamed x14, local copies, waits for them, and re-layouts  6.54 us
  transfers between devices with their start and end apart: 7, of which 5 were waited for; matrix products, arithmetic and copies ran while one was open for 31% of the time, Pallas kernels for 0%

commit v1 on v0

v1 whole, which is shorter than its diff:
```python
import jax
import jax.numpy as jnp
from jax import lax
from jax.experimental import pallas as pl
from jax.experimental.pallas import tpu as pltpu
from jax.sharding import Mesh, PartitionSpec as P

CONTEXT = ("z", "yl", "core")
TENSOR = ("x", "yh")
F32 = jnp.float32
BF16 = jnp.bfloat16
HEADS = 8
WIDTH = 64
TOKENS = 256
STATE = 256
COLS = HEADS * WIDTH
BLOCKS = 32
LINES = STATE // BLOCKS


def call(body, outs, scratch=(), smem=0, flops=0):
    vmem = pl.BlockSpec(memory_space=pltpu.VMEM)
    scalar = pl.BlockSpec(memory_space=pltpu.SMEM)

    def run(*args):
        return pl.pallas_call(
            body,
            out_shape=[jax.ShapeDtypeStruct(s, d) for s, d in outs],
            in_specs=[scalar] * smem + [vmem] * (len(args) - smem),
            out_specs=[vmem] * len(outs),
            scratch_shapes=list(scratch),
            compiler_params=pltpu.CompilerParams(vmem_limit_bytes=40 * 1024 * 1024),
            cost_estimate=pl.CostEstimate(flops=flops, bytes_accessed=2**20, transcendentals=0),
        )(*args)

    return run


def iota(shape, dim):
    return lax.broadcasted_iota(jnp.int32, shape, dim)


def dot(a, b, ca, cb):
    return lax.dot_general(a, b, (((ca,), (cb,)), ((), ())), preferred_element_type=F32)


def split3(v):
    hi = v.astype(BF16).astype(F32)
    mid = (v - hi).astype(BF16).astype(F32)
    low = (v - hi - mid).astype(BF16).astype(F32)
    return hi, mid, low


def pair(cols, at, lane):
    return jnp.where(lane < WIDTH, cols[:, at : at + 1], cols[:, at + 1 : at + 2])


def pair_decay(run, cols, h):
    diff = run[h : h + 1, :] - cols[:, h : h + 1]
    causal = iota((TOKENS, TOKENS), 1) >= iota((TOKENS, TOKENS), 0)
    return jnp.exp(jnp.where(causal, diff, -jnp.inf))


def local_body(x_ref, dy_ref, dt_ref, ld_ref, wx_ref, wdy_ref, ms_ref, run_ref, cols_ref, ext_ref):
    tri = jnp.where(iota((TOKENS, TOKENS), 0) <= iota((TOKENS, TOKENS), 1), 1.0, 0.0).astype(BF16)
    parts = jnp.concatenate(split3(ld_ref[...]), axis=0).astype(BF16)
    sums = dot(parts, tri, 1, 0)
    run = sums[:HEADS] + sums[HEADS : 2 * HEADS] + sums[2 * HEADS :]
    run_ref[...] = run
    dt = dt_ref[...]
    end = run[:, TOKENS - 1 :]
    fwd = dt * jnp.exp(end - run)
    start = jnp.exp(run)
    stack = jnp.concatenate(
        [run, dt, fwd, start, jnp.zeros((128 - 4 * HEADS, TOKENS), F32)], axis=0
    )
    cols = stack.T
    cols_ref[...] = cols

    hi, mid, low = split3(jnp.exp(end))
    lane8, row8 = iota((HEADS, 128), 1), iota((HEADS, 128), 0)
    spread = jnp.where(lane8 == row8, hi, 0.0)
    spread = spread + jnp.where(lane8 == row8 + HEADS, mid, 0.0)
    spread = spread + jnp.where(lane8 == row8 + 2 * HEADS, low, 0.0)
    ext_ref[...] = jnp.sum(spread, axis=0, keepdims=True)

    lane = iota((TOKENS, 128), 1)
    total = jnp.zeros((TOKENS, TOKENS), F32)
    for i in range(HEADS // 2):
        at = slice(128 * i, 128 * (i + 1))
        xp, dyp = x_ref[:, at], dy_ref[:, at]
        wx_ref[:, at] = (pair(cols, 2 * HEADS + 2 * i, lane) * xp.astype(F32)).astype(BF16)
        wdy_ref[:, at] = (pair(cols, 3 * HEADS + 2 * i, lane) * dyp.astype(F32)).astype(BF16)
        for k in range(2):
            h = 2 * i + k
            own = (lane < WIDTH) if k == 0 else (lane >= WIDTH)
            inter = dot(jnp.where(own, xp, jnp.zeros_like(xp)), dyp, 1, 1)
            decay = pair_decay(run, cols, h)
            mixing = (decay * inter * cols[:, HEADS + h : HEADS + h + 1]).astype(BF16)
            total = total + mixing.astype(F32)
    ms_ref[...] = total.astype(BF16)


def ends_body(parity_ref, b_ref, c_ref, bc_ref, wx_ref, wdy_ref, ext_ref, bf_ref, cf_ref, send_ref):
    half = STATE // 2
    mine = pl.multiple_of(parity_ref[0] * half, half)
    other = pl.multiple_of((1 - parity_ref[0]) * half, half)
    bf_ref[pl.ds(mine, half), :] = b_ref[...]
    bf_ref[pl.ds(other, half), :] = bc_ref[:half, :]
    cf_ref[pl.ds(mine, half), :] = c_ref[...]
    cf_ref[pl.ds(other, half), :] = bc_ref[half:, :]
    send_ref[:, :COLS] = dot(bf_ref[...], wx_ref[...], 1, 0).astype(BF16)
    send_ref[:, COLS : 2 * COLS] = dot(cf_ref[...], wdy_ref[...], 1, 0).astype(BF16)
    send_ref[:, 2 * COLS :] = jnp.broadcast_to(ext_ref[...], (STATE, 128)).astype(BF16)


def scan_body(got_ref, out_ref, decay_ref):
    source, target = iota((128, COLS), 0), iota((128, COLS), 1)
    expand = (source < 3 * HEADS) & (source % HEADS == target // WIDTH)
    expand = jnp.where(expand, 1.0, 0.0).astype(BF16)
    decay_ref[...] = dot(got_ref[:, 2 * COLS :], expand, 1, 0)
    two = 2 * LINES
    state = jnp.zeros((LINES, COLS), F32)
    for c in range(BLOCKS // 2):
        at = slice(c * two, (c + 1) * two)
        term, decay = got_ref[at, :COLS].astype(F32), decay_ref[at, :]
        after = state * decay[:LINES] + term[:LINES]
        out_ref[at, :COLS] = jnp.concatenate([state, after], axis=0).astype(BF16)
        state = after * decay[LINES:] + term[LINES:]
    state = jnp.zeros((LINES, COLS), F32)
    for c in range(BLOCKS // 2 - 1, -1, -1):
        at = slice(c * two, (c + 1) * two)
        term, decay = got_ref[at, COLS : 2 * COLS].astype(F32), decay_ref[at, :]
        before = state * decay[LINES:] + term[LINES:]
        out_ref[at, COLS:] = jnp.concatenate([before, state], axis=0).astype(BF16)
        state = before * decay[:LINES] + term[:LINES]


def grad_x_body(dy_ref, bf_ref, cf_ref, run_ref, cols_ref, states_ref, gx_ref):
    run, cols = run_ref[...], cols_ref[...]
    bt = bf_ref[...].T
    score = dot(bt, cf_ref[...], 1, 0)
    lane = iota((TOKENS, 128), 1)
    for i in range(HEADS // 2):
        at = slice(128 * i, 128 * (i + 1))
        dyp = dy_ref[:, at]
        local = []
        for k in range(2):
            kernel = (pair_decay(run, cols, 2 * i + k) * score).astype(BF16)
            local.append(dot(kernel, dyp, 1, 0))
        local = jnp.where(lane < WIDTH, local[0], local[1])
        carried = dot(bt, states_ref[:, COLS + 128 * i : COLS + 128 * (i + 1)], 1, 0)
        dt, fwd = pair(cols, HEADS + 2 * i, lane), pair(cols, 2 * HEADS + 2 * i, lane)
        gx_ref[:, at] = (dt * local + fwd * carried).astype(BF16)


def grad_bc_body(parity_ref, bf_ref, cf_ref, ms_ref, wx_ref, wdy_ref, states_ref, mine_ref, send_ref, pb_ref, pc_ref):
    half = STATE // 2
    pb_ref[...] = (
        dot(cf_ref[...], ms_ref[...], 1, 1) + dot(states_ref[:, COLS:], wx_ref[...], 1, 1)
    ).astype(BF16)
    pc_ref[...] = (
        dot(bf_ref[...], ms_ref[...], 1, 0) + dot(states_ref[:, :COLS], wdy_ref[...], 1, 1)
    ).astype(BF16)
    mine = pl.multiple_of(parity_ref[0] * half, half)
    other = pl.multiple_of((1 - parity_ref[0]) * half, half)
    mine_ref[:half, :] = pb_ref[pl.ds(mine, half), :]
    mine_ref[half:, :] = pc_ref[pl.ds(mine, half), :]
    send_ref[:half, :] = pb_ref[pl.ds(other, half), :]
    send_ref[half:, :] = pc_ref[pl.ds(other, half), :]


def add_bc_body(mine_ref, got_ref, gb_ref, gc_ref):
    half = STATE // 2
    total = (mine_ref[...].astype(F32) + got_ref[...].astype(F32)).astype(BF16)
    gb_ref[...] = total[:half]
    gc_ref[...] = total[half:]


def project_body(gx_ref, w_ref, out_ref):
    tile = out_ref.shape[2]
    for j in range(out_ref.shape[0]):
        out_ref[j] = dot(gx_ref[...], w_ref[:, j * tile : (j + 1) * tile], 1, 0).astype(BF16)


def add_x_body(got_ref, out_ref):
    total = got_ref[0].astype(F32)
    for k in range(1, got_ref.shape[0]):
        total = total + got_ref[k].astype(F32)
    out_ref[...] = total.astype(BF16)


def add_y_body(got_ref, out_ref):
    total = got_ref[0].astype(F32)
    for k in range(1, got_ref.shape[0]):
        total = total + got_ref[k].astype(F32)
    out_ref[...] = total.T.astype(BF16)


def per_device(x_in, grad_out, step_size, log_decay, b_proj, c_proj, w_in):
    parity = (lax.axis_index("yh") % 2).reshape(1)
    flip = [(i, i ^ 1) for i in range(lax.axis_size("yh"))]
    bc = lax.ppermute(jnp.concatenate([b_proj, c_proj], axis=0), "yh", flip)

    square = (TOKENS, TOKENS)
    wide = (TOKENS, COLS)
    wx, wdy, mixed, run, cols, ext = call(
        local_body,
        [(wide, BF16), (wide, BF16), (square, BF16), ((HEADS, TOKENS), F32), ((TOKENS, 128), F32), ((1, 128), F32)],
        flops=10**9,
    )(x_in, grad_out, step_size, log_decay)
    b_full, c_full, send = call(
        ends_body,
        [(square, BF16), (square, BF16), ((STATE, 2 * COLS + 128), BF16)],
        smem=1,
        flops=10**9,
    )(parity, b_proj, c_proj, bc, wx, wdy, ext)
    got = lax.all_to_all(send, CONTEXT, 0, 0, tiled=True)
    (scanned,) = call(
        scan_body, [((STATE, 2 * COLS), BF16)], [pltpu.VMEM((STATE, COLS), F32)], flops=10**9
    )(got)
    states = lax.all_to_all(scanned, CONTEXT, 0, 0, tiled=True)

    (gx,) = call(grad_x_body, [(wide, BF16)], flops=10**9)(grad_out, b_full, c_full, run, cols, states)
    (partial,) = call(project_body, [((16, TOKENS, TOKENS), BF16)], flops=10**9)(gx, w_in)
    over_x = lax.all_to_all(partial, "x", 0, 0, tiled=True)

    mine, send_bc = call(
        grad_bc_body,
        [(square, BF16), (square, BF16)],
        [pltpu.VMEM(square, BF16), pltpu.VMEM(square, BF16)],
        smem=1,
        flops=10**9,
    )(parity, b_full, c_full, mixed, wx, wdy, states)
    got_bc = lax.ppermute(send_bc, "yh", flip)

    (summed,) = call(add_x_body, [((4, TOKENS, TOKENS), BF16)], flops=10**8)(
        over_x.reshape(4, 4, TOKENS, TOKENS)
    )
    over_y = lax.all_to_all(summed, "yh", 0, 0, tiled=True)
    (grad_input,) = call(add_y_body, [(square, BF16)], flops=10**8)(over_y)
    grad_b, grad_c = call(add_bc_body, [((128, TOKENS), BF16)] * 2, flops=10**8)(mine, got_bc)
    return grad_input, grad_b, grad_c


def solution(mesh):
    fine = Mesh(mesh.devices.reshape(8, 2, 2, 4, 4), CONTEXT + TENSOR)
    by_token, by_head = P(CONTEXT, TENSOR), P(TENSOR, CONTEXT)
    return jax.shard_map(
        per_device,
        mesh=fine,
        in_specs=(by_token, by_token, by_head, by_head, by_head, by_head, P(TENSOR, None)),
        out_specs=(by_head, by_head, by_head),
        check_vma=False,
    )
```

time: 283 us -> 125 us (0.44)
  the two profiles are of different devices: /device:TPU:1 before, /device:TPU:57 now
where the time goes in v1:
time: 125 us
  blocking collectives  81.7 us (65%)
  waiting for transfers between devices  16.4 us (13%)
  starting transfers between devices  14 us (11%)
  Pallas kernels  7.43 us (6%)
  local copies, waits for them, and re-layouts  3.31 us (3%)
    all_to_all x1, blocking collectives, per_device(): got = lax.all_to_all(send, CONTEXT, 0, 0, tiled=True)  31.1 us
    all_to_all x1, blocking collectives, per_device(): over_x = lax.all_to_all(partial, 'x', 0, 0, tiled=True)  29.1 us
    all_to_all x1, blocking collectives, per_device(): states = lax.all_to_all(scanned, CONTEXT, 0, 0, tiled=True)  21.5 us
    ppermute x1, waiting for transfers between devices, per_device(): got_bc = lax.ppermute(send_bc, 'yh', flip)  14.9 us
    pallas_call x9, Pallas kernels, run(): pl.pallas_call(body, out_shape=[jax.ShapeDtypeStruct(s, d) for s, d in ou...  7.43 us
    all_to_all x1, starting transfers between devices, per_device(): over_y = lax.all_to_all(summed, 'yh', 0, 0, tiled=True)  6.29 us
    ppermute x1, starting transfers between devices, per_device(): got_bc = lax.ppermute(send_bc, 'yh', flip)  3.99 us
    ppermute x1, starting transfers between devices, per_device(): bc = lax.ppermute(jnp.concatenate([b_proj, c_proj], axis=0), 'yh', flip)  3.76 us
  transfers between devices with their start and end apart: 3, of which 2 were waited for; matrix products, arithmetic and copies ran while one was open for 0% of the time, Pallas kernels for 2%

profile of v1, /device:TPU:57, one launch (start us, length us, event | category | flops | bytes accessed | tf_op | source)
XLA Modules:
  0.0 124.5 jit_solution(7528943592636173526)
XLA Ops:
  0.6 0.0 copy-start.2
  0.6 0.0 copy-start.1
  0.7 0.9 pad_maximum_fusion
  1.6 3.8 %collective-permute-start = (bf16[256,256]{1,0:T(8,128)(2,1)S(1)}, bf16[256,256]{1,0:T(8,128)(2,1)S(1)}, u32[]{:S(2)}, u32[]{:S(2)}) collective-permute-start(bf16[256,256]{1,0:T(8,128)(2,1)S(1)} %pad_maximum_fusion), channel_id=1, source_target_pairs={{0,1},{1,0},{2,3},{3,2},{4,5},{5,4},{6,7},{7,6},{8,9},{9,8},{10,11... | collective-permute-start | bytes 393224 | tf_op jit(solution)/shard_map/ppermute | solution.py:203
  5.3 0.0 copy-start.3
  5.4 0.9 copy-done.3
  6.3 0.0 copy-start.4
  6.3 0.9 copy-done.4
  7.3 0.0 copy-start.6
  7.3 0.7 copy-done.6
  8.0 0.0 copy-start.7
  8.0 0.7 copy-done.7
  8.6 1.6 %shard_map.94 = (bf16[256,512]{1,0:T(8,128)(2,1)S(1)}, bf16[256,512]{1,0:T(8,128)(2,1)S(1)}, bf16[256,256]{1,0:T(8,128)(2,1)S(1)}, f32[8,256]{1,0:T(8,128)S(1)},...) custom-call(bf16[256,512]{1,0:T(8,128)(2,1)S(1)} %copy-done.3, bf16[256,512]{1,0:T(8,128)(2,1)S(1)} %copy-done.4, ...), custom_call_target="tpu_custom_call" | custom-call | flops 1000000000 | bytes 1048576 | tf_op jit(solution)/shard_map/pallas_call | solution.py:26
  10.2 1.5 %collective-permute-done.bc_ref = bf16[256,256]{1,0:T(8,128)(2,1)S(1)} collective-permute-done((bf16[256,256]{1,0:T(8,128)(2,1)S(1)}, bf16[256,256]{1,0:T(8,128)(2,1)S(1)}, u32[]{:S(2)}, u32[]{:S(2)}) %collective-permute-start) | collective-permute-done | bytes 131104 | tf_op jit(solution)/shard_map/ppermute | solution.py:203
  11.8 0.0 copy-done.2
  11.8 0.0 copy-done.1
  11.8 0.3 shard_map.95
  12.1 31.1 %all_to_all.32 = bf16[32,8,1152]{2,1,0:T(8,128)(2,1)S(1)} all-to-all(bf16[32,8,1152]{2,1,0:T(8,128)(2,1)S(1)} %bitcast.7), channel_id=1, replica_groups=mesh['z'=8,'yl'=2,'core'=2,'x'=4,'yh'=4] {'z','yl','core'}, dimensions={0} | all-to-all | bytes 1179648 | tf_op jit(solution)/shard_map/all_to_all | solution.py:218
  43.2 0.0 copy-start.5
  43.2 0.3 shard_map.96
  43.4 0.0 copy-start
  43.4 21.5 %all_to_all.33 = bf16[32,8,1024]{2,1,0:T(8,128)(2,1)S(1)} all-to-all(bf16[32,8,1024]{2,1,0:T(8,128)(2,1)S(1)} %bitcast.11), channel_id=1, replica_groups=mesh['z'=8,'yl'=2,'core'=2,'x'=4,'yh'=4] {'z','yl','core'}, dimensions={0} | all-to-all | bytes 1048576 | tf_op jit(solution)/shard_map/all_to_all | solution.py:222
  65.0 0.0 copy-done.5
  65.0 1.1 shard_map.97.gx_ref
  66.1 0.0 copy-done
  66.1 1.3 %shard_map.98 = bf16[16,256,256]{2,1,0:T(8,128)(2,1)S(1)} custom-call(bf16[256,512]{1,0:T(8,128)(2,1)S(1)} %shard_map.97.gx_ref, bf16[512,4096]{1,0:T(8,128)(2,1)S(1)} %copy-done), custom_call_target="tpu_custom_call" | custom-call | flops 1000000000 | bytes 1048576 | tf_op jit(solution)/shard_map/pallas_call | solution.py:26
  67.4 29.1 %all_to_all.34 = bf16[16,256,256]{2,1,0:T(8,128)(2,1)S(1)} all-to-all(bf16[16,256,256]{2,1,0:T(8,128)(2,1)S(1)} %shard_map.98), channel_id=1, replica_groups=mesh['z'=8,'yl'=2,'core'=2,'x'=4,'yh'=4] {'x'}, dimensions={0} | all-to-all | bytes 4194304 | tf_op jit(solution)/shard_map/all_to_all | solution.py:226
  96.5 1.0 shard_map.99
  97.5 6.3 %all-to-all-start.3 = ((bf16[4,256,256]{2,1,0:T(8,128)(2,1)}), bf16[4,256,256]{2,1,0:T(8,128)(2,1)S(1)}, u32[]{:S(2)}, u32[]{:S(2)}) async-start(bf16[4,256,256]{2,1,0:T(8,128)(2,1)} %shard_map.99), calls=%async_computation.3 | async-start | bytes 1048576 | tf_op jit(solution)/shard_map/all_to_all | solution.py:240
  103.8 0.4 shard_map.101
  104.2 4.0 %collective-permute-start.1 = (bf16[256,256]{1,0:T(8,128)(2,1)S(1)}, bf16[256,256]{1,0:T(8,128)(2,1)S(1)}, u32[]{:S(2)}, u32[]{:S(2)}) collective-permute-start(bf16[256,256]{1,0:T(8,128)(2,1)S(1)} %get-tuple-element.26), channel_id=1, source_target_pairs={{0,1},{1,0},{2,3},{3,2},{4,5},{5,4},{6,7},{7,6},{8,9},{9,8},{10,11... | collective-permute-start | bytes 393224 | tf_op jit(solution)/shard_map/ppermute | solution.py:235
  108.2 14.9 %collective-permute-done.1.got_ref = bf16[256,256]{1,0:T(8,128)(2,1)S(1)} collective-permute-done((bf16[256,256]{1,0:T(8,128)(2,1)S(1)}, bf16[256,256]{1,0:T(8,128)(2,1)S(1)}, u32[]{:S(2)}, u32[]{:S(2)}) %collective-permute-start.1) | collective-permute-done | bytes 131104 | tf_op jit(solution)/shard_map/ppermute | solution.py:235
  123.1 0.7 shard_map.102
  123.7 0.0 all-to-all-done.3.got_ref
  123.7 0.8 shard_map.100
Async XLA Ops:
  0.6 11.2 %copy-start.2 = (bf16[128,256]{1,0:T(8,128)(2,1)S(1)}, bf16[128,256]{1,0:T(8,128)(2,1)}, u32[]{:S(2)}) copy-start(bf16[128,256]{1,0:T(8,128)(2,1)} %c_ref.1) | copy-start | bytes 196612
  0.6 11.1 %copy-start.1 = (bf16[128,256]{1,0:T(8,128)(2,1)S(1)}, bf16[128,256]{1,0:T(8,128)(2,1)}, u32[]{:S(2)}) copy-start(bf16[128,256]{1,0:T(8,128)(2,1)} %b_ref.1) | copy-start | bytes 196612
  1.6 10.2 %collective-permute-start = (bf16[256,256]{1,0:T(8,128)(2,1)S(1)}, bf16[256,256]{1,0:T(8,128)(2,1)S(1)}, u32[]{:S(2)}, u32[]{:S(2)}) collective-permute-start(bf16[256,256]{1,0:T(8,128)(2,1)S(1)} %pad_maximum_fusion), channel_id=1, source_target_pairs={{0,1},{1,0},{2,3},{3,2},{4,5},{5,4},{6,7},{7,6},{8,9},{9,8},{10,11... | collective-permute-start | bytes 393224 | tf_op jit(solution)/shard_map/ppermute | solution.py:203
  5.3 1.0 copy-start.3
  6.3 0.9 copy-start.4
  7.3 0.7 copy-start.6
  8.0 0.7 copy-start.7
  43.2 21.8 %copy-start.5 = (bf16[256,512]{1,0:T(8,128)(2,1)S(1)}, bf16[256,512]{1,0:T(8,128)(2,1)}, u32[]{:S(2)}) copy-start(bf16[256,512]{1,0:T(8,128)(2,1)} %dy_ref.3) | copy-start | bytes 786436
  43.4 22.7 %copy-start = (bf16[512,4096]{1,0:T(8,128)(2,1)S(1)}, bf16[512,4096]{1,0:T(8,128)(2,1)}, u32[]{:S(2)}) copy-start(bf16[512,4096]{1,0:T(8,128)(2,1)} %w_ref.1) | copy-start | bytes 12582916
  97.5 26.2 %all-to-all-start.3 = ((bf16[4,256,256]{2,1,0:T(8,128)(2,1)}), bf16[4,256,256]{2,1,0:T(8,128)(2,1)S(1)}, u32[]{:S(2)}, u32[]{:S(2)}) async-start(bf16[4,256,256]{2,1,0:T(8,128)(2,1)} %shard_map.99), calls=%async_computation.3 | async-start | bytes 1048576 | tf_op jit(solution)/shard_map/all_to_all | solution.py:240
  104.2 18.9 %collective-permute-start.1 = (bf16[256,256]{1,0:T(8,128)(2,1)S(1)}, bf16[256,256]{1,0:T(8,128)(2,1)S(1)}, u32[]{:S(2)}, u32[]{:S(2)}) collective-permute-start(bf16[256,256]{1,0:T(8,128)(2,1)S(1)} %get-tuple-element.26), channel_id=1, source_target_pairs={{0,1},{1,0},{2,3},{3,2},{4,5},{5,4},{6,7},{7,6},{8,9},{9,8},{10,11... | collective-permute-start | bytes 393224 | tf_op jit(solution)/shard_map/ppermute | solution.py:235

commit v2 on v1

v2 whole, which is shorter than its diff:
```python
import jax
import jax.numpy as jnp
from jax import lax
from jax.experimental import pallas as pl
from jax.experimental.pallas import tpu as pltpu
from jax.sharding import Mesh, PartitionSpec as P

CONTEXT = ("z", "yl", "core")
TENSOR = ("x", "yh")
F32 = jnp.float32
BF16 = jnp.bfloat16
HEADS = 8
WIDTH = 64
TOKENS = 256
STATE = 256
COLS = HEADS * WIDTH
HALF = STATE // 2
BLOCKS = 32
LINES = STATE // BLOCKS


SPACES = {
    "s": pl.BlockSpec(memory_space=pltpu.SMEM),
    "v": pl.BlockSpec(memory_space=pltpu.VMEM),
    "V": pl.BlockSpec(memory_space=pltpu.VMEM),
    "b": pl.BlockSpec(memory_space=pltpu.VMEM),
    "h": pl.BlockSpec(memory_space=pltpu.HBM),
    "a": pl.BlockSpec(memory_space=pl.ANY),
}
PLACES = {"h": pltpu.HBM, "b": pltpu.HBM, "V": pltpu.VMEM}
PASS_FLOPS = 2 * 10**10
LIMIT = 16 * 1024 * 1024


def call(body, spaces, outs, scratch=(), copies=0, out_spaces="", flops=10**9):
    run = pl.pallas_call(
        body,
        out_shape=[
            PLACES[k](s, d) if k in PLACES else jax.ShapeDtypeStruct(s, d)
            for (s, d), k in zip(outs, out_spaces or "V" * len(outs))
        ],
        in_specs=[SPACES[k] for k in spaces],
        out_specs=[SPACES[k] for k in out_spaces or "V" * len(outs)],
        scratch_shapes=[pltpu.VMEM(s, d) for s, d in scratch]
        + ([pltpu.SemaphoreType.DMA((copies,))] if copies else []),
        compiler_params=pltpu.CompilerParams(vmem_limit_bytes=LIMIT),
        cost_estimate=pl.CostEstimate(flops=flops, bytes_accessed=2**20, transcendentals=0),
    )

    def pinned(*args):
        return run(
            *(pltpu.with_memory_space_constraint(a, PLACES[k]) if k in PLACES else a for a, k in zip(args, spaces))
        )

    return pinned


def fetch(pairs, sems):
    copies = [pltpu.make_async_copy(a, b, sems.at[i]) for i, (a, b) in enumerate(pairs)]
    for copy in copies:
        copy.start()
    return copies


def iota(shape, dim):
    return lax.broadcasted_iota(jnp.int32, shape, dim)


def dot(a, b, ca, cb):
    return lax.dot_general(a, b, (((ca,), (cb,)), ((), ())), preferred_element_type=F32)


def split3(v):
    hi = v.astype(BF16).astype(F32)
    mid = (v - hi).astype(BF16).astype(F32)
    low = (v - hi - mid).astype(BF16).astype(F32)
    return hi, mid, low


def pair(cols, at, lane):
    return jnp.where(lane < WIDTH, cols[:, at : at + 1], cols[:, at + 1 : at + 2])


def pair_decay(run, cols, h):
    diff = run[h : h + 1, :] - cols[:, h : h + 1]
    causal = iota((TOKENS, TOKENS), 1) >= iota((TOKENS, TOKENS), 0)
    return jnp.exp(jnp.where(causal, diff, -jnp.inf))


def expanded(ext):
    source, target = iota((128, COLS), 0), iota((128, COLS), 1)
    spread = (source < 3 * HEADS) & (source % HEADS == target // WIDTH)
    return dot(ext, jnp.where(spread, 1.0, 0.0).astype(BF16), 1, 0)


def local_body(
    where_ref, x_hbm, dy_hbm, dt_hbm, ld_hbm, b_hbm, c_hbm, w_hbm,
    wx_ref, wdy_ref, ms_ref, run_ref, cols_ref, ext_ref, b_ref, c_ref, w1_hbm, w3_hbm, w2_hbm,
    x_ref, dy_ref, dt_ref, ld_ref, w_ref, sems,
):
    rows, share = w1_hbm.shape
    down = pl.ds(pl.multiple_of(where_ref[0] * rows, rows), rows)
    pieces = [(ld_hbm, ld_ref), (dt_hbm, dt_ref), (x_hbm, x_ref), (dy_hbm, dy_ref), (b_hbm, b_ref), (c_hbm, c_ref)]
    for i, ahead in enumerate((1, 3, 2)):
        across = pl.ds(pl.multiple_of(lax.rem(where_ref[1] + ahead, 4) * share, share), share)
        pieces.append((w_hbm.at[down, across], w_ref.at[i]))
    late = fetch(pieces, sems)
    late[0].wait()
    tri = jnp.where(iota((TOKENS, TOKENS), 0) <= iota((TOKENS, TOKENS), 1), 1.0, 0.0).astype(BF16)
    parts = jnp.concatenate(split3(ld_ref[...]), axis=0).astype(BF16)
    sums = dot(parts, tri, 1, 0)
    run = sums[:HEADS] + sums[HEADS : 2 * HEADS] + sums[2 * HEADS :]
    run_ref[...] = run
    late[1].wait()
    dt = dt_ref[...]
    end = run[:, TOKENS - 1 :]
    fwd = dt * jnp.exp(end - run)
    start = jnp.exp(run)
    stack = jnp.concatenate(
        [run, dt, fwd, start, jnp.zeros((128 - 4 * HEADS, TOKENS), F32)], axis=0
    )
    cols = stack.T
    cols_ref[...] = cols

    hi, mid, low = split3(jnp.exp(end))
    lane8, row8 = iota((HEADS, 128), 1), iota((HEADS, 128), 0)
    spread = jnp.where(lane8 == row8, hi, 0.0)
    spread = spread + jnp.where(lane8 == row8 + HEADS, mid, 0.0)
    spread = spread + jnp.where(lane8 == row8 + 2 * HEADS, low, 0.0)
    ext_ref[...] = jnp.sum(spread, axis=0, keepdims=True)

    late[2].wait()
    late[3].wait()
    lane = iota((TOKENS, 128), 1)
    total = jnp.zeros((TOKENS, TOKENS), F32)
    for i in range(HEADS // 2):
        if i == HEADS // 2 - 2:
            for copy in late[4:]:
                copy.wait()
            out = [pltpu.make_async_copy(w_ref.at[k], w, sems.at[9 + k]) for k, w in enumerate((w1_hbm, w3_hbm, w2_hbm))]
            for copy in out:
                copy.start()
        at = slice(128 * i, 128 * (i + 1))
        xp, dyp = x_ref[:, at], dy_ref[:, at]
        wx_ref[:, at] = (pair(cols, 2 * HEADS + 2 * i, lane) * xp.astype(F32)).astype(BF16)
        wdy_ref[:, at] = (pair(cols, 3 * HEADS + 2 * i, lane) * dyp.astype(F32)).astype(BF16)
        for k in range(2):
            h = 2 * i + k
            own = (lane < WIDTH) if k == 0 else (lane >= WIDTH)
            inter = dot(jnp.where(own, xp, jnp.zeros_like(xp)), dyp, 1, 1)
            decay = pair_decay(run, cols, h)
            mixing = (decay * inter * cols[:, HEADS + h : HEADS + h + 1]).astype(BF16)
            total = total + mixing.astype(F32)
    ms_ref[...] = total.astype(BF16)
    for copy in out:
        copy.wait()


def whole(own_ref, other):
    return jnp.concatenate([own_ref[...], other], axis=0)


def ends_body(b_ref, c_ref, bc_ref, wx_ref, wdy_ref, ext_ref, send_ref):
    send_ref[:, :COLS] = dot(whole(b_ref, bc_ref[:HALF]), wx_ref[...], 1, 0).astype(BF16)
    send_ref[:, COLS : 2 * COLS] = dot(whole(c_ref, bc_ref[HALF:]), wdy_ref[...], 1, 0).astype(BF16)
    send_ref[:, 2 * COLS :] = jnp.broadcast_to(ext_ref[...], (STATE, 128)).astype(BF16)


def scan_body(got_ref, out_ref, decay_ref):
    decay_ref[...] = expanded(got_ref[:, 2 * COLS :])
    two = 2 * LINES
    state = jnp.zeros((LINES, COLS), F32)
    for c in range(BLOCKS // 2):
        at = slice(c * two, (c + 1) * two)
        term, decay = got_ref[at, :COLS].astype(F32), decay_ref[at, :]
        after = state * decay[:LINES] + term[:LINES]
        out_ref[at, :COLS] = jnp.concatenate([state, after], axis=0).astype(BF16)
        state = after * decay[LINES:] + term[LINES:]
    state = jnp.zeros((LINES, COLS), F32)
    for c in range(BLOCKS // 2 - 1, -1, -1):
        at = slice(c * two, (c + 1) * two)
        term, decay = got_ref[at, COLS : 2 * COLS].astype(F32), decay_ref[at, :]
        before = state * decay[LINES:] + term[LINES:]
        out_ref[at, COLS:] = jnp.concatenate([before, state], axis=0).astype(BF16)
        state = before * decay[:LINES] + term[:LINES]


def local_x_body(dy_ref, b_ref, c_ref, bc_ref, run_ref, cols_ref, loc_ref, bt_ref):
    run, cols = run_ref[...], cols_ref[...]
    bt = whole(b_ref, bc_ref[:HALF]).T
    bt_ref[...] = bt
    score = dot(bt, whole(c_ref, bc_ref[HALF:]), 1, 0)
    lane = iota((TOKENS, 128), 1)
    for i in range(HEADS // 2):
        at = slice(128 * i, 128 * (i + 1))
        dyp = dy_ref[:, at]
        local = []
        for k in range(2):
            kernel = (pair_decay(run, cols, 2 * i + k) * score).astype(BF16)
            local.append(dot(kernel, dyp, 1, 0))
        loc_ref[:, at] = pair(cols, HEADS + 2 * i, lane) * jnp.where(lane < WIDTH, local[0], local[1])


def grad_x_body(bt_hbm, cols_hbm, loc_hbm, states_ref, out_ref, bt_ref, cols_ref, loc_ref, gx_ref, sems):
    count = out_ref.shape[0]
    early = fetch([(bt_hbm, bt_ref), (cols_hbm, cols_ref), (loc_hbm, loc_ref)], sems)
    lane = iota((TOKENS, 128), 1)
    early[0].wait()
    carried = dot(bt_ref[...], states_ref[:, COLS:], 1, 0)
    early[1].wait()
    early[2].wait()
    late = []
    for i in range(HEADS // 2):
        at = slice(128 * i, 128 * (i + 1))
        fwd = pair(cols_ref[...], 2 * HEADS + 2 * i, lane)
        gx_ref[:, at] = (loc_ref[:, at] + fwd * carried[:, at]).astype(BF16)
        if i % 2 == 1:
            done = slice(128 * (i - 1), 128 * (i + 1))
            for k in range(count):
                copy = pltpu.make_async_copy(gx_ref.at[:, done], out_ref.at[k, :, done], sems.at[3 + len(late)])
                copy.start()
                late.append(copy)
    for copy in late:
        copy.wait()


def grad_bc_body(b_ref, c_ref, bc_ref, ms_ref, wx_ref, wdy_ref, states_ref, keep_ref, send_ref):
    b_full, c_full = whole(b_ref, bc_ref[:HALF]), whole(c_ref, bc_ref[HALF:])
    part_b = (dot(c_full, ms_ref[...], 1, 1) + dot(states_ref[:, COLS:], wx_ref[...], 1, 1)).astype(BF16)
    part_c = (dot(b_full, ms_ref[...], 1, 0) + dot(states_ref[:, :COLS], wdy_ref[...], 1, 1)).astype(BF16)
    keep_ref[:HALF, :] = part_b[:HALF]
    keep_ref[HALF:, :] = part_c[:HALF]
    send_ref[:HALF, :] = part_b[HALF:]
    send_ref[HALF:, :] = part_c[HALF:]


def add_bc_body(mine_ref, got_ref, gb_ref, gc_ref):
    half = STATE // 2
    total = (mine_ref[...].astype(F32) + got_ref[...].astype(F32)).astype(BF16)
    gb_ref[...] = total[:half]
    gc_ref[...] = total[half:]


def pass_body(*refs):
    pass


def passed(*arrays):
    anywhere = [SPACES["a"]] * len(arrays)
    return pl.pallas_call(
        pass_body,
        out_shape=[jax.ShapeDtypeStruct(v.shape, v.dtype) for v in arrays],
        in_specs=anywhere,
        out_specs=anywhere,
        input_output_aliases={i: i for i in range(len(arrays))},
        cost_estimate=pl.CostEstimate(flops=PASS_FLOPS, bytes_accessed=2**20, transcendentals=0),
    )(*arrays)


def load_body(where_ref, w_hbm, *refs):
    *pieces, out_ref, sems = refs
    core, here, share, half = where_ref[0], where_ref[1], out_ref.shape[1], COLS // 2
    pairs = [(w_hbm.at[:, pl.ds(pl.multiple_of(here * share, share), share)], out_ref.at[:COLS, :])]
    for i, piece in enumerate(pieces):
        side = core if i < 3 else 1 - core
        start = pl.multiple_of((i % 3 + 1) * COLS + side * half, half)
        pairs.append((piece, out_ref.at[pl.ds(start, half), :]))
    for copy in fetch(pairs, sems):
        copy.wait()


def project_body(where_ref, gx_ref, w_ref, out_ref, tiles_ref, sems):
    tile, count = out_ref.shape[2], gx_ref.shape[0]
    gx = [gx_ref[lax.rem(where_ref[1] + count - i, count)] for i in range(count)]
    gx = jnp.concatenate(gx, axis=1)
    late = []
    for j in range(out_ref.shape[0]):
        tiles_ref[j] = dot(gx, w_ref[:, j * tile : (j + 1) * tile], 1, 0).astype(BF16)
        copy = pltpu.make_async_copy(tiles_ref.at[j], out_ref.at[j], sems.at[j])
        copy.start()
        late.append(copy)
    for copy in late:
        copy.wait()


def add_y_body(got_ref, out_ref):
    total = got_ref[0].astype(F32)
    for k in range(1, got_ref.shape[0]):
        total = total + got_ref[k].astype(F32)
    out_ref[...] = total.T.astype(BF16)


def per_device(x_in, grad_out, step_size, log_decay, b_proj, c_proj, w_in):
    hold = lax.optimization_barrier
    core, x_index = lax.axis_index("core"), lax.axis_index("x")
    flip = [(i, i ^ 1) for i in range(lax.axis_size("yh"))]
    half = w_in.shape[0] // 2
    share = w_in.shape[1] // 4
    square, wide, own_half = (TOKENS, TOKENS), (TOKENS, COLS), (HALF, TOKENS)

    def ahead_on_x(shard, ahead):
        return lax.ppermute(shard, "x", [(i, (i + ahead) % 4) for i in range(4)])

    def other_core(shard):
        return lax.ppermute(shard, "core", [(0, 1), (1, 0)])

    where = jnp.stack([core, x_index])
    bc = lax.ppermute(jnp.concatenate([b_proj, c_proj], axis=0), "yh", flip)
    wx, wdy, mixed, run, cols, ext, b_own, c_own, w_next, w_prev, w_far = call(
        local_body,
        "shhhhhhh",
        [(wide, BF16), (wide, BF16), (square, BF16), ((HEADS, TOKENS), F32), ((TOKENS, 128), F32), ((1, 128), F32)]
        + [(own_half, BF16)] * 2
        + [((half, share), BF16)] * 3,
        [(wide, BF16), (wide, BF16), ((HEADS, TOKENS), F32), ((HEADS, TOKENS), F32), ((3, half, share), BF16)],
        copies=12,
        out_spaces="vvbvbvvvhhh",
    )(where, x_in, grad_out, step_size, log_decay, b_proj, c_proj, w_in)
    (send,) = call(ends_body, "vvvvvv", [((STATE, 2 * COLS + 128), BF16)], out_spaces="v")(
        b_own, c_own, bc, wx, wdy, ext
    )

    terms = lax.all_to_all(send, CONTEXT, 0, 0, tiled=True)
    w_next, w_prev, w_far, bc, _ = hold((w_next, w_prev, w_far, bc, send))
    w_prev, w_next, w_far = ahead_on_x(w_next, 1), ahead_on_x(w_prev, 3), ahead_on_x(w_far, 2)
    local_x, b_rows = call(local_x_body, "vbbvvb", [(wide, F32), (square, BF16)], out_spaces="bb")(
        grad_out, b_proj, c_proj, bc, run, cols
    )
    (scanned,) = call(scan_body, "v", [((STATE, 2 * COLS), BF16)], [((STATE, COLS), F32)], out_spaces="v")(terms)
    states = lax.all_to_all(scanned, CONTEXT, 0, 0, tiled=True)
    w_prev, w_far, w_next, _ = hold((w_prev, w_far, w_next, scanned))
    w_mine = passed(w_prev, w_far, w_next)
    w_theirs = [other_core(w) for w in w_mine]
    states, w_mine, w_theirs = hold((states, w_mine, w_theirs))

    (gx,) = call(
        grad_x_body,
        "hhhv",
        [((4, *wide), BF16)],
        [(square, BF16), ((TOKENS, 128), F32), (wide, F32), (wide, BF16)],
        copies=11,
        out_spaces="h",
    )(b_rows, cols, local_x, states)
    gx_x = lax.all_to_all(gx, "x", 0, 0, tiled=True)
    states, w_mine, _ = hold((states, w_mine, gx))
    keep_bc, send_bc = call(grad_bc_body, "bbvbvvv", [(square, BF16), (square, BF16)], out_spaces="vv")(
        b_proj, c_proj, bc, mixed, wx, wdy, states
    )
    got_bc = lax.ppermute(send_bc, "yh", flip)
    (w_here,) = call(load_body, "shhhhhhh", [((4 * COLS, share), BF16)], copies=7, out_spaces="V")(
        where, w_in, *w_mine, *w_theirs
    )
    gx_x, got_bc, w_here = hold((gx_x, got_bc, w_here))

    (partial,) = call(
        project_body, "svV", [((4, *square), BF16)], [((4, *square), BF16)], copies=4, out_spaces="h"
    )(where, gx_x, w_here)
    over_y = lax.all_to_all(partial, "yh", 0, 0, tiled=True)
    (grad_input,) = call(add_y_body, "v", [(square, BF16)], out_spaces="v")(over_y)
    grad_b, grad_c = call(add_bc_body, "vv", [(own_half, BF16), (own_half, BF16)], out_spaces="vv")(keep_bc, got_bc)
    return grad_input, grad_b, grad_c


def solution(mesh):
    fine = Mesh(mesh.devices.reshape(8, 2, 2, 4, 4), CONTEXT + TENSOR)
    by_token, by_head = P(CONTEXT, TENSOR), P(TENSOR, CONTEXT)
    return jax.shard_map(
        per_device,
        mesh=fine,
        in_specs=(by_token, by_token, by_head, by_head, by_head, by_head, P(TENSOR, None)),
        out_specs=(by_head, by_head, by_head),
        check_vma=False,
    )
```

time: 125 us -> 116 us (0.928)
  the two profiles are of different devices: /device:TPU:57 before, /device:TPU:8 now
where the time goes in v2:
time: 116 us; the launch traced here: 115 us
  starting transfers between devices  54.7 us (47%)
  waiting for transfers between devices  34.6 us (30%)
  Pallas kernels  19.7 us (17%)
  local copies, waits for them, and re-layouts  4.15 us (4%)
    pallas_call x10, Pallas kernels, pinned(): run(*(pltpu.with_memory_space_constraint(a, PLACES[k]) if k in PLACES els...  19.7 us
    all_to_all x1, waiting for transfers between devices, per_device(): over_y = lax.all_to_all(partial, 'yh', 0, 0, tiled=True)  13.3 us
    all_to_all x1, starting transfers between devices, per_device(): terms = lax.all_to_all(send, CONTEXT, 0, 0, tiled=True)  11.9 us
    ppermute x3, starting transfers between devices, ahead_on_x(): return lax.ppermute(shard, 'x', [(i, (i + ahead) % 4) for i in range(4)])  11.4 us
    all_to_all x1, waiting for transfers between devices, per_device(): terms = lax.all_to_all(send, CONTEXT, 0, 0, tiled=True)  7.71 us
    all_to_all x1, starting transfers between devices, per_device(): over_y = lax.all_to_all(partial, 'yh', 0, 0, tiled=True)  6.99 us
    ppermute x3, waiting for transfers between devices, ahead_on_x(): return lax.ppermute(shard, 'x', [(i, (i + ahead) % 4) for i in range(4)])  6.82 us
    ppermute x3, starting transfers between devices, other_core(): return lax.ppermute(shard, 'core', [(0, 1), (1, 0)])  6.24 us
  transfers between devices with their start and end apart: 12, of which 7 were waited for; matrix products, arithmetic and copies ran while one was open for 0% of the time, Pallas kernels for 11%

profile of v2, /device:TPU:8, one launch (start us, length us, event | category | flops | bytes accessed | tf_op | source)
XLA Modules:
  0.0 114.9 jit_solution(3517423885550617944)
XLA Ops:
  0.6 0.9 pad_maximum_fusion
  1.5 4.5 %collective-permute-start = (bf16[256,256]{1,0:T(8,128)(2,1)S(1)}, bf16[256,256]{1,0:T(8,128)(2,1)S(1)}, u32[]{:S(2)}, u32[]{:S(2)}) collective-permute-start(bf16[256,256]{1,0:T(8,128)(2,1)S(1)} %pad_maximum_fusion), channel_id=1, source_target_pairs={{0,1},{1,0},{2,3},{3,2},{4,5},{5,4},{6,7},{7,6},{8,9},{9,8},{10,11... | collective-permute-start | bytes 393224 | tf_op jit(solution)/shard_map/ppermute | solution.py:308
  6.0 0.1 pad_add_fusion.where_ref
  6.1 4.2 %shard_map.94 = (bf16[256,512]{1,0:T(8,128)(2,1)S(1)}, bf16[256,512]{1,0:T(8,128)(2,1)S(1)}, bf16[256,256]{1,0:T(8,128)(2,1)}, f32[8,256]{1,0:T(8,128)S(1)}, f32...) custom-call(s32[2]{0:T(128)S(1)} %pad_add_fusion.where_ref, ...), custom_call_target="tpu_custom_call" | custom-call | flops 1000000000 | bytes 1048576 | tf_op jit(solution)/shard_map/pallas_call | solution.py:51
  10.3 1.1 collective-permute-done.bc_ref
  11.5 1.1 %shard_map.95 = bf16[256,1152]{1,0:T(8,128)(2,1)} custom-call(bf16[128,256]{1,0:T(8,128)(2,1)S(1)} %get-tuple-element.47.b_ref, bf16[128,256]{1,0:T(8,128)(2,1)S(1)} %get-tuple-element.48.c_ref, bf16[256,256]{1,0:T(8,128)(2,1)S(1)} %collective-permute-done.bc_ref, bf16[256,512]{1,0:T(8,128)(2,1)S(1)} %get-tuple-element.49.wx_ref, ...), custom_call_target="tpu_custom_call" | custom-call | flops 1000000000 | bytes 1048576 | tf_op jit(solution)/shard_map/pallas_call | solution.py:51
  12.6 11.9 %all-to-all-start = ((bf16[32,8,1152]{2,1,0:T(8,128)(2,1)}), bf16[32,8,1152]{2,1,0:T(8,128)(2,1)S(1)}, u32[]{:S(2)}, u32[]{:S(2)}) async-start(bf16[32,8,1152]{2,1,0:T(8,128)(2,1)} %bitcast.2), calls=%async_computation | async-start | bytes 1179648 | tf_op jit(solution)/shard_map/all_to_all | solution.py:323
  24.5 3.4 %collective-permute-start.1 = (bf16[256,1024]{1,0:T(8,128)(2,1)}, bf16[256,1024]{1,0:T(8,128)(2,1)S(1)}, u32[]{:S(2)}, u32[]{:S(2)}) collective-permute-start(bf16[256,1024]{1,0:T(8,128)(2,1)} %get-tuple-element.57), channel_id=1, source_target_pairs={{0,4},{4,8},{8,12},{12,0},{1,5},{5,9},{9,13},{13,1},{2,6},{6,10},{... | collective-permute-start | bytes 1572872 | tf_op jit(solution)/shard_map/ppermute | solution.py:302
  27.9 4.6 %collective-permute-start.2 = (bf16[256,1024]{1,0:T(8,128)(2,1)}, bf16[256,1024]{1,0:T(8,128)(2,1)S(1)}, u32[]{:S(2)}, u32[]{:S(2)}) collective-permute-start(bf16[256,1024]{1,0:T(8,128)(2,1)} %get-tuple-element.58), channel_id=1, source_target_pairs={{0,8},{4,12},{8,0},{12,4},{1,9},{5,13},{9,1},{13,5},{2,10},{6,14},... | collective-permute-start | bytes 1572872 | tf_op jit(solution)/shard_map/ppermute | solution.py:302
  32.6 3.3 %collective-permute-start.3 = (bf16[256,1024]{1,0:T(8,128)(2,1)}, bf16[256,1024]{1,0:T(8,128)(2,1)}, u32[]{:S(2)}, u32[]{:S(2)}) collective-permute-start(bf16[256,1024]{1,0:T(8,128)(2,1)} %get-tuple-element.59), channel_id=1, source_target_pairs={{0,12},{4,0},{8,4},{12,8},{1,13},{5,1},{9,5},{13,9},{2,14},{6,2},{... | collective-permute-start | bytes 1572872 | tf_op jit(solution)/shard_map/ppermute | solution.py:302
  35.9 7.7 %all-to-all-done = bf16[32,8,1152]{2,1,0:T(8,128)(2,1)S(1)} async-done(((bf16[32,8,1152]{2,1,0:T(8,128)(2,1)}), bf16[32,8,1152]{2,1,0:T(8,128)(2,1)S(1)}, u32[]{:S(2)}, u32[]{:S(2)}) %all-to-all-start) | async-done | bytes 589856 | tf_op jit(solution)/shard_map/all_to_all | solution.py:323
  43.7 1.1 shard_map.97
  44.7 4.1 %all-to-all-start.1 = ((bf16[32,8,1024]{2,1,0:T(8,128)(2,1)}), bf16[32,8,1024]{2,1,0:T(8,128)(2,1)S(1)}, u32[]{:S(2)}, u32[]{:S(2)}) async-start(bf16[32,8,1024]{2,1,0:T(8,128)(2,1)} %bitcast.4), calls=%async_computation.1 | async-start | bytes 1048576 | tf_op jit(solution)/shard_map/all_to_all | solution.py:330
  48.9 0.0 copy-start.2
  48.9 0.0 collective-permute-done.1.refs_0_
  48.9 0.0 copy-start.6
  48.9 5.2 %collective-permute-done.2.refs_1_ = bf16[256,1024]{1,0:T(8,128)(2,1)S(1)} collective-permute-done((bf16[256,1024]{1,0:T(8,128)(2,1)}, bf16[256,1024]{1,0:T(8,128)(2,1)S(1)}, u32[]{:S(2)}, u32[]{:S(2)}) %collective-permute-start.2) | collective-permute-done | bytes 524320 | tf_op jit(solution)/shard_map/ppermute | solution.py:302
  54.1 0.0 copy-start.7
  54.1 1.7 %collective-permute-done.3.refs_2_ = bf16[256,1024]{1,0:T(8,128)(2,1)} collective-permute-done((bf16[256,1024]{1,0:T(8,128)(2,1)}, bf16[256,1024]{1,0:T(8,128)(2,1)}, u32[]{:S(2)}, u32[]{:S(2)}) %collective-permute-start.3) | collective-permute-done | bytes 524320 | tf_op jit(solution)/shard_map/ppermute | solution.py:302
  55.7 0.0 copy-done.6
  55.7 0.0 copy-done.7
  55.7 1.9 %collective-permute-start.4 = (bf16[256,1024]{1,0:T(8,128)(2,1)}, bf16[256,1024]{1,0:T(8,128)(2,1)S(1)}, u32[]{:S(2)}, u32[]{:S(2)}) collective-permute-start(bf16[256,1024]{1,0:T(8,128)(2,1)} %get-tuple-element.73.refs_0_), channel_id=1, source_target_pairs={{0,16},{16,0},{1,17},{17,1},{2,18},{18,2},{3,19},{19,3},{4,20},{20... | collective-permute-start | bytes 1572872 | tf_op jit(solution)/shard_map/ppermute | solution.py:305
  57.6 2.4 %collective-permute-start.5 = (bf16[256,1024]{1,0:T(8,128)(2,1)}, bf16[256,1024]{1,0:T(8,128)(2,1)S(1)}, u32[]{:S(2)}, u32[]{:S(2)}) collective-permute-start(bf16[256,1024]{1,0:T(8,128)(2,1)} %get-tuple-element.74.refs_1_), channel_id=1, source_target_pairs={{0,16},{16,0},{1,17},{17,1},{2,18},{18,2},{3,19},{19,3},{4,20},{20... | collective-permute-start | bytes 1572872 | tf_op jit(solution)/shard_map/ppermute | solution.py:305
  60.0 1.9 %collective-permute-start.6 = (bf16[256,1024]{1,0:T(8,128)(2,1)}, bf16[256,1024]{1,0:T(8,128)(2,1)S(1)}, u32[]{:S(2)}, u32[]{:S(2)}) collective-permute-start(bf16[256,1024]{1,0:T(8,128)(2,1)} %get-tuple-element.75.refs_2_), channel_id=1, source_target_pairs={{0,16},{16,0},{1,17},{17,1},{2,18},{18,2},{3,19},{19,3},{4,20},{20... | collective-permute-start | bytes 1572872 | tf_op jit(solution)/shard_map/ppermute | solution.py:305
  62.0 0.0 copy-done.2
  62.0 2.6 %shard_map.96 = (f32[256,512]{1,0:T(8,128)}, bf16[256,256]{1,0:T(8,128)(2,1)}) custom-call(bf16[256,512]{1,0:T(8,128)(2,1)S(1)} %copy-done.2, bf16[128,256]{1,0:T(8,128)(2,1)} %b_ref.3, bf16[128,256]{1,0:T(8,128)(2,1)} %c_ref.3, bf16[256,256]{1,0:T(8,128)(2,1)S(1)} %collective-permute-done.bc_ref, f32[8,256]{1,0:T(8,128)S(1)} %get-tuple-element.53.run_ref, ...), custom_call_target="tpu_custom_call" | custom-call | flops 1000000000 | bytes 1048576 | tf_op jit(solution)/shard_map/pallas_call | solution.py:51
  64.6 0.0 collective-permute-done.4.refs_3_
  64.6 0.0 copy-start.3
  64.6 0.0 collective-permute-done.5.refs_4_
  64.6 0.0 copy-start.4
  64.6 0.0 collective-permute-done.6.refs_5_
  64.6 0.0 copy-start.5
  64.6 2.0 %all-to-all-done.1 = bf16[32,8,1024]{2,1,0:T(8,128)(2,1)S(1)} async-done(((bf16[32,8,1024]{2,1,0:T(8,128)(2,1)}), bf16[32,8,1024]{2,1,0:T(8,128)(2,1)S(1)}, u32[]{:S(2)}, u32[]{:S(2)}) %all-to-all-start.1) | async-done | bytes 524320 | tf_op jit(solution)/shard_map/all_to_all | solution.py:330
  66.7 2.5 %shard_map.99 = bf16[4,256,512]{2,1,0:T(8,128)(2,1)} custom-call(bf16[256,256]{1,0:T(8,128)(2,1)} %get-tuple-element.55.bt_hbm, f32[256,128]{1,0:T(8,128)} %get-tuple-element.54.cols_ref.cols_hbm, f32[256,512]{1,0:T(8,128)} %get-tuple-element.56.loc_hbm, bf16[256,1024]{1,0:T(8,128)(2,1)S(1)} %bitcast.7), custom_call_target="tpu_custom_call" | custom-call | flops 1000000000 | bytes 1048576 | tf_op jit(solution)/shard_map/pallas_call | solution.py:51
  69.2 0.0 copy-done.5
  69.2 4.3 %all-to-all-start.2 = ((bf16[4,256,512]{2,1,0:T(8,128)(2,1)}), bf16[4,256,512]{2,1,0:T(8,128)(2,1)S(1)}, u32[]{:S(2)}, u32[]{:S(2)}) async-start(bf16[4,256,512]{2,1,0:T(8,128)(2,1)} %shard_map.99), calls=%async_computation.2 | async-start | bytes 2097152 | tf_op jit(solution)/shard_map/all_to_all | solution.py:344
  73.5 1.4 %shard_map.100 = (bf16[256,256]{1,0:T(8,128)(2,1)S(1)}, bf16[256,256]{1,0:T(8,128)(2,1)S(1)}) custom-call(bf16[128,256]{1,0:T(8,128)(2,1)} %b_ref.3, bf16[128,256]{1,0:T(8,128)(2,1)} %c_ref.3, bf16[256,256]{1,0:T(8,128)(2,1)S(1)} %collective-permute-done.bc_ref, bf16[256,256]{1,0:T(8,128)(2,1)} %get-tuple-element.67.ms_ref, ...), custom_call_target="tpu_custom_call" | custom-call | flops 1000000000 | bytes 1048576 | tf_op jit(solution)/shard_map/pallas_call | solution.py:51
  74.9 0.0 copy-done.3
  74.9 0.0 copy-done.4
  74.9 5.3 %collective-permute-start.7 = (bf16[256,256]{1,0:T(8,128)(2,1)S(1)}, bf16[256,256]{1,0:T(8,128)(2,1)S(1)}, u32[]{:S(2)}, u32[]{:S(2)}) collective-permute-start(bf16[256,256]{1,0:T(8,128)(2,1)S(1)} %get-tuple-element.72), channel_id=1, source_target_pairs={{0,1},{1,0},{2,3},{3,2},{4,5},{5,4},{6,7},{7,6},{8,9},{9,8},{10,11... | collective-permute-start | bytes 393224 | tf_op jit(solution)/shard_map/ppermute | solution.py:349
  80.2 2.8 %shard_map.101.w_ref = bf16[2048,1024]{1,0:T(8,128)(2,1)S(1)} custom-call(s32[2]{0:T(128)S(1)} %pad_add_fusion.where_ref, bf16[512,4096]{1,0:T(8,128)(2,1)} %w_hbm.3, bf16[256,1024]{1,0:T(8,128)(2,1)} %get-tuple-element.73.refs_0_, bf16[256,1024]{1,0:T(8,128)(2,1)} %get-tuple-element.74.refs_1_, bf16[256,1024]{1,0:T(8,128)(2,1)} %get-tuple-element.75.refs_2_, ...), custom_call_target="tpu_custom_call" | custom-call | flops 1000000000 | bytes 1048576 | tf_op jit(solution)/shard_map/pallas_call | solution.py:51
  83.0 0.0 copy-start
  83.0 1.9 %copy-done = bf16[2048,1024]{1,0:T(8,128)(2,1)} copy-done((bf16[2048,1024]{1,0:T(8,128)(2,1)}, bf16[2048,1024]{1,0:T(8,128)(2,1)S(1)}, u32[]{:S(2)}) %copy-start) | copy-done | bytes 4194328
  84.9 0.0 collective-permute-done.7.got_ref
  84.9 3.5 %all-to-all-done.2.gx_ref = bf16[4,256,512]{2,1,0:T(8,128)(2,1)S(1)} async-done(((bf16[4,256,512]{2,1,0:T(8,128)(2,1)}), bf16[4,256,512]{2,1,0:T(8,128)(2,1)S(1)}, u32[]{:S(2)}, u32[]{:S(2)}) %all-to-all-start.2) | async-done | bytes 1048608 | tf_op jit(solution)/shard_map/all_to_all | solution.py:344
  88.4 0.0 copy-start.1
  88.4 2.2 %copy-done.1 = bf16[2048,1024]{1,0:T(8,128)(2,1)S(1)} copy-done((bf16[2048,1024]{1,0:T(8,128)(2,1)S(1)}, bf16[2048,1024]{1,0:T(8,128)(2,1)}, u32[]{:S(2)}) %copy-start.1) | copy-done | bytes 4194328
  90.6 2.5 %shard_map.102 = bf16[4,256,256]{2,1,0:T(8,128)(2,1)} custom-call(s32[2]{0:T(128)S(1)} %pad_add_fusion.where_ref, bf16[4,256,512]{2,1,0:T(8,128)(2,1)S(1)} %all-to-all-done.2.gx_ref, bf16[2048,1024]{1,0:T(8,128)(2,1)S(1)} %copy-done.1), custom_call_target="tpu_custom_call" | custom-call | flops 1000000000 | bytes 1048576 | tf_op jit(solution)/shard_map/pallas_call | solution.py:51
  93.1 7.0 %all-to-all-start.3 = ((bf16[4,256,256]{2,1,0:T(8,128)(2,1)}), bf16[4,256,256]{2,1,0:T(8,128)(2,1)S(1)}, u32[]{:S(2)}, u32[]{:S(2)}) async-start(bf16[4,256,256]{2,1,0:T(8,128)(2,1)} %shard_map.102), calls=%async_computation.3 | async-start | bytes 1048576 | tf_op jit(solution)/shard_map/all_to_all | solution.py:358
  100.1 0.7 shard_map.104
  100.8 13.3 %all-to-all-done.3.got_ref = bf16[4,256,256]{2,1,0:T(8,128)(2,1)S(1)} async-done(((bf16[4,256,256]{2,1,0:T(8,128)(2,1)}), bf16[4,256,256]{2,1,0:T(8,128)(2,1)S(1)}, u32[]{:S(2)}, u32[]{:S(2)}) %all-to-all-start.3) | async-done | bytes 524320 | tf_op jit(solution)/shard_map/all_to_all | solution.py:358
  114.1 0.8 shard_map.103
  (1 shorter events, 0.0 us)
Async XLA Ops:
  1.5 10.0 %collective-permute-start = (bf16[256,256]{1,0:T(8,128)(2,1)S(1)}, bf16[256,256]{1,0:T(8,128)(2,1)S(1)}, u32[]{:S(2)}, u32[]{:S(2)}) collective-permute-start(bf16[256,256]{1,0:T(8,128)(2,1)S(1)} %pad_maximum_fusion), channel_id=1, source_target_pairs={{0,1},{1,0},{2,3},{3,2},{4,5},{5,4},{6,7},{7,6},{8,9},{9,8},{10,11... | collective-permute-start | bytes 393224 | tf_op jit(solution)/shard_map/ppermute | solution.py:308
  12.6 31.0 %all-to-all-start = ((bf16[32,8,1152]{2,1,0:T(8,128)(2,1)}), bf16[32,8,1152]{2,1,0:T(8,128)(2,1)S(1)}, u32[]{:S(2)}, u32[]{:S(2)}) async-start(bf16[32,8,1152]{2,1,0:T(8,128)(2,1)} %bitcast.2), calls=%async_computation | async-start | bytes 1179648 | tf_op jit(solution)/shard_map/all_to_all | solution.py:323
  24.5 24.3 %collective-permute-start.1 = (bf16[256,1024]{1,0:T(8,128)(2,1)}, bf16[256,1024]{1,0:T(8,128)(2,1)S(1)}, u32[]{:S(2)}, u32[]{:S(2)}) collective-permute-start(bf16[256,1024]{1,0:T(8,128)(2,1)} %get-tuple-element.57), channel_id=1, source_target_pairs={{0,4},{4,8},{8,12},{12,0},{1,5},{5,9},{9,13},{13,1},{2,6},{6,10},{... | collective-permute-start | bytes 1572872 | tf_op jit(solution)/shard_map/ppermute | solution.py:302
  27.9 26.1 %collective-permute-start.2 = (bf16[256,1024]{1,0:T(8,128)(2,1)}, bf16[256,1024]{1,0:T(8,128)(2,1)S(1)}, u32[]{:S(2)}, u32[]{:S(2)}) collective-permute-start(bf16[256,1024]{1,0:T(8,128)(2,1)} %get-tuple-element.58), channel_id=1, source_target_pairs={{0,8},{4,12},{8,0},{12,4},{1,9},{5,13},{9,1},{13,5},{2,10},{6,14},... | collective-permute-start | bytes 1572872 | tf_op jit(solution)/shard_map/ppermute | solution.py:302
  32.6 23.1 %collective-permute-start.3 = (bf16[256,1024]{1,0:T(8,128)(2,1)}, bf16[256,1024]{1,0:T(8,128)(2,1)}, u32[]{:S(2)}, u32[]{:S(2)}) collective-permute-start(bf16[256,1024]{1,0:T(8,128)(2,1)} %get-tuple-element.59), channel_id=1, source_target_pairs={{0,12},{4,0},{8,4},{12,8},{1,13},{5,1},{9,5},{13,9},{2,14},{6,2},{... | collective-permute-start | bytes 1572872 | tf_op jit(solution)/shard_map/ppermute | solution.py:302
  44.7 21.9 %all-to-all-start.1 = ((bf16[32,8,1024]{2,1,0:T(8,128)(2,1)}), bf16[32,8,1024]{2,1,0:T(8,128)(2,1)S(1)}, u32[]{:S(2)}, u32[]{:S(2)}) async-start(bf16[32,8,1024]{2,1,0:T(8,128)(2,1)} %bitcast.4), calls=%async_computation.1 | async-start | bytes 1048576 | tf_op jit(solution)/shard_map/all_to_all | solution.py:330
  48.9 13.1 %copy-start.2 = (bf16[256,512]{1,0:T(8,128)(2,1)S(1)}, bf16[256,512]{1,0:T(8,128)(2,1)}, u32[]{:S(2)}) copy-start(bf16[256,512]{1,0:T(8,128)(2,1)} %dy_ref.1) | copy-start | bytes 786436
  48.9 6.8 %copy-start.6 = (bf16[256,1024]{1,0:T(8,128)(2,1)}, bf16[256,1024]{1,0:T(8,128)(2,1)S(1)}, u32[]{:S(2)}) copy-start(bf16[256,1024]{1,0:T(8,128)(2,1)S(1)} %collective-permute-done.1.refs_0_) | copy-start | bytes 1572868
  54.1 1.7 %copy-start.7 = (bf16[256,1024]{1,0:T(8,128)(2,1)}, bf16[256,1024]{1,0:T(8,128)(2,1)S(1)}, u32[]{:S(2)}) copy-start(bf16[256,1024]{1,0:T(8,128)(2,1)S(1)} %collective-permute-done.2.refs_1_) | copy-start | bytes 1572868
  55.7 8.9 %collective-permute-start.4 = (bf16[256,1024]{1,0:T(8,128)(2,1)}, bf16[256,1024]{1,0:T(8,128)(2,1)S(1)}, u32[]{:S(2)}, u32[]{:S(2)}) collective-permute-start(bf16[256,1024]{1,0:T(8,128)(2,1)} %get-tuple-element.73.refs_0_), channel_id=1, source_target_pairs={{0,16},{16,0},{1,17},{17,1},{2,18},{18,2},{3,19},{19,3},{4,20},{20... | collective-permute-start | bytes 1572872 | tf_op jit(solution)/shard_map/ppermute | solution.py:305
  57.6 6.9 %collective-permute-start.5 = (bf16[256,1024]{1,0:T(8,128)(2,1)}, bf16[256,1024]{1,0:T(8,128)(2,1)S(1)}, u32[]{:S(2)}, u32[]{:S(2)}) collective-permute-start(bf16[256,1024]{1,0:T(8,128)(2,1)} %get-tuple-element.74.refs_1_), channel_id=1, source_target_pairs={{0,16},{16,0},{1,17},{17,1},{2,18},{18,2},{3,19},{19,3},{4,20},{20... | collective-permute-start | bytes 1572872 | tf_op jit(solution)/shard_map/ppermute | solution.py:305
  60.0 4.5 %collective-permute-start.6 = (bf16[256,1024]{1,0:T(8,128)(2,1)}, bf16[256,1024]{1,0:T(8,128)(2,1)S(1)}, u32[]{:S(2)}, u32[]{:S(2)}) collective-permute-start(bf16[256,1024]{1,0:T(8,128)(2,1)} %get-tuple-element.75.refs_2_), channel_id=1, source_target_pairs={{0,16},{16,0},{1,17},{17,1},{2,18},{18,2},{3,19},{19,3},{4,20},{20... | collective-permute-start | bytes 1572872 | tf_op jit(solution)/shard_map/ppermute | solution.py:305
  64.6 10.3 %copy-start.3 = (bf16[256,1024]{1,0:T(8,128)(2,1)}, bf16[256,1024]{1,0:T(8,128)(2,1)S(1)}, u32[]{:S(2)}) copy-start(bf16[256,1024]{1,0:T(8,128)(2,1)S(1)} %collective-permute-done.4.refs_3_) | copy-start | bytes 1572868
  64.6 10.3 %copy-start.4 = (bf16[256,1024]{1,0:T(8,128)(2,1)}, bf16[256,1024]{1,0:T(8,128)(2,1)S(1)}, u32[]{:S(2)}) copy-start(bf16[256,1024]{1,0:T(8,128)(2,1)S(1)} %collective-permute-done.5.refs_4_) | copy-start | bytes 1572868
  64.6 4.6 %copy-start.5 = (bf16[256,1024]{1,0:T(8,128)(2,1)}, bf16[256,1024]{1,0:T(8,128)(2,1)S(1)}, u32[]{:S(2)}) copy-start(bf16[256,1024]{1,0:T(8,128)(2,1)S(1)} %collective-permute-done.6.refs_5_) | copy-start | bytes 1572868
  69.2 19.2 %all-to-all-start.2 = ((bf16[4,256,512]{2,1,0:T(8,128)(2,1)}), bf16[4,256,512]{2,1,0:T(8,128)(2,1)S(1)}, u32[]{:S(2)}, u32[]{:S(2)}) async-start(bf16[4,256,512]{2,1,0:T(8,128)(2,1)} %shard_map.99), calls=%async_computation.2 | async-start | bytes 2097152 | tf_op jit(solution)/shard_map/all_to_all | solution.py:344
  74.9 10.0 %collective-permute-start.7 = (bf16[256,256]{1,0:T(8,128)(2,1)S(1)}, bf16[256,256]{1,0:T(8,128)(2,1)S(1)}, u32[]{:S(2)}, u32[]{:S(2)}) collective-permute-start(bf16[256,256]{1,0:T(8,128)(2,1)S(1)} %get-tuple-element.72), channel_id=1, source_target_pairs={{0,1},{1,0},{2,3},{3,2},{4,5},{5,4},{6,7},{7,6},{8,9},{9,8},{10,11... | collective-permute-start | bytes 393224 | tf_op jit(solution)/shard_map/ppermute | solution.py:349
  83.0 1.9 %copy-start = (bf16[2048,1024]{1,0:T(8,128)(2,1)}, bf16[2048,1024]{1,0:T(8,128)(2,1)S(1)}, u32[]{:S(2)}) copy-start(bf16[2048,1024]{1,0:T(8,128)(2,1)S(1)} %shard_map.101.w_ref) | copy-start | bytes 12582916
  88.4 2.2 %copy-start.1 = (bf16[2048,1024]{1,0:T(8,128)(2,1)S(1)}, bf16[2048,1024]{1,0:T(8,128)(2,1)}, u32[]{:S(2)}) copy-start(bf16[2048,1024]{1,0:T(8,128)(2,1)} %copy-done) | copy-start | bytes 12582916
  93.1 21.0 %all-to-all-start.3 = ((bf16[4,256,256]{2,1,0:T(8,128)(2,1)}), bf16[4,256,256]{2,1,0:T(8,128)(2,1)S(1)}, u32[]{:S(2)}, u32[]{:S(2)}) async-start(bf16[4,256,256]{2,1,0:T(8,128)(2,1)} %shard_map.102), calls=%async_computation.3 | async-start | bytes 1048576 | tf_op jit(solution)/shard_map/all_to_all | solution.py:358

commit v3 on v2

--- a/solution.py
+++ b/solution.py
@@ -28,7 +28,8 @@
     "a": pl.BlockSpec(memory_space=pl.ANY),
 }
 PLACES = {"h": pltpu.HBM, "b": pltpu.HBM, "V": pltpu.VMEM}
-PASS_FLOPS = 2 * 10**10
+ADD_FLOPS = 10 * 10**9
+PASS_FLOPS = 4 * 10**9
 LIMIT = 16 * 1024 * 1024
 
 
@@ -95,7 +96,7 @@
 
 def local_body(
     where_ref, x_hbm, dy_hbm, dt_hbm, ld_hbm, b_hbm, c_hbm, w_hbm,
-    wx_ref, wdy_ref, ms_ref, run_ref, cols_ref, ext_ref, b_ref, c_ref, w1_hbm, w3_hbm, w2_hbm,
+    wx_ref, wdy_ref, ms_ref, run_ref, cols_ref, ext_ref, b_ref, c_ref, w1_hbm, w3_hbm, w2_hbm, wx_hbm, wdy_hbm,
     x_ref, dy_ref, dt_ref, ld_ref, w_ref, sems,
 ):
     rows, share = w1_hbm.shape
@@ -152,6 +153,9 @@
             mixing = (decay * inter * cols[:, HEADS + h : HEADS + h + 1]).astype(BF16)
             total = total + mixing.astype(F32)
     ms_ref[...] = total.astype(BF16)
+    for i, (a, b) in enumerate(((wx_ref, wx_hbm), (wdy_ref, wdy_hbm))):
+        out.append(pltpu.make_async_copy(a, b, sems.at[12 + i]))
+        out[-1].start()
     for copy in out:
         copy.wait()
 
@@ -160,13 +164,21 @@
     return jnp.concatenate([own_ref[...], other], axis=0)
 
 
-def ends_body(b_ref, c_ref, bc_ref, wx_ref, wdy_ref, ext_ref, send_ref):
-    send_ref[:, :COLS] = dot(whole(b_ref, bc_ref[:HALF]), wx_ref[...], 1, 0).astype(BF16)
-    send_ref[:, COLS : 2 * COLS] = dot(whole(c_ref, bc_ref[HALF:]), wdy_ref[...], 1, 0).astype(BF16)
+def ends_body(b_ref, c_ref, other_b, other_c, wx_ref, wdy_ref, ext_ref, send_hbm, send_ref, sems):
+    parts = [slice(0, COLS), slice(COLS, 2 * COLS + 128)]
+    copies = [pltpu.make_async_copy(send_ref.at[:, at], send_hbm.at[:, at], sems.at[i]) for i, at in enumerate(parts)]
+    send_ref[:, :COLS] = dot(whole(b_ref, other_b[...]), wx_ref[...], 1, 0).astype(BF16)
+    copies[0].start()
+    send_ref[:, COLS : 2 * COLS] = dot(whole(c_ref, other_c[...]), wdy_ref[...], 1, 0).astype(BF16)
     send_ref[:, 2 * COLS :] = jnp.broadcast_to(ext_ref[...], (STATE, 128)).astype(BF16)
-
-
-def scan_body(got_ref, out_ref, decay_ref):
+    copies[1].start()
+    for copy in copies:
+        copy.wait()
+
+
+def scan_body(got_ref, out_hbm, out_ref, decay_ref, sems):
+    halves = [slice(0, COLS), slice(COLS, 2 * COLS)]
+    copies = [pltpu.make_async_copy(out_ref.at[:, at], out_hbm.at[:, at], sems.at[i]) for i, at in enumerate(halves)]
     decay_ref[...] = expanded(got_ref[:, 2 * COLS :])
     two = 2 * LINES
     state = jnp.zeros((LINES, COLS), F32)
@@ -176,6 +188,7 @@
         after = state * decay[:LINES] + term[:LINES]
         out_ref[at, :COLS] = jnp.concatenate([state, after], axis=0).astype(BF16)
         state = after * decay[LINES:] + term[LINES:]
+    copies[0].start()
     state = jnp.zeros((LINES, COLS), F32)
     for c in range(BLOCKS // 2 - 1, -1, -1):
         at = slice(c * two, (c + 1) * two)
@@ -183,13 +196,16 @@
         before = state * decay[LINES:] + term[LINES:]
         out_ref[at, COLS:] = jnp.concatenate([before, state], axis=0).astype(BF16)
         state = before * decay[:LINES] + term[:LINES]
-
-
-def local_x_body(dy_ref, b_ref, c_ref, bc_ref, run_ref, cols_ref, loc_ref, bt_ref):
+    copies[1].start()
+    for copy in copies:
+        copy.wait()
+
+
+def local_x_body(dy_ref, b_ref, c_ref, other_b, other_c, run_ref, cols_ref, loc_ref, bt_ref):
     run, cols = run_ref[...], cols_ref[...]
-    bt = whole(b_ref, bc_ref[:HALF]).T
+    bt = whole(b_ref, other_b[...]).T
     bt_ref[...] = bt
-    score = dot(bt, whole(c_ref, bc_ref[HALF:]), 1, 0)
+    score = dot(bt, whole(c_ref, other_c[...]), 1, 0)
     lane = iota((TOKENS, 128), 1)
     for i in range(HEADS // 2):
         at = slice(128 * i, 128 * (i + 1))
@@ -201,31 +217,21 @@
         loc_ref[:, at] = pair(cols, HEADS + 2 * i, lane) * jnp.where(lane < WIDTH, local[0], local[1])
 
 
-def grad_x_body(bt_hbm, cols_hbm, loc_hbm, states_ref, out_ref, bt_ref, cols_ref, loc_ref, gx_ref, sems):
-    count = out_ref.shape[0]
+def grad_x_body(bt_hbm, cols_hbm, loc_hbm, states_ref, gx_ref, bt_ref, cols_ref, loc_ref, sems):
     early = fetch([(bt_hbm, bt_ref), (cols_hbm, cols_ref), (loc_hbm, loc_ref)], sems)
     lane = iota((TOKENS, 128), 1)
     early[0].wait()
     carried = dot(bt_ref[...], states_ref[:, COLS:], 1, 0)
     early[1].wait()
     early[2].wait()
-    late = []
     for i in range(HEADS // 2):
         at = slice(128 * i, 128 * (i + 1))
         fwd = pair(cols_ref[...], 2 * HEADS + 2 * i, lane)
         gx_ref[:, at] = (loc_ref[:, at] + fwd * carried[:, at]).astype(BF16)
-        if i % 2 == 1:
-            done = slice(128 * (i - 1), 128 * (i + 1))
-            for k in range(count):
-                copy = pltpu.make_async_copy(gx_ref.at[:, done], out_ref.at[k, :, done], sems.at[3 + len(late)])
-                copy.start()
-                late.append(copy)
-    for copy in late:
-        copy.wait()
-
-
-def grad_bc_body(b_ref, c_ref, bc_ref, ms_ref, wx_ref, wdy_ref, states_ref, keep_ref, send_ref):
-    b_full, c_full = whole(b_ref, bc_ref[:HALF]), whole(c_ref, bc_ref[HALF:])
+
+
+def grad_bc_body(b_ref, c_ref, other_b, other_c, ms_ref, wx_ref, wdy_ref, states_ref, keep_ref, send_ref):
+    b_full, c_full = whole(b_ref, other_b[...]), whole(c_ref, other_c[...])
     part_b = (dot(c_full, ms_ref[...], 1, 1) + dot(states_ref[:, COLS:], wx_ref[...], 1, 1)).astype(BF16)
     part_c = (dot(b_full, ms_ref[...], 1, 0) + dot(states_ref[:, :COLS], wdy_ref[...], 1, 1)).astype(BF16)
     keep_ref[:HALF, :] = part_b[:HALF]
@@ -253,30 +259,33 @@
         in_specs=anywhere,
         out_specs=anywhere,
         input_output_aliases={i: i for i in range(len(arrays))},
+        compiler_params=pltpu.CompilerParams(vmem_limit_bytes=LIMIT),
         cost_estimate=pl.CostEstimate(flops=PASS_FLOPS, bytes_accessed=2**20, transcendentals=0),
     )(*arrays)
 
 
 def load_body(where_ref, w_hbm, *refs):
-    *pieces, out_ref, sems = refs
-    core, here, share, half = where_ref[0], where_ref[1], out_ref.shape[1], COLS // 2
-    pairs = [(w_hbm.at[:, pl.ds(pl.multiple_of(here * share, share), share)], out_ref.at[:COLS, :])]
+    *pieces, w_ref, sems = refs
+    core, here, share, half = where_ref[0], where_ref[1], w_ref.shape[1], COLS // 2
+    pairs = [(w_hbm.at[:, pl.ds(pl.multiple_of(here * share, share), share)], w_ref.at[:COLS, :])]
     for i, piece in enumerate(pieces):
         side = core if i < 3 else 1 - core
         start = pl.multiple_of((i % 3 + 1) * COLS + side * half, half)
-        pairs.append((piece, out_ref.at[pl.ds(start, half), :]))
+        pairs.append((piece, w_ref.at[pl.ds(start, half), :]))
     for copy in fetch(pairs, sems):
         copy.wait()
 
 
-def project_body(where_ref, gx_ref, w_ref, out_ref, tiles_ref, sems):
-    tile, count = out_ref.shape[2], gx_ref.shape[0]
-    gx = [gx_ref[lax.rem(where_ref[1] + count - i, count)] for i in range(count)]
-    gx = jnp.concatenate(gx, axis=1)
+def project_body(w_ref, *refs):
+    *gx_refs, out_hbm, tiles_ref, sems = refs
+    tile = out_hbm.shape[2]
     late = []
-    for j in range(out_ref.shape[0]):
-        tiles_ref[j] = dot(gx, w_ref[:, j * tile : (j + 1) * tile], 1, 0).astype(BF16)
-        copy = pltpu.make_async_copy(tiles_ref.at[j], out_ref.at[j], sems.at[j])
+    for j in range(out_hbm.shape[0]):
+        total = jnp.zeros((TOKENS, tile), F32)
+        for k, gx_ref in enumerate(gx_refs):
+            total = total + dot(gx_ref[...], w_ref[k * COLS : (k + 1) * COLS, j * tile : (j + 1) * tile], 1, 0)
+        tiles_ref[j] = total.astype(BF16)
+        copy = pltpu.make_async_copy(tiles_ref.at[j], out_hbm.at[j], sems.at[j])
         copy.start()
         late.append(copy)
     for copy in late:
@@ -305,28 +314,30 @@
         return lax.ppermute(shard, "core", [(0, 1), (1, 0)])
 
     where = jnp.stack([core, x_index])
-    bc = lax.ppermute(jnp.concatenate([b_proj, c_proj], axis=0), "yh", flip)
-    wx, wdy, mixed, run, cols, ext, b_own, c_own, w_next, w_prev, w_far = call(
+    bc = lax.ppermute(b_proj, "yh", flip), lax.ppermute(c_proj, "yh", flip)
+    wx, wdy, mixed, run, cols, ext, b_own, c_own, w_next, w_prev, w_far, wx_late, wdy_late = call(
         local_body,
         "shhhhhhh",
         [(wide, BF16), (wide, BF16), (square, BF16), ((HEADS, TOKENS), F32), ((TOKENS, 128), F32), ((1, 128), F32)]
         + [(own_half, BF16)] * 2
-        + [((half, share), BF16)] * 3,
+        + [((half, share), BF16)] * 3
+        + [(wide, BF16)] * 2,
         [(wide, BF16), (wide, BF16), ((HEADS, TOKENS), F32), ((HEADS, TOKENS), F32), ((3, half, share), BF16)],
-        copies=12,
-        out_spaces="vvbvbvvvhhh",
+        copies=14,
+        out_spaces="vvbvbvvvhhhhh",
     )(where, x_in, grad_out, step_size, log_decay, b_proj, c_proj, w_in)
-    (send,) = call(ends_body, "vvvvvv", [((STATE, 2 * COLS + 128), BF16)], out_spaces="v")(
-        b_own, c_own, bc, wx, wdy, ext
-    )
+    ends = ((STATE, 2 * COLS + 128), BF16)
+    (send,) = call(ends_body, "vvvvvvv", [ends], [ends], copies=2, out_spaces="h")(b_own, c_own, *bc, wx, wdy, ext)
 
     terms = lax.all_to_all(send, CONTEXT, 0, 0, tiled=True)
     w_next, w_prev, w_far, bc, _ = hold((w_next, w_prev, w_far, bc, send))
     w_prev, w_next, w_far = ahead_on_x(w_next, 1), ahead_on_x(w_prev, 3), ahead_on_x(w_far, 2)
-    local_x, b_rows = call(local_x_body, "vbbvvb", [(wide, F32), (square, BF16)], out_spaces="bb")(
-        grad_out, b_proj, c_proj, bc, run, cols
-    )
-    (scanned,) = call(scan_body, "v", [((STATE, 2 * COLS), BF16)], [((STATE, COLS), F32)], out_spaces="v")(terms)
+    local_x, b_rows = call(local_x_body, "vbbvvvb", [(wide, F32), (square, BF16)], out_spaces="bb")(
+        grad_out, b_proj, c_proj, *bc, run, cols
+    )
+    terms, local_x, b_rows = hold((terms, local_x, b_rows))
+    both = ((STATE, 2 * COLS), BF16)
+    (scanned,) = call(scan_body, "v", [both], [both, ((STATE, COLS), F32)], copies=2, out_spaces="h")(terms)
     states = lax.all_to_all(scanned, CONTEXT, 0, 0, tiled=True)
     w_prev, w_far, w_next, _ = hold((w_prev, w_far, w_next, scanned))
     w_mine = passed(w_prev, w_far, w_next)
@@ -334,30 +345,29 @@
     states, w_mine, w_theirs = hold((states, w_mine, w_theirs))
 
     (gx,) = call(
-        grad_x_body,
-        "hhhv",
-        [((4, *wide), BF16)],
-        [(square, BF16), ((TOKENS, 128), F32), (wide, F32), (wide, BF16)],
-        copies=11,
-        out_spaces="h",
+        grad_x_body, "hhhv", [(wide, BF16)], [(square, BF16), ((TOKENS, 128), F32), (wide, F32)], copies=3, out_spaces="v"
     )(b_rows, cols, local_x, states)
-    gx_x = lax.all_to_all(gx, "x", 0, 0, tiled=True)
+    gx_far = ahead_on_x(gx, 2)
+    gx_prev, gx_next = ahead_on_x(gx, 1), ahead_on_x(gx, 3)
     states, w_mine, _ = hold((states, w_mine, gx))
-    keep_bc, send_bc = call(grad_bc_body, "bbvbvvv", [(square, BF16), (square, BF16)], out_spaces="vv")(
-        b_proj, c_proj, bc, mixed, wx, wdy, states
+    keep_bc, send_bc = call(grad_bc_body, "bbvvbbbv", [(square, BF16), (square, BF16)], out_spaces="vv")(
+        b_proj, c_proj, *bc, mixed, wx_late, wdy_late, states
     )
     got_bc = lax.ppermute(send_bc, "yh", flip)
     (w_here,) = call(load_body, "shhhhhhh", [((4 * COLS, share), BF16)], copies=7, out_spaces="V")(
         where, w_in, *w_mine, *w_theirs
     )
-    gx_x, got_bc, w_here = hold((gx_x, got_bc, w_here))
-
-    (partial,) = call(
-        project_body, "svV", [((4, *square), BF16)], [((4, *square), BF16)], copies=4, out_spaces="h"
-    )(where, gx_x, w_here)
+    gx_prev, gx_far, gx_next, w_here = hold((gx_prev, gx_far, gx_next, w_here))
+
+    four = ((4, *square), BF16)
+    (partial,) = call(project_body, "Vvvvv", [four], [four], copies=4, out_spaces="h")(
+        w_here, gx, gx_prev, gx_far, gx_next
+    )
     over_y = lax.all_to_all(partial, "yh", 0, 0, tiled=True)
     (grad_input,) = call(add_y_body, "v", [(square, BF16)], out_spaces="v")(over_y)
-    grad_b, grad_c = call(add_bc_body, "vv", [(own_half, BF16), (own_half, BF16)], out_spaces="vv")(keep_bc, got_bc)
+    grad_b, grad_c = call(
+        add_bc_body, "vv", [(own_half, BF16), (own_half, BF16)], out_spaces="vv", flops=ADD_FLOPS
+    )(keep_bc, got_bc)
     return grad_input, grad_b, grad_c
 
 

time: 116 us -> 112 us (0.966)
  the two profiles are of different devices: /device:TPU:8 before, /device:TPU:72 now
where the time goes in v3:
time: 112 us; the launch traced here: 111 us
  starting transfers between devices  61.1 us (55%)
  waiting for transfers between devices  30.8 us (28%)
  Pallas kernels  18.5 us (17%)
    ppermute x6, starting transfers between devices, ahead_on_x(): return lax.ppermute(shard, 'x', [(i, (i + ahead) % 4) for i in range(4)])  22.2 us
    pallas_call x10, Pallas kernels, pinned(): run(*(pltpu.with_memory_space_constraint(a, PLACES[k]) if k in PLACES els...  18.5 us
    all_to_all x1, waiting for transfers between devices, per_device(): over_y = lax.all_to_all(partial, 'yh', 0, 0, tiled=True)  13.5 us
    all_to_all x1, starting transfers between devices, per_device(): terms = lax.all_to_all(send, CONTEXT, 0, 0, tiled=True)  11 us
    ppermute x6, waiting for transfers between devices, ahead_on_x(): return lax.ppermute(shard, 'x', [(i, (i + ahead) % 4) for i in range(4)])  8.82 us
    ppermute x2, starting transfers between devices, per_device(): bc = (lax.ppermute(b_proj, 'yh', flip), lax.ppermute(c_proj, 'yh', flip))  6.75 us
    ppermute x3, starting transfers between devices, other_core(): return lax.ppermute(shard, 'core', [(0, 1), (1, 0)])  6.24 us
    all_to_all x1, starting transfers between devices, per_device(): over_y = lax.all_to_all(partial, 'yh', 0, 0, tiled=True)  5.77 us
  transfers between devices with their start and end apart: 15, of which 8 were waited for; matrix products, arithmetic and copies ran while one was open for 0% of the time, Pallas kernels for 14%

profile of v3, /device:TPU:72, one launch (start us, length us, event | category | flops | bytes accessed | tf_op | source)
XLA Modules:
  0.0 111.3 jit_solution(15058642347236277417)
XLA Ops:
  0.6 4.5 %collective-permute-start = (bf16[128,256]{1,0:T(8,128)(2,1)}, bf16[128,256]{1,0:T(8,128)(2,1)S(1)}, u32[]{:S(2)}, u32[]{:S(2)}) collective-permute-start(bf16[128,256]{1,0:T(8,128)(2,1)} %b_ref.3), channel_id=1, source_target_pairs={{0,1},{1,0},{2,3},{3,2},{4,5},{5,4},{6,7},{7,6},{8,9},{9,8},{10,11... | collective-permute-start | bytes 196616 | tf_op jit(solution)/shard_map/ppermute | solution.py:317
  5.1 2.2 %collective-permute-start.1 = (bf16[128,256]{1,0:T(8,128)(2,1)}, bf16[128,256]{1,0:T(8,128)(2,1)S(1)}, u32[]{:S(2)}, u32[]{:S(2)}) collective-permute-start(bf16[128,256]{1,0:T(8,128)(2,1)} %c_ref.3), channel_id=1, source_target_pairs={{0,1},{1,0},{2,3},{3,2},{4,5},{5,4},{6,7},{7,6},{8,9},{9,8},{10,11... | collective-permute-start | bytes 196616 | tf_op jit(solution)/shard_map/ppermute | solution.py:317
  7.4 0.1 pad_add_fusion.where_ref
  7.5 0.0 copy-start.3
  7.5 4.5 %shard_map.94 = (bf16[256,512]{1,0:T(8,128)(2,1)S(1)}, bf16[256,512]{1,0:T(8,128)(2,1)S(1)}, bf16[256,256]{1,0:T(8,128)(2,1)}, f32[8,256]{1,0:T(8,128)S(1)}, f32...) custom-call(s32[2]{0:T(128)S(1)} %pad_add_fusion.where_ref, ...), custom_call_target="tpu_custom_call" | custom-call | flops 1000000000 | bytes 1048576 | tf_op jit(solution)/shard_map/pallas_call | solution.py:52
  11.9 0.0 copy-start.6
  11.9 0.0 collective-permute-done.other_b
  12.0 0.5 collective-permute-done.1.other_c
  12.4 1.1 shard_map.95
  13.5 11.0 %all-to-all-start = ((bf16[32,8,1152]{2,1,0:T(8,128)(2,1)}), bf16[32,8,1152]{2,1,0:T(8,128)(2,1)S(1)}, u32[]{:S(2)}, u32[]{:S(2)}) async-start(bf16[32,8,1152]{2,1,0:T(8,128)(2,1)} %bitcast.9), calls=%async_computation | async-start | bytes 1179648 | tf_op jit(solution)/shard_map/all_to_all | solution.py:332
  24.5 3.4 %collective-permute-start.2 = (bf16[256,1024]{1,0:T(8,128)(2,1)}, bf16[256,1024]{1,0:T(8,128)(2,1)S(1)}, u32[]{:S(2)}, u32[]{:S(2)}) collective-permute-start(bf16[256,1024]{1,0:T(8,128)(2,1)} %get-tuple-element.68), channel_id=1, source_target_pairs={{0,4},{4,8},{8,12},{12,0},{1,5},{5,9},{9,13},{13,1},{2,6},{6,10},{... | collective-permute-start | bytes 1572872 | tf_op jit(solution)/shard_map/ppermute | solution.py:311
  27.9 4.6 %collective-permute-start.3 = (bf16[256,1024]{1,0:T(8,128)(2,1)}, bf16[256,1024]{1,0:T(8,128)(2,1)S(1)}, u32[]{:S(2)}, u32[]{:S(2)}) collective-permute-start(bf16[256,1024]{1,0:T(8,128)(2,1)} %get-tuple-element.69), channel_id=1, source_target_pairs={{0,8},{4,12},{8,0},{12,4},{1,9},{5,13},{9,1},{13,5},{2,10},{6,14},... | collective-permute-start | bytes 1572872 | tf_op jit(solution)/shard_map/ppermute | solution.py:311
  32.6 0.0 copy-done.6
  32.6 3.3 %collective-permute-start.4 = (bf16[256,1024]{1,0:T(8,128)(2,1)S(1)}, bf16[256,1024]{1,0:T(8,128)(2,1)S(1)}, u32[]{:S(2)}, u32[]{:S(2)}) collective-permute-start(bf16[256,1024]{1,0:T(8,128)(2,1)S(1)} %copy-done.6), channel_id=1, source_target_pairs={{0,12},{4,0},{8,4},{12,8},{1,13},{5,1},{9,5},{13,9},{2,14},{6,2},{... | collective-permute-start | bytes 1572872 | tf_op jit(solution)/shard_map/ppermute | solution.py:311
  35.9 0.0 copy-done.3
  36.0 2.6 %shard_map.96 = (f32[256,512]{1,0:T(8,128)}, bf16[256,256]{1,0:T(8,128)(2,1)}) custom-call(bf16[256,512]{1,0:T(8,128)(2,1)S(1)} %copy-done.3, bf16[128,256]{1,0:T(8,128)(2,1)} %b_ref.3, bf16[128,256]{1,0:T(8,128)(2,1)} %c_ref.3, bf16[128,256]{1,0:T(8,128)(2,1)S(1)} %collective-permute-done.other_b, bf16[128,256]{1,0:T(8,128)(2,1)S(1)} %collective-permute-done.1.other_c, ...), custom_call_target="tpu_custom_call" | custom-call | flops 1000000000 | bytes 1048576 | tf_op jit(solution)/shard_map/pallas_call | solution.py:52
  38.6 4.2 %all-to-all-done = bf16[32,8,1152]{2,1,0:T(8,128)(2,1)S(1)} async-done(((bf16[32,8,1152]{2,1,0:T(8,128)(2,1)}), bf16[32,8,1152]{2,1,0:T(8,128)(2,1)S(1)}, u32[]{:S(2)}, u32[]{:S(2)}) %all-to-all-start) | async-done | bytes 589856 | tf_op jit(solution)/shard_map/all_to_all | solution.py:332
  42.8 1.0 shard_map.97
  43.8 5.0 %all-to-all-start.1 = ((bf16[32,8,1024]{2,1,0:T(8,128)(2,1)}), bf16[32,8,1024]{2,1,0:T(8,128)(2,1)S(1)}, u32[]{:S(2)}, u32[]{:S(2)}) async-start(bf16[32,8,1024]{2,1,0:T(8,128)(2,1)} %bitcast.10), calls=%async_computation.1 | async-start | bytes 1048576 | tf_op jit(solution)/shard_map/all_to_all | solution.py:341
  48.8 0.0 collective-permute-done.2.refs_0_
  48.8 5.2 %collective-permute-done.3.refs_1_ = bf16[256,1024]{1,0:T(8,128)(2,1)S(1)} collective-permute-done((bf16[256,1024]{1,0:T(8,128)(2,1)}, bf16[256,1024]{1,0:T(8,128)(2,1)S(1)}, u32[]{:S(2)}, u32[]{:S(2)}) %collective-permute-start.3) | collective-permute-done | bytes 524320 | tf_op jit(solution)/shard_map/ppermute | solution.py:311
  54.0 1.6 %collective-permute-done.4.refs_2_ = bf16[256,1024]{1,0:T(8,128)(2,1)S(1)} collective-permute-done((bf16[256,1024]{1,0:T(8,128)(2,1)S(1)}, bf16[256,1024]{1,0:T(8,128)(2,1)S(1)}, u32[]{:S(2)}, u32[]{:S(2)}) %collective-permute-start.4) | collective-permute-done | bytes 524320 | tf_op jit(solution)/shard_map/ppermute | solution.py:311
  55.6 0.0 copy-start
  55.6 0.0 copy-start.1
  55.6 0.0 copy-start.2
  55.6 1.9 %collective-permute-start.5 = (bf16[256,1024]{1,0:T(8,128)(2,1)S(1)}, bf16[256,1024]{1,0:T(8,128)(2,1)S(1)}, u32[]{:S(2)}, u32[]{:S(2)}) collective-permute-start(bf16[256,1024]{1,0:T(8,128)(2,1)S(1)} %get-tuple-element.81.refs_0_), channel_id=1, source_target_pairs={{0,16},{16,0},{1,17},{17,1},{2,18},{18,2},{3,19},{19,3},{4,20},{20... | collective-permute-start | bytes 1572872 | tf_op jit(solution)/shard_map/ppermute | solution.py:314
  57.5 2.4 %collective-permute-start.6 = (bf16[256,1024]{1,0:T(8,128)(2,1)S(1)}, bf16[256,1024]{1,0:T(8,128)(2,1)S(1)}, u32[]{:S(2)}, u32[]{:S(2)}) collective-permute-start(bf16[256,1024]{1,0:T(8,128)(2,1)S(1)} %get-tuple-element.82.refs_1_), channel_id=1, source_target_pairs={{0,16},{16,0},{1,17},{17,1},{2,18},{18,2},{3,19},{19,3},{4,20},{20... | collective-permute-start | bytes 1572872 | tf_op jit(solution)/shard_map/ppermute | solution.py:314
  59.9 1.9 %collective-permute-start.7 = (bf16[256,1024]{1,0:T(8,128)(2,1)S(1)}, bf16[256,1024]{1,0:T(8,128)(2,1)}, u32[]{:S(2)}, u32[]{:S(2)}) collective-permute-start(bf16[256,1024]{1,0:T(8,128)(2,1)S(1)} %get-tuple-element.83.refs_2_), channel_id=1, source_target_pairs={{0,16},{16,0},{1,17},{17,1},{2,18},{18,2},{3,19},{19,3},{4,20},{20... | collective-permute-start | bytes 1572872 | tf_op jit(solution)/shard_map/ppermute | solution.py:314
  61.9 0.0 collective-permute-done.5.refs_3_
  61.9 0.0 copy-start.4
  61.9 0.0 collective-permute-done.6.refs_4_
  61.9 0.0 copy-start.5
  61.9 2.0 %collective-permute-done.7.refs_5_ = bf16[256,1024]{1,0:T(8,128)(2,1)} collective-permute-done((bf16[256,1024]{1,0:T(8,128)(2,1)S(1)}, bf16[256,1024]{1,0:T(8,128)(2,1)}, u32[]{:S(2)}, u32[]{:S(2)}) %collective-permute-start.7) | collective-permute-done | bytes 524320 | tf_op jit(solution)/shard_map/ppermute | solution.py:314
  63.9 1.8 %all-to-all-done.1 = bf16[32,8,1024]{2,1,0:T(8,128)(2,1)S(1)} async-done(((bf16[32,8,1024]{2,1,0:T(8,128)(2,1)}), bf16[32,8,1024]{2,1,0:T(8,128)(2,1)S(1)}, u32[]{:S(2)}, u32[]{:S(2)}) %all-to-all-start.1) | async-done | bytes 524320 | tf_op jit(solution)/shard_map/all_to_all | solution.py:341
  65.7 1.6 %shard_map.99.refs_0_ = bf16[256,512]{1,0:T(8,128)(2,1)S(1)} custom-call(bf16[256,256]{1,0:T(8,128)(2,1)} %get-tuple-element.65.bt_hbm, f32[256,128]{1,0:T(8,128)} %get-tuple-element.62.cols_ref.cols_hbm, f32[256,512]{1,0:T(8,128)} %get-tuple-element.66.loc_hbm, bf16[256,1024]{1,0:T(8,128)(2,1)S(1)} %bitcast.7), custom_call_target="tpu_custom_call" | custom-call | flops 1000000000 | bytes 1048576 | tf_op jit(solution)/shard_map/pallas_call | solution.py:52
  67.3 4.7 %collective-permute-start.10 = (bf16[256,512]{1,0:T(8,128)(2,1)S(1)}, bf16[256,512]{1,0:T(8,128)(2,1)S(1)}, u32[]{:S(2)}, u32[]{:S(2)}) collective-permute-start(bf16[256,512]{1,0:T(8,128)(2,1)S(1)} %shard_map.99.refs_0_), channel_id=1, source_target_pairs={{0,12},{4,0},{8,4},{12,8},{1,13},{5,1},{9,5},{13,9},{2,14},{6,2},{... | collective-permute-start | bytes 786440 | tf_op jit(solution)/shard_map/ppermute | solution.py:311
  71.9 1.9 %collective-permute-start.8 = (bf16[256,512]{1,0:T(8,128)(2,1)S(1)}, bf16[256,512]{1,0:T(8,128)(2,1)S(1)}, u32[]{:S(2)}, u32[]{:S(2)}) collective-permute-start(bf16[256,512]{1,0:T(8,128)(2,1)S(1)} %shard_map.99.refs_0_), channel_id=1, source_target_pairs={{0,4},{4,8},{8,12},{12,0},{1,5},{5,9},{9,13},{13,1},{2,6},{6,10},{... | collective-permute-start | bytes 786440 | tf_op jit(solution)/shard_map/ppermute | solution.py:311
  73.9 4.2 %collective-permute-start.9 = (bf16[256,512]{1,0:T(8,128)(2,1)S(1)}, bf16[256,512]{1,0:T(8,128)(2,1)S(1)}, u32[]{:S(2)}, u32[]{:S(2)}) collective-permute-start(bf16[256,512]{1,0:T(8,128)(2,1)S(1)} %shard_map.99.refs_0_), channel_id=1, source_target_pairs={{0,8},{4,12},{8,0},{12,4},{1,9},{5,13},{9,1},{13,5},{2,10},{6,14},... | collective-permute-start | bytes 786440 | tf_op jit(solution)/shard_map/ppermute | solution.py:311
  78.1 1.6 %shard_map.103 = (bf16[256,256]{1,0:T(8,128)(2,1)S(1)}, bf16[256,256]{1,0:T(8,128)(2,1)S(1)}) custom-call(bf16[128,256]{1,0:T(8,128)(2,1)} %b_ref.3, bf16[128,256]{1,0:T(8,128)(2,1)} %c_ref.3, bf16[128,256]{1,0:T(8,128)(2,1)S(1)} %collective-permute-done.other_b, bf16[128,256]{1,0:T(8,128)(2,1)S(1)} %collective-permute-done.1.other_c, ...), custom_call_target="tpu_custom_call" | custom-call | flops 1000000000 | bytes 1048576 | tf_op jit(solution)/shard_map/pallas_call | solution.py:52
  79.6 4.1 %collective-permute-start.11 = (bf16[256,256]{1,0:T(8,128)(2,1)S(1)}, bf16[256,256]{1,0:T(8,128)(2,1)S(1)}, u32[]{:S(2)}, u32[]{:S(2)}) collective-permute-start(bf16[256,256]{1,0:T(8,128)(2,1)S(1)} %get-tuple-element.96), channel_id=1, source_target_pairs={{0,1},{1,0},{2,3},{3,2},{4,5},{5,4},{6,7},{7,6},{8,9},{9,8},{10,11... | collective-permute-start | bytes 393224 | tf_op jit(solution)/shard_map/ppermute | solution.py:356
  83.7 0.0 copy-done
  83.7 0.0 copy-done.1
  83.7 0.0 copy-done.2
  83.7 0.0 copy-done.4
  83.7 0.0 copy-done.5
  83.8 2.8 %shard_map.100.w_ref = bf16[2048,1024]{1,0:T(8,128)(2,1)S(1)} custom-call(s32[2]{0:T(128)S(1)} %pad_add_fusion.where_ref, bf16[512,4096]{1,0:T(8,128)(2,1)} %w_hbm.3, bf16[256,1024]{1,0:T(8,128)(2,1)} %copy-done, bf16[256,1024]{1,0:T(8,128)(2,1)} %copy-done.1, bf16[256,1024]{1,0:T(8,128)(2,1)} %copy-done.2, bf16[256,1024]{1,0:T(8,128)(2,1)} %copy-done.4, ...), custom_call_target="tpu_custom_call" | custom-call | flops 1000000000 | bytes 1048576 | tf_op jit(solution)/shard_map/pallas_call | solution.py:52
  86.5 0.0 collective-permute-done.10.refs_3_
  86.5 2.1 %collective-permute-done.8.refs_1_ = bf16[256,512]{1,0:T(8,128)(2,1)S(1)} collective-permute-done((bf16[256,512]{1,0:T(8,128)(2,1)S(1)}, bf16[256,512]{1,0:T(8,128)(2,1)S(1)}, u32[]{:S(2)}, u32[]{:S(2)}) %collective-permute-start.8) | collective-permute-done | bytes 262176 | tf_op jit(solution)/shard_map/ppermute | solution.py:311
  88.6 0.0 collective-permute-done.9.refs_2_
  88.6 2.0 %shard_map.101 = bf16[4,256,256]{2,1,0:T(8,128)(2,1)} custom-call(bf16[2048,1024]{1,0:T(8,128)(2,1)S(1)} %shard_map.100.w_ref, bf16[256,512]{1,0:T(8,128)(2,1)S(1)} %shard_map.99.refs_0_, bf16[256,512]{1,0:T(8,128)(2,1)S(1)} %collective-permute-done.8.refs_1_, bf16[256,512]{1,0:T(8,128)(2,1)S(1)} %collective-permute-done.9.refs_2_, ...), custom_call_target="tpu_custom_call" | custom-call | flops 1000000000 | bytes 1048576 | tf_op jit(solution)/shard_map/pallas_call | solution.py:52
  90.6 5.8 %all-to-all-start.2 = ((bf16[4,256,256]{2,1,0:T(8,128)(2,1)}), bf16[4,256,256]{2,1,0:T(8,128)(2,1)S(1)}, u32[]{:S(2)}, u32[]{:S(2)}) async-start(bf16[4,256,256]{2,1,0:T(8,128)(2,1)} %shard_map.101), calls=%async_computation.2 | async-start | bytes 1048576 | tf_op jit(solution)/shard_map/all_to_all | solution.py:366
  96.4 0.0 collective-permute-done.11.got_ref
  96.4 0.7 shard_map.104
  97.0 13.5 %all-to-all-done.2.got_ref = bf16[4,256,256]{2,1,0:T(8,128)(2,1)S(1)} async-done(((bf16[4,256,256]{2,1,0:T(8,128)(2,1)}), bf16[4,256,256]{2,1,0:T(8,128)(2,1)S(1)}, u32[]{:S(2)}, u32[]{:S(2)}) %all-to-all-start.2) | async-done | bytes 524320 | tf_op jit(solution)/shard_map/all_to_all | solution.py:366
  110.5 0.8 shard_map.102
  (1 shorter events, 0.0 us)
Async XLA Ops:
  0.6 11.3 %collective-permute-start = (bf16[128,256]{1,0:T(8,128)(2,1)}, bf16[128,256]{1,0:T(8,128)(2,1)S(1)}, u32[]{:S(2)}, u32[]{:S(2)}) collective-permute-start(bf16[128,256]{1,0:T(8,128)(2,1)} %b_ref.3), channel_id=1, source_target_pairs={{0,1},{1,0},{2,3},{3,2},{4,5},{5,4},{6,7},{7,6},{8,9},{9,8},{10,11... | collective-permute-start | bytes 196616 | tf_op jit(solution)/shard_map/ppermute | solution.py:317
  5.1 7.3 %collective-permute-start.1 = (bf16[128,256]{1,0:T(8,128)(2,1)}, bf16[128,256]{1,0:T(8,128)(2,1)S(1)}, u32[]{:S(2)}, u32[]{:S(2)}) collective-permute-start(bf16[128,256]{1,0:T(8,128)(2,1)} %c_ref.3), channel_id=1, source_target_pairs={{0,1},{1,0},{2,3},{3,2},{4,5},{5,4},{6,7},{7,6},{8,9},{9,8},{10,11... | collective-permute-start | bytes 196616 | tf_op jit(solution)/shard_map/ppermute | solution.py:317
  7.5 28.5 %copy-start.3 = (bf16[256,512]{1,0:T(8,128)(2,1)S(1)}, bf16[256,512]{1,0:T(8,128)(2,1)}, u32[]{:S(2)}) copy-start(bf16[256,512]{1,0:T(8,128)(2,1)} %dy_ref.1) | copy-start | bytes 786436
  11.9 20.7 %copy-start.6 = (bf16[256,1024]{1,0:T(8,128)(2,1)S(1)}, bf16[256,1024]{1,0:T(8,128)(2,1)}, u32[]{:S(2)}) copy-start(bf16[256,1024]{1,0:T(8,128)(2,1)} %get-tuple-element.70) | copy-start | bytes 1572868
  13.5 29.3 %all-to-all-start = ((bf16[32,8,1152]{2,1,0:T(8,128)(2,1)}), bf16[32,8,1152]{2,1,0:T(8,128)(2,1)S(1)}, u32[]{:S(2)}, u32[]{:S(2)}) async-start(bf16[32,8,1152]{2,1,0:T(8,128)(2,1)} %bitcast.9), calls=%async_computation | async-start | bytes 1179648 | tf_op jit(solution)/shard_map/all_to_all | solution.py:332
  24.5 24.3 %collective-permute-start.2 = (bf16[256,1024]{1,0:T(8,128)(2,1)}, bf16[256,1024]{1,0:T(8,128)(2,1)S(1)}, u32[]{:S(2)}, u32[]{:S(2)}) collective-permute-start(bf16[256,1024]{1,0:T(8,128)(2,1)} %get-tuple-element.68), channel_id=1, source_target_pairs={{0,4},{4,8},{8,12},{12,0},{1,5},{5,9},{9,13},{13,1},{2,6},{6,10},{... | collective-permute-start | bytes 1572872 | tf_op jit(solution)/shard_map/ppermute | solution.py:311
  27.9 26.1 %collective-permute-start.3 = (bf16[256,1024]{1,0:T(8,128)(2,1)}, bf16[256,1024]{1,0:T(8,128)(2,1)S(1)}, u32[]{:S(2)}, u32[]{:S(2)}) collective-permute-start(bf16[256,1024]{1,0:T(8,128)(2,1)} %get-tuple-element.69), channel_id=1, source_target_pairs={{0,8},{4,12},{8,0},{12,4},{1,9},{5,13},{9,1},{13,5},{2,10},{6,14},... | collective-permute-start | bytes 1572872 | tf_op jit(solution)/shard_map/ppermute | solution.py:311
  32.6 23.0 %collective-permute-start.4 = (bf16[256,1024]{1,0:T(8,128)(2,1)S(1)}, bf16[256,1024]{1,0:T(8,128)(2,1)S(1)}, u32[]{:S(2)}, u32[]{:S(2)}) collective-permute-start(bf16[256,1024]{1,0:T(8,128)(2,1)S(1)} %copy-done.6), channel_id=1, source_target_pairs={{0,12},{4,0},{8,4},{12,8},{1,13},{5,1},{9,5},{13,9},{2,14},{6,2},{... | collective-permute-start | bytes 1572872 | tf_op jit(solution)/shard_map/ppermute | solution.py:311
  43.8 21.9 %all-to-all-start.1 = ((bf16[32,8,1024]{2,1,0:T(8,128)(2,1)}), bf16[32,8,1024]{2,1,0:T(8,128)(2,1)S(1)}, u32[]{:S(2)}, u32[]{:S(2)}) async-start(bf16[32,8,1024]{2,1,0:T(8,128)(2,1)} %bitcast.10), calls=%async_computation.1 | async-start | bytes 1048576 | tf_op jit(solution)/shard_map/all_to_all | solution.py:341
  55.6 28.1 %copy-start = (bf16[256,1024]{1,0:T(8,128)(2,1)}, bf16[256,1024]{1,0:T(8,128)(2,1)S(1)}, u32[]{:S(2)}) copy-start(bf16[256,1024]{1,0:T(8,128)(2,1)S(1)} %get-tuple-element.81.refs_0_) | copy-start | bytes 1572868
  55.6 28.1 %copy-start.1 = (bf16[256,1024]{1,0:T(8,128)(2,1)}, bf16[256,1024]{1,0:T(8,128)(2,1)S(1)}, u32[]{:S(2)}) copy-start(bf16[256,1024]{1,0:T(8,128)(2,1)S(1)} %get-tuple-element.82.refs_1_) | copy-start | bytes 1572868
  55.6 28.1 %copy-start.2 = (bf16[256,1024]{1,0:T(8,128)(2,1)}, bf16[256,1024]{1,0:T(8,128)(2,1)S(1)}, u32[]{:S(2)}) copy-start(bf16[256,1024]{1,0:T(8,128)(2,1)S(1)} %get-tuple-element.83.refs_2_) | copy-start | bytes 1572868
  55.6 6.3 %collective-permute-start.5 = (bf16[256,1024]{1,0:T(8,128)(2,1)S(1)}, bf16[256,1024]{1,0:T(8,128)(2,1)S(1)}, u32[]{:S(2)}, u32[]{:S(2)}) collective-permute-start(bf16[256,1024]{1,0:T(8,128)(2,1)S(1)} %get-tuple-element.81.refs_0_), channel_id=1, source_target_pairs={{0,16},{16,0},{1,17},{17,1},{2,18},{18,2},{3,19},{19,3},{4,20},{20... | collective-permute-start | bytes 1572872 | tf_op jit(solution)/shard_map/ppermute | solution.py:314
  57.5 4.4 %collective-permute-start.6 = (bf16[256,1024]{1,0:T(8,128)(2,1)S(1)}, bf16[256,1024]{1,0:T(8,128)(2,1)S(1)}, u32[]{:S(2)}, u32[]{:S(2)}) collective-permute-start(bf16[256,1024]{1,0:T(8,128)(2,1)S(1)} %get-tuple-element.82.refs_1_), channel_id=1, source_target_pairs={{0,16},{16,0},{1,17},{17,1},{2,18},{18,2},{3,19},{19,3},{4,20},{20... | collective-permute-start | bytes 1572872 | tf_op jit(solution)/shard_map/ppermute | solution.py:314
  59.9 3.9 %collective-permute-start.7 = (bf16[256,1024]{1,0:T(8,128)(2,1)S(1)}, bf16[256,1024]{1,0:T(8,128)(2,1)}, u32[]{:S(2)}, u32[]{:S(2)}) collective-permute-start(bf16[256,1024]{1,0:T(8,128)(2,1)S(1)} %get-tuple-element.83.refs_2_), channel_id=1, source_target_pairs={{0,16},{16,0},{1,17},{17,1},{2,18},{18,2},{3,19},{19,3},{4,20},{20... | collective-permute-start | bytes 1572872 | tf_op jit(solution)/shard_map/ppermute | solution.py:314
  61.9 21.8 %copy-start.4 = (bf16[256,1024]{1,0:T(8,128)(2,1)}, bf16[256,1024]{1,0:T(8,128)(2,1)S(1)}, u32[]{:S(2)}) copy-start(bf16[256,1024]{1,0:T(8,128)(2,1)S(1)} %collective-permute-done.5.refs_3_) | copy-start | bytes 1572868
  61.9 21.8 %copy-start.5 = (bf16[256,1024]{1,0:T(8,128)(2,1)}, bf16[256,1024]{1,0:T(8,128)(2,1)S(1)}, u32[]{:S(2)}) copy-start(bf16[256,1024]{1,0:T(8,128)(2,1)S(1)} %collective-permute-done.6.refs_4_) | copy-start | bytes 1572868
  67.3 19.3 %collective-permute-start.10 = (bf16[256,512]{1,0:T(8,128)(2,1)S(1)}, bf16[256,512]{1,0:T(8,128)(2,1)S(1)}, u32[]{:S(2)}, u32[]{:S(2)}) collective-permute-start(bf16[256,512]{1,0:T(8,128)(2,1)S(1)} %shard_map.99.refs_0_), channel_id=1, source_target_pairs={{0,12},{4,0},{8,4},{12,8},{1,13},{5,1},{9,5},{13,9},{2,14},{6,2},{... | collective-permute-start | bytes 786440 | tf_op jit(solution)/shard_map/ppermute | solution.py:311
  71.9 16.7 %collective-permute-start.8 = (bf16[256,512]{1,0:T(8,128)(2,1)S(1)}, bf16[256,512]{1,0:T(8,128)(2,1)S(1)}, u32[]{:S(2)}, u32[]{:S(2)}) collective-permute-start(bf16[256,512]{1,0:T(8,128)(2,1)S(1)} %shard_map.99.refs_0_), channel_id=1, source_target_pairs={{0,4},{4,8},{8,12},{12,0},{1,5},{5,9},{9,13},{13,1},{2,6},{6,10},{... | collective-permute-start | bytes 786440 | tf_op jit(solution)/shard_map/ppermute | solution.py:311
  73.9 14.7 %collective-permute-start.9 = (bf16[256,512]{1,0:T(8,128)(2,1)S(1)}, bf16[256,512]{1,0:T(8,128)(2,1)S(1)}, u32[]{:S(2)}, u32[]{:S(2)}) collective-permute-start(bf16[256,512]{1,0:T(8,128)(2,1)S(1)} %shard_map.99.refs_0_), channel_id=1, source_target_pairs={{0,8},{4,12},{8,0},{12,4},{1,9},{5,13},{9,1},{13,5},{2,10},{6,14},... | collective-permute-start | bytes 786440 | tf_op jit(solution)/shard_map/ppermute | solution.py:311
  79.6 16.7 %collective-permute-start.11 = (bf16[256,256]{1,0:T(8,128)(2,1)S(1)}, bf16[256,256]{1,0:T(8,128)(2,1)S(1)}, u32[]{:S(2)}, u32[]{:S(2)}) collective-permute-start(bf16[256,256]{1,0:T(8,128)(2,1)S(1)} %get-tuple-element.96), channel_id=1, source_target_pairs={{0,1},{1,0},{2,3},{3,2},{4,5},{5,4},{6,7},{7,6},{8,9},{9,8},{10,11... | collective-permute-start | bytes 393224 | tf_op jit(solution)/shard_map/ppermute | solution.py:356
  90.6 20.0 %all-to-all-start.2 = ((bf16[4,256,256]{2,1,0:T(8,128)(2,1)}), bf16[4,256,256]{2,1,0:T(8,128)(2,1)S(1)}, u32[]{:S(2)}, u32[]{:S(2)}) async-start(bf16[4,256,256]{2,1,0:T(8,128)(2,1)} %shard_map.101), calls=%async_computation.2 | async-start | bytes 1048576 | tf_op jit(solution)/shard_map/all_to_all | solution.py:366

commit v4 on v3

--- a/solution.py
+++ b/solution.py
@@ -94,10 +94,10 @@
     return dot(ext, jnp.where(spread, 1.0, 0.0).astype(BF16), 1, 0)
 
 
-def local_body(
+def weights_body(
     where_ref, x_hbm, dy_hbm, dt_hbm, ld_hbm, b_hbm, c_hbm, w_hbm,
-    wx_ref, wdy_ref, ms_ref, run_ref, cols_ref, ext_ref, b_ref, c_ref, w1_hbm, w3_hbm, w2_hbm, wx_hbm, wdy_hbm,
-    x_ref, dy_ref, dt_ref, ld_ref, w_ref, sems,
+    wx_ref, wdy_ref, run_ref, cols_hbm, ext_ref, b_ref, c_ref, w1_hbm, w3_hbm, w2_hbm, wx_hbm, wdy_hbm, fwd_hbm,
+    x_ref, dy_ref, dt_ref, ld_ref, cols_ref, w_ref, fwd_ref, sems,
 ):
     rows, share = w1_hbm.shape
     down = pl.ds(pl.multiple_of(where_ref[0] * rows, rows), rows)
@@ -106,6 +106,12 @@
         across = pl.ds(pl.multiple_of(lax.rem(where_ref[1] + ahead, 4) * share, share), share)
         pieces.append((w_hbm.at[down, across], w_ref.at[i]))
     late = fetch(pieces, sems)
+    out = []
+
+    def put(source, target):
+        out.append(pltpu.make_async_copy(source, target, sems.at[len(pieces) + len(out)]))
+        out[-1].start()
+
     late[0].wait()
     tri = jnp.where(iota((TOKENS, TOKENS), 0) <= iota((TOKENS, TOKENS), 1), 1.0, 0.0).astype(BF16)
     parts = jnp.concatenate(split3(ld_ref[...]), axis=0).astype(BF16)
@@ -116,12 +122,15 @@
     dt = dt_ref[...]
     end = run[:, TOKENS - 1 :]
     fwd = dt * jnp.exp(end - run)
+    fwd_ref[...] = fwd
+    put(fwd_ref, fwd_hbm)
     start = jnp.exp(run)
     stack = jnp.concatenate(
         [run, dt, fwd, start, jnp.zeros((128 - 4 * HEADS, TOKENS), F32)], axis=0
     )
     cols = stack.T
     cols_ref[...] = cols
+    put(cols_ref, cols_hbm)
 
     hi, mid, low = split3(jnp.exp(end))
     lane8, row8 = iota((HEADS, 128), 1), iota((HEADS, 128), 0)
@@ -130,32 +139,21 @@
     spread = spread + jnp.where(lane8 == row8 + 2 * HEADS, low, 0.0)
     ext_ref[...] = jnp.sum(spread, axis=0, keepdims=True)
 
+    lane = iota((TOKENS, 128), 1)
     late[2].wait()
+    for i in range(HEADS // 2):
+        at = slice(128 * i, 128 * (i + 1))
+        wx_ref[:, at] = (pair(cols, 2 * HEADS + 2 * i, lane) * x_ref[:, at].astype(F32)).astype(BF16)
+    put(wx_ref, wx_hbm)
     late[3].wait()
-    lane = iota((TOKENS, 128), 1)
-    total = jnp.zeros((TOKENS, TOKENS), F32)
     for i in range(HEADS // 2):
-        if i == HEADS // 2 - 2:
-            for copy in late[4:]:
-                copy.wait()
-            out = [pltpu.make_async_copy(w_ref.at[k], w, sems.at[9 + k]) for k, w in enumerate((w1_hbm, w3_hbm, w2_hbm))]
-            for copy in out:
-                copy.start()
         at = slice(128 * i, 128 * (i + 1))
-        xp, dyp = x_ref[:, at], dy_ref[:, at]
-        wx_ref[:, at] = (pair(cols, 2 * HEADS + 2 * i, lane) * xp.astype(F32)).astype(BF16)
-        wdy_ref[:, at] = (pair(cols, 3 * HEADS + 2 * i, lane) * dyp.astype(F32)).astype(BF16)
-        for k in range(2):
-            h = 2 * i + k
-            own = (lane < WIDTH) if k == 0 else (lane >= WIDTH)
-            inter = dot(jnp.where(own, xp, jnp.zeros_like(xp)), dyp, 1, 1)
-            decay = pair_decay(run, cols, h)
-            mixing = (decay * inter * cols[:, HEADS + h : HEADS + h + 1]).astype(BF16)
-            total = total + mixing.astype(F32)
-    ms_ref[...] = total.astype(BF16)
-    for i, (a, b) in enumerate(((wx_ref, wx_hbm), (wdy_ref, wdy_hbm))):
-        out.append(pltpu.make_async_copy(a, b, sems.at[12 + i]))
-        out[-1].start()
+        wdy_ref[:, at] = (pair(cols, 3 * HEADS + 2 * i, lane) * dy_ref[:, at].astype(F32)).astype(BF16)
+    put(wdy_ref, wdy_hbm)
+    for copy in late[4:]:
+        copy.wait()
+    for k, w in enumerate((w1_hbm, w3_hbm, w2_hbm)):
+        put(w_ref.at[k], w)
     for copy in out:
         copy.wait()
 
@@ -201,33 +199,41 @@
         copy.wait()
 
 
-def local_x_body(dy_ref, b_ref, c_ref, other_b, other_c, run_ref, cols_ref, loc_ref, bt_ref):
+def local_x_body(x_ref, dy_ref, b_ref, c_ref, other_b, other_c, run_ref, cols_ref, loc_ref, bt_ref, ms_ref):
     run, cols = run_ref[...], cols_ref[...]
     bt = whole(b_ref, other_b[...]).T
     bt_ref[...] = bt
     score = dot(bt, whole(c_ref, other_c[...]), 1, 0)
     lane = iota((TOKENS, 128), 1)
+    total = jnp.zeros((TOKENS, TOKENS), F32)
     for i in range(HEADS // 2):
         at = slice(128 * i, 128 * (i + 1))
-        dyp = dy_ref[:, at]
+        xp, dyp = x_ref[:, at], dy_ref[:, at]
         local = []
         for k in range(2):
-            kernel = (pair_decay(run, cols, 2 * i + k) * score).astype(BF16)
-            local.append(dot(kernel, dyp, 1, 0))
-        loc_ref[:, at] = pair(cols, HEADS + 2 * i, lane) * jnp.where(lane < WIDTH, local[0], local[1])
-
-
-def grad_x_body(bt_hbm, cols_hbm, loc_hbm, states_ref, gx_ref, bt_ref, cols_ref, loc_ref, sems):
-    early = fetch([(bt_hbm, bt_ref), (cols_hbm, cols_ref), (loc_hbm, loc_ref)], sems)
+            h = 2 * i + k
+            own = (lane < WIDTH) if k == 0 else (lane >= WIDTH)
+            decay = pair_decay(run, cols, h)
+            inter = dot(jnp.where(own, xp, jnp.zeros_like(xp)), dyp, 1, 1)
+            mixing = (decay * inter * cols[:, HEADS + h : HEADS + h + 1]).astype(BF16)
+            total = total + mixing.astype(F32)
+            local.append(dot((decay * score).astype(BF16), dyp, 1, 0))
+        local = pair(cols, HEADS + 2 * i, lane) * jnp.where(lane < WIDTH, local[0], local[1])
+        loc_ref[:, at] = local.astype(BF16)
+    ms_ref[...] = total.astype(BF16)
+
+
+def grad_x_body(bt_hbm, fwd_hbm, loc_hbm, states_ref, gx_ref, bt_ref, fwd_ref, loc_ref, sems):
+    early = fetch([(bt_hbm, bt_ref), (fwd_hbm, fwd_ref), (loc_hbm, loc_ref)], sems)
     lane = iota((TOKENS, 128), 1)
+    early[1].wait()
+    cols = jnp.concatenate([fwd_ref[...], jnp.zeros((128 - HEADS, TOKENS), F32)], axis=0).T
     early[0].wait()
-    carried = dot(bt_ref[...], states_ref[:, COLS:], 1, 0)
-    early[1].wait()
     early[2].wait()
     for i in range(HEADS // 2):
         at = slice(128 * i, 128 * (i + 1))
-        fwd = pair(cols_ref[...], 2 * HEADS + 2 * i, lane)
-        gx_ref[:, at] = (loc_ref[:, at] + fwd * carried[:, at]).astype(BF16)
+        carried = dot(bt_ref[...], states_ref[:, COLS + 128 * i : COLS + 128 * (i + 1)], 1, 0)
+        gx_ref[:, at] = (loc_ref[:, at].astype(F32) + pair(cols, 2 * i, lane) * carried).astype(BF16)
 
 
 def grad_bc_body(b_ref, c_ref, other_b, other_c, ms_ref, wx_ref, wdy_ref, states_ref, keep_ref, send_ref):
@@ -315,16 +321,18 @@
 
     where = jnp.stack([core, x_index])
     bc = lax.ppermute(b_proj, "yh", flip), lax.ppermute(c_proj, "yh", flip)
-    wx, wdy, mixed, run, cols, ext, b_own, c_own, w_next, w_prev, w_far, wx_late, wdy_late = call(
-        local_body,
+    wx, wdy, run, cols, ext, b_own, c_own, w_next, w_prev, w_far, wx_late, wdy_late, fwd = call(
+        weights_body,
         "shhhhhhh",
-        [(wide, BF16), (wide, BF16), (square, BF16), ((HEADS, TOKENS), F32), ((TOKENS, 128), F32), ((1, 128), F32)]
+        [(wide, BF16), (wide, BF16), ((HEADS, TOKENS), F32), ((TOKENS, 128), F32), ((1, 128), F32)]
         + [(own_half, BF16)] * 2
         + [((half, share), BF16)] * 3
-        + [(wide, BF16)] * 2,
-        [(wide, BF16), (wide, BF16), ((HEADS, TOKENS), F32), ((HEADS, TOKENS), F32), ((3, half, share), BF16)],
-        copies=14,
-        out_spaces="vvbvbvvvhhhhh",
+        + [(wide, BF16)] * 2
+        + [((HEADS, TOKENS), F32)],
+        [(wide, BF16), (wide, BF16), ((HEADS, TOKENS), F32), ((HEADS, TOKENS), F32)]
+        + [((TOKENS, 128), F32), ((3, half, share), BF16), ((HEADS, TOKENS), F32)],
+        copies=16,
+        out_spaces="vvvhvvvhhhhhh",
     )(where, x_in, grad_out, step_size, log_decay, b_proj, c_proj, w_in)
     ends = ((STATE, 2 * COLS + 128), BF16)
     (send,) = call(ends_body, "vvvvvvv", [ends], [ends], copies=2, out_spaces="h")(b_own, c_own, *bc, wx, wdy, ext)
@@ -332,10 +340,10 @@
     terms = lax.all_to_all(send, CONTEXT, 0, 0, tiled=True)
     w_next, w_prev, w_far, bc, _ = hold((w_next, w_prev, w_far, bc, send))
     w_prev, w_next, w_far = ahead_on_x(w_next, 1), ahead_on_x(w_prev, 3), ahead_on_x(w_far, 2)
-    local_x, b_rows = call(local_x_body, "vbbvvvb", [(wide, F32), (square, BF16)], out_spaces="bb")(
-        grad_out, b_proj, c_proj, *bc, run, cols
-    )
-    terms, local_x, b_rows = hold((terms, local_x, b_rows))
+    local_x, b_rows, mixed = call(
+        local_x_body, "bbbbvvvb", [(wide, BF16), (square, BF16), (square, BF16)], out_spaces="bbb"
+    )(x_in, grad_out, b_proj, c_proj, *bc, run, cols)
+    terms, local_x, b_rows, mixed = hold((terms, local_x, b_rows, mixed))
     both = ((STATE, 2 * COLS), BF16)
     (scanned,) = call(scan_body, "v", [both], [both, ((STATE, COLS), F32)], copies=2, out_spaces="h")(terms)
     states = lax.all_to_all(scanned, CONTEXT, 0, 0, tiled=True)
@@ -345,8 +353,8 @@
     states, w_mine, w_theirs = hold((states, w_mine, w_theirs))
 
     (gx,) = call(
-        grad_x_body, "hhhv", [(wide, BF16)], [(square, BF16), ((TOKENS, 128), F32), (wide, F32)], copies=3, out_spaces="v"
-    )(b_rows, cols, local_x, states)
+        grad_x_body, "hhhv", [(wide, BF16)], [(square, BF16), ((HEADS, TOKENS), F32), (wide, BF16)], copies=3, out_spaces="v"
+    )(b_rows, fwd, local_x, states)
     gx_far = ahead_on_x(gx, 2)
     gx_prev, gx_next = ahead_on_x(gx, 1), ahead_on_x(gx, 3)
     states, w_mine, _ = hold((states, w_mine, gx))

time: 112 us -> 112 us (level)
  the two profiles are of different devices: /device:TPU:72 before, /device:TPU:8 now
where the time goes in v4:
time: 112 us; the launch traced here: 111 us
  starting transfers between devices  60.1 us (54%)
  waiting for transfers between devices  31.9 us (28%)
  Pallas kernels  18 us (16%)
    ppermute x6, starting transfers between devices, ahead_on_x(): return lax.ppermute(shard, 'x', [(i, (i + ahead) % 4) for i in range(4)])  22.2 us
    pallas_call x10, Pallas kernels, pinned(): run(*(pltpu.with_memory_space_constraint(a, PLACES[k]) if k in PLACES els...  18 us
    all_to_all x1, waiting for transfers between devices, per_device(): over_y = lax.all_to_all(partial, 'yh', 0, 0, tiled=True)  12.2 us
    all_to_all x1, starting transfers between devices, per_device(): terms = lax.all_to_all(send, CONTEXT, 0, 0, tiled=True)  11.8 us
    ppermute x6, waiting for transfers between devices, ahead_on_x(): return lax.ppermute(shard, 'x', [(i, (i + ahead) % 4) for i in range(4)])  8.69 us
    ppermute x2, starting transfers between devices, per_device(): bc = (lax.ppermute(b_proj, 'yh', flip), lax.ppermute(c_proj, 'yh', flip))  6.75 us
    ppermute x3, starting transfers between devices, other_core(): return lax.ppermute(shard, 'core', [(0, 1), (1, 0)])  6.24 us
    all_to_all x1, starting transfers between devices, per_device(): over_y = lax.all_to_all(partial, 'yh', 0, 0, tiled=True)  5.36 us
  transfers between devices with their start and end apart: 15, of which 8 were waited for; matrix products, arithmetic and copies ran while one was open for 0% of the time, Pallas kernels for 13%

profile of v4, /device:TPU:8, one launch (start us, length us, event | category | flops | bytes accessed | tf_op | source)
XLA Modules:
  0.0 111.0 jit_solution(14330956985568808256)
XLA Ops:
  0.6 4.5 %collective-permute-start = (bf16[128,256]{1,0:T(8,128)(2,1)}, bf16[128,256]{1,0:T(8,128)(2,1)S(1)}, u32[]{:S(2)}, u32[]{:S(2)}) collective-permute-start(bf16[128,256]{1,0:T(8,128)(2,1)} %b_ref.3), channel_id=1, source_target_pairs={{0,1},{1,0},{2,3},{3,2},{4,5},{5,4},{6,7},{7,6},{8,9},{9,8},{10,11... | collective-permute-start | bytes 196616 | tf_op jit(solution)/shard_map/ppermute | solution.py:323
  5.1 2.2 %collective-permute-start.1 = (bf16[128,256]{1,0:T(8,128)(2,1)}, bf16[128,256]{1,0:T(8,128)(2,1)S(1)}, u32[]{:S(2)}, u32[]{:S(2)}) collective-permute-start(bf16[128,256]{1,0:T(8,128)(2,1)} %c_ref.3), channel_id=1, source_target_pairs={{0,1},{1,0},{2,3},{3,2},{4,5},{5,4},{6,7},{7,6},{8,9},{9,8},{10,11... | collective-permute-start | bytes 196616 | tf_op jit(solution)/shard_map/ppermute | solution.py:323
  7.4 0.1 pad_add_fusion.where_ref
  7.5 3.7 %shard_map.94 = (bf16[256,512]{1,0:T(8,128)(2,1)S(1)}, bf16[256,512]{1,0:T(8,128)(2,1)S(1)}, f32[8,256]{1,0:T(8,128)S(1)}, f32[256,128]{1,0:T(8,128)}, f32[1,128...) custom-call(s32[2]{0:T(128)S(1)} %pad_add_fusion.where_ref, ...), custom_call_target="tpu_custom_call" | custom-call | flops 1000000000 | bytes 1048576 | tf_op jit(solution)/shard_map/pallas_call | solution.py:52
  11.1 0.0 copy-start.6
  11.1 0.0 copy-start.5
  11.2 0.0 collective-permute-done.other_b
  11.2 1.3 %collective-permute-done.1.other_c = bf16[128,256]{1,0:T(8,128)(2,1)S(1)} collective-permute-done((bf16[128,256]{1,0:T(8,128)(2,1)}, bf16[128,256]{1,0:T(8,128)(2,1)S(1)}, u32[]{:S(2)}, u32[]{:S(2)}) %collective-permute-start.1) | collective-permute-done | bytes 65568 | tf_op jit(solution)/shard_map/ppermute | solution.py:323
  12.5 1.1 shard_map.95
  13.6 11.8 %all-to-all-start = ((bf16[32,8,1152]{2,1,0:T(8,128)(2,1)}), bf16[32,8,1152]{2,1,0:T(8,128)(2,1)S(1)}, u32[]{:S(2)}, u32[]{:S(2)}) async-start(bf16[32,8,1152]{2,1,0:T(8,128)(2,1)} %bitcast.9), calls=%async_computation | async-start | bytes 1179648 | tf_op jit(solution)/shard_map/all_to_all | solution.py:340
  25.5 3.4 %collective-permute-start.2 = (bf16[256,1024]{1,0:T(8,128)(2,1)}, bf16[256,1024]{1,0:T(8,128)(2,1)S(1)}, u32[]{:S(2)}, u32[]{:S(2)}) collective-permute-start(bf16[256,1024]{1,0:T(8,128)(2,1)} %get-tuple-element.72), channel_id=1, source_target_pairs={{0,4},{4,8},{8,12},{12,0},{1,5},{5,9},{9,13},{13,1},{2,6},{6,10},{... | collective-permute-start | bytes 1572872 | tf_op jit(solution)/shard_map/ppermute | solution.py:317
  28.9 0.0 copy-done.6
  28.9 4.6 %collective-permute-start.3 = (bf16[256,1024]{1,0:T(8,128)(2,1)S(1)}, bf16[256,1024]{1,0:T(8,128)(2,1)S(1)}, u32[]{:S(2)}, u32[]{:S(2)}) collective-permute-start(bf16[256,1024]{1,0:T(8,128)(2,1)S(1)} %copy-done.6), channel_id=1, source_target_pairs={{0,8},{4,12},{8,0},{12,4},{1,9},{5,13},{9,1},{13,5},{2,10},{6,14},... | collective-permute-start | bytes 1572872 | tf_op jit(solution)/shard_map/ppermute | solution.py:317
  33.5 0.0 copy-done.5
  33.5 3.3 %collective-permute-start.4 = (bf16[256,1024]{1,0:T(8,128)(2,1)S(1)}, bf16[256,1024]{1,0:T(8,128)(2,1)S(1)}, u32[]{:S(2)}, u32[]{:S(2)}) collective-permute-start(bf16[256,1024]{1,0:T(8,128)(2,1)S(1)} %copy-done.5), channel_id=1, source_target_pairs={{0,12},{4,0},{8,4},{12,8},{1,13},{5,1},{9,5},{13,9},{2,14},{6,2},{... | collective-permute-start | bytes 1572872 | tf_op jit(solution)/shard_map/ppermute | solution.py:317
  36.9 3.0 %shard_map.96 = (bf16[256,512]{1,0:T(8,128)(2,1)}, bf16[256,256]{1,0:T(8,128)(2,1)}, bf16[256,256]{1,0:T(8,128)(2,1)}) custom-call(bf16[256,512]{1,0:T(8,128)(2,1)} %x_ref.1, bf16[256,512]{1,0:T(8,128)(2,1)} %dy_ref.1, bf16[128,256]{1,0:T(8,128)(2,1)} %b_ref.3, bf16[128,256]{1,0:T(8,128)(2,1)} %c_ref.3, bf16[128,256]{1,0:T(8,128)(2,1)S(1)} %collective-permute-done.other_b, ...), custom_call_target="tpu_custom_call" | custom-call | flops 1000000000 | bytes 1048576 | tf_op jit(solution)/shard_map/pallas_call | solution.py:52
  39.9 4.7 %all-to-all-done = bf16[32,8,1152]{2,1,0:T(8,128)(2,1)S(1)} async-done(((bf16[32,8,1152]{2,1,0:T(8,128)(2,1)}), bf16[32,8,1152]{2,1,0:T(8,128)(2,1)S(1)}, u32[]{:S(2)}, u32[]{:S(2)}) %all-to-all-start) | async-done | bytes 589856 | tf_op jit(solution)/shard_map/all_to_all | solution.py:340
  44.6 1.0 shard_map.97
  45.6 4.1 %all-to-all-start.1 = ((bf16[32,8,1024]{2,1,0:T(8,128)(2,1)}), bf16[32,8,1024]{2,1,0:T(8,128)(2,1)S(1)}, u32[]{:S(2)}, u32[]{:S(2)}) async-start(bf16[32,8,1024]{2,1,0:T(8,128)(2,1)} %bitcast.10), calls=%async_computation.1 | async-start | bytes 1048576 | tf_op jit(solution)/shard_map/all_to_all | solution.py:349
  49.8 0.0 collective-permute-done.2.refs_0_
  49.8 5.2 %collective-permute-done.3.refs_1_ = bf16[256,1024]{1,0:T(8,128)(2,1)S(1)} collective-permute-done((bf16[256,1024]{1,0:T(8,128)(2,1)S(1)}, bf16[256,1024]{1,0:T(8,128)(2,1)S(1)}, u32[]{:S(2)}, u32[]{:S(2)}) %collective-permute-start.3) | collective-permute-done | bytes 524320 | tf_op jit(solution)/shard_map/ppermute | solution.py:317
  55.0 1.4 %collective-permute-done.4.refs_2_ = bf16[256,1024]{1,0:T(8,128)(2,1)S(1)} collective-permute-done((bf16[256,1024]{1,0:T(8,128)(2,1)S(1)}, bf16[256,1024]{1,0:T(8,128)(2,1)S(1)}, u32[]{:S(2)}, u32[]{:S(2)}) %collective-permute-start.4) | collective-permute-done | bytes 524320 | tf_op jit(solution)/shard_map/ppermute | solution.py:317
  56.3 0.0 copy-start
  56.3 0.0 copy-start.1
  56.3 0.0 copy-start.2
  56.3 1.9 %collective-permute-start.5 = (bf16[256,1024]{1,0:T(8,128)(2,1)S(1)}, bf16[256,1024]{1,0:T(8,128)(2,1)S(1)}, u32[]{:S(2)}, u32[]{:S(2)}) collective-permute-start(bf16[256,1024]{1,0:T(8,128)(2,1)S(1)} %get-tuple-element.85.refs_0_), channel_id=1, source_target_pairs={{0,16},{16,0},{1,17},{17,1},{2,18},{18,2},{3,19},{19,3},{4,20},{20... | collective-permute-start | bytes 1572872 | tf_op jit(solution)/shard_map/ppermute | solution.py:320
  58.3 2.4 %collective-permute-start.6 = (bf16[256,1024]{1,0:T(8,128)(2,1)S(1)}, bf16[256,1024]{1,0:T(8,128)(2,1)S(1)}, u32[]{:S(2)}, u32[]{:S(2)}) collective-permute-start(bf16[256,1024]{1,0:T(8,128)(2,1)S(1)} %get-tuple-element.86.refs_1_), channel_id=1, source_target_pairs={{0,16},{16,0},{1,17},{17,1},{2,18},{18,2},{3,19},{19,3},{4,20},{20... | collective-permute-start | bytes 1572872 | tf_op jit(solution)/shard_map/ppermute | solution.py:320
  60.7 1.9 %collective-permute-start.7 = (bf16[256,1024]{1,0:T(8,128)(2,1)S(1)}, bf16[256,1024]{1,0:T(8,128)(2,1)}, u32[]{:S(2)}, u32[]{:S(2)}) collective-permute-start(bf16[256,1024]{1,0:T(8,128)(2,1)S(1)} %get-tuple-element.87.refs_2_), channel_id=1, source_target_pairs={{0,16},{16,0},{1,17},{17,1},{2,18},{18,2},{3,19},{19,3},{4,20},{20... | collective-permute-start | bytes 1572872 | tf_op jit(solution)/shard_map/ppermute | solution.py:320
  62.6 0.0 collective-permute-done.5.refs_3_
  62.6 0.0 copy-start.3
  62.6 0.0 collective-permute-done.6.refs_4_
  62.6 0.0 copy-start.4
  62.7 2.0 %collective-permute-done.7.refs_5_ = bf16[256,1024]{1,0:T(8,128)(2,1)} collective-permute-done((bf16[256,1024]{1,0:T(8,128)(2,1)S(1)}, bf16[256,1024]{1,0:T(8,128)(2,1)}, u32[]{:S(2)}, u32[]{:S(2)}) %collective-permute-start.7) | collective-permute-done | bytes 524320 | tf_op jit(solution)/shard_map/ppermute | solution.py:320
  64.6 3.0 %all-to-all-done.1 = bf16[32,8,1024]{2,1,0:T(8,128)(2,1)S(1)} async-done(((bf16[32,8,1024]{2,1,0:T(8,128)(2,1)}), bf16[32,8,1024]{2,1,0:T(8,128)(2,1)S(1)}, u32[]{:S(2)}, u32[]{:S(2)}) %all-to-all-start.1) | async-done | bytes 524320 | tf_op jit(solution)/shard_map/all_to_all | solution.py:349
  67.6 1.4 %shard_map.99.refs_0_ = bf16[256,512]{1,0:T(8,128)(2,1)S(1)} custom-call(bf16[256,256]{1,0:T(8,128)(2,1)} %get-tuple-element.68.bt_hbm, f32[8,256]{1,0:T(8,128)} %get-tuple-element.69.fwd_hbm, bf16[256,512]{1,0:T(8,128)(2,1)} %get-tuple-element.70.loc_hbm, bf16[256,1024]{1,0:T(8,128)(2,1)S(1)} %bitcast.7), custom_call_target="tpu_custom_call" | custom-call | flops 1000000000 | bytes 1048576 | tf_op jit(solution)/shard_map/pallas_call | solution.py:52
  69.0 4.7 %collective-permute-start.10 = (bf16[256,512]{1,0:T(8,128)(2,1)S(1)}, bf16[256,512]{1,0:T(8,128)(2,1)S(1)}, u32[]{:S(2)}, u32[]{:S(2)}) collective-permute-start(bf16[256,512]{1,0:T(8,128)(2,1)S(1)} %shard_map.99.refs_0_), channel_id=1, source_target_pairs={{0,12},{4,0},{8,4},{12,8},{1,13},{5,1},{9,5},{13,9},{2,14},{6,2},{... | collective-permute-start | bytes 786440 | tf_op jit(solution)/shard_map/ppermute | solution.py:317
  73.7 1.9 %collective-permute-start.8 = (bf16[256,512]{1,0:T(8,128)(2,1)S(1)}, bf16[256,512]{1,0:T(8,128)(2,1)S(1)}, u32[]{:S(2)}, u32[]{:S(2)}) collective-permute-start(bf16[256,512]{1,0:T(8,128)(2,1)S(1)} %shard_map.99.refs_0_), channel_id=1, source_target_pairs={{0,4},{4,8},{8,12},{12,0},{1,5},{5,9},{9,13},{13,1},{2,6},{6,10},{... | collective-permute-start | bytes 786440 | tf_op jit(solution)/shard_map/ppermute | solution.py:317
  75.6 4.2 %collective-permute-start.9 = (bf16[256,512]{1,0:T(8,128)(2,1)S(1)}, bf16[256,512]{1,0:T(8,128)(2,1)S(1)}, u32[]{:S(2)}, u32[]{:S(2)}) collective-permute-start(bf16[256,512]{1,0:T(8,128)(2,1)S(1)} %shard_map.99.refs_0_), channel_id=1, source_target_pairs={{0,8},{4,12},{8,0},{12,4},{1,9},{5,13},{9,1},{13,5},{2,10},{6,14},... | collective-permute-start | bytes 786440 | tf_op jit(solution)/shard_map/ppermute | solution.py:317
  79.8 1.6 %shard_map.103 = (bf16[256,256]{1,0:T(8,128)(2,1)S(1)}, bf16[256,256]{1,0:T(8,128)(2,1)S(1)}) custom-call(bf16[128,256]{1,0:T(8,128)(2,1)} %b_ref.3, bf16[128,256]{1,0:T(8,128)(2,1)} %c_ref.3, bf16[128,256]{1,0:T(8,128)(2,1)S(1)} %collective-permute-done.other_b, bf16[128,256]{1,0:T(8,128)(2,1)S(1)} %collective-permute-done.1.other_c, ...), custom_call_target="tpu_custom_call" | custom-call | flops 1000000000 | bytes 1048576 | tf_op jit(solution)/shard_map/pallas_call | solution.py:52
  81.4 3.7 %collective-permute-start.11 = (bf16[256,256]{1,0:T(8,128)(2,1)S(1)}, bf16[256,256]{1,0:T(8,128)(2,1)S(1)}, u32[]{:S(2)}, u32[]{:S(2)}) collective-permute-start(bf16[256,256]{1,0:T(8,128)(2,1)S(1)} %get-tuple-element.100), channel_id=1, source_target_pairs={{0,1},{1,0},{2,3},{3,2},{4,5},{5,4},{6,7},{7,6},{8,9},{9,8},{10,11... | collective-permute-start | bytes 393224 | tf_op jit(solution)/shard_map/ppermute | solution.py:364
  85.1 0.0 copy-done
  85.1 0.0 copy-done.1
  85.1 0.0 copy-done.2
  85.1 0.0 copy-done.3
  85.1 0.0 copy-done.4
  85.1 2.8 %shard_map.100.w_ref = bf16[2048,1024]{1,0:T(8,128)(2,1)S(1)} custom-call(s32[2]{0:T(128)S(1)} %pad_add_fusion.where_ref, bf16[512,4096]{1,0:T(8,128)(2,1)} %w_hbm.3, bf16[256,1024]{1,0:T(8,128)(2,1)} %copy-done, bf16[256,1024]{1,0:T(8,128)(2,1)} %copy-done.1, bf16[256,1024]{1,0:T(8,128)(2,1)} %copy-done.2, bf16[256,1024]{1,0:T(8,128)(2,1)} %copy-done.3, ...), custom_call_target="tpu_custom_call" | custom-call | flops 1000000000 | bytes 1048576 | tf_op jit(solution)/shard_map/pallas_call | solution.py:52
  87.9 0.0 collective-permute-done.10.refs_3_
  87.9 2.1 %collective-permute-done.8.refs_1_ = bf16[256,512]{1,0:T(8,128)(2,1)S(1)} collective-permute-done((bf16[256,512]{1,0:T(8,128)(2,1)S(1)}, bf16[256,512]{1,0:T(8,128)(2,1)S(1)}, u32[]{:S(2)}, u32[]{:S(2)}) %collective-permute-start.8) | collective-permute-done | bytes 262176 | tf_op jit(solution)/shard_map/ppermute | solution.py:317
  90.0 0.0 collective-permute-done.9.refs_2_
  90.0 2.0 %shard_map.101 = bf16[4,256,256]{2,1,0:T(8,128)(2,1)} custom-call(bf16[2048,1024]{1,0:T(8,128)(2,1)S(1)} %shard_map.100.w_ref, bf16[256,512]{1,0:T(8,128)(2,1)S(1)} %shard_map.99.refs_0_, bf16[256,512]{1,0:T(8,128)(2,1)S(1)} %collective-permute-done.8.refs_1_, bf16[256,512]{1,0:T(8,128)(2,1)S(1)} %collective-permute-done.9.refs_2_, ...), custom_call_target="tpu_custom_call" | custom-call | flops 1000000000 | bytes 1048576 | tf_op jit(solution)/shard_map/pallas_call | solution.py:52
  92.0 5.4 %all-to-all-start.2 = ((bf16[4,256,256]{2,1,0:T(8,128)(2,1)}), bf16[4,256,256]{2,1,0:T(8,128)(2,1)S(1)}, u32[]{:S(2)}, u32[]{:S(2)}) async-start(bf16[4,256,256]{2,1,0:T(8,128)(2,1)} %shard_map.101), calls=%async_computation.2 | async-start | bytes 1048576 | tf_op jit(solution)/shard_map/all_to_all | solution.py:374
  97.4 0.0 collective-permute-done.11.got_ref
  97.4 0.7 shard_map.104
  98.0 12.2 %all-to-all-done.2.got_ref = bf16[4,256,256]{2,1,0:T(8,128)(2,1)S(1)} async-done(((bf16[4,256,256]{2,1,0:T(8,128)(2,1)}), bf16[4,256,256]{2,1,0:T(8,128)(2,1)S(1)}, u32[]{:S(2)}, u32[]{:S(2)}) %all-to-all-start.2) | async-done | bytes 524320 | tf_op jit(solution)/shard_map/all_to_all | solution.py:374
  110.3 0.8 shard_map.102
  (1 shorter events, 0.0 us)
Async XLA Ops:
  0.6 10.5 %collective-permute-start = (bf16[128,256]{1,0:T(8,128)(2,1)}, bf16[128,256]{1,0:T(8,128)(2,1)S(1)}, u32[]{:S(2)}, u32[]{:S(2)}) collective-permute-start(bf16[128,256]{1,0:T(8,128)(2,1)} %b_ref.3), channel_id=1, source_target_pairs={{0,1},{1,0},{2,3},{3,2},{4,5},{5,4},{6,7},{7,6},{8,9},{9,8},{10,11... | collective-permute-start | bytes 196616 | tf_op jit(solution)/shard_map/ppermute | solution.py:323
  5.1 7.4 %collective-permute-start.1 = (bf16[128,256]{1,0:T(8,128)(2,1)}, bf16[128,256]{1,0:T(8,128)(2,1)S(1)}, u32[]{:S(2)}, u32[]{:S(2)}) collective-permute-start(bf16[128,256]{1,0:T(8,128)(2,1)} %c_ref.3), channel_id=1, source_target_pairs={{0,1},{1,0},{2,3},{3,2},{4,5},{5,4},{6,7},{7,6},{8,9},{9,8},{10,11... | collective-permute-start | bytes 196616 | tf_op jit(solution)/shard_map/ppermute | solution.py:323
  11.1 17.7 %copy-start.6 = (bf16[256,1024]{1,0:T(8,128)(2,1)S(1)}, bf16[256,1024]{1,0:T(8,128)(2,1)}, u32[]{:S(2)}) copy-start(bf16[256,1024]{1,0:T(8,128)(2,1)} %get-tuple-element.73) | copy-start | bytes 1572868
  11.1 22.4 %copy-start.5 = (bf16[256,1024]{1,0:T(8,128)(2,1)S(1)}, bf16[256,1024]{1,0:T(8,128)(2,1)}, u32[]{:S(2)}) copy-start(bf16[256,1024]{1,0:T(8,128)(2,1)} %get-tuple-element.74) | copy-start | bytes 1572868
  13.6 31.0 %all-to-all-start = ((bf16[32,8,1152]{2,1,0:T(8,128)(2,1)}), bf16[32,8,1152]{2,1,0:T(8,128)(2,1)S(1)}, u32[]{:S(2)}, u32[]{:S(2)}) async-start(bf16[32,8,1152]{2,1,0:T(8,128)(2,1)} %bitcast.9), calls=%async_computation | async-start | bytes 1179648 | tf_op jit(solution)/shard_map/all_to_all | solution.py:340
  25.5 24.3 %collective-permute-start.2 = (bf16[256,1024]{1,0:T(8,128)(2,1)}, bf16[256,1024]{1,0:T(8,128)(2,1)S(1)}, u32[]{:S(2)}, u32[]{:S(2)}) collective-permute-start(bf16[256,1024]{1,0:T(8,128)(2,1)} %get-tuple-element.72), channel_id=1, source_target_pairs={{0,4},{4,8},{8,12},{12,0},{1,5},{5,9},{9,13},{13,1},{2,6},{6,10},{... | collective-permute-start | bytes 1572872 | tf_op jit(solution)/shard_map/ppermute | solution.py:317
  28.9 26.1 %collective-permute-start.3 = (bf16[256,1024]{1,0:T(8,128)(2,1)S(1)}, bf16[256,1024]{1,0:T(8,128)(2,1)S(1)}, u32[]{:S(2)}, u32[]{:S(2)}) collective-permute-start(bf16[256,1024]{1,0:T(8,128)(2,1)S(1)} %copy-done.6), channel_id=1, source_target_pairs={{0,8},{4,12},{8,0},{12,4},{1,9},{5,13},{9,1},{13,5},{2,10},{6,14},... | collective-permute-start | bytes 1572872 | tf_op jit(solution)/shard_map/ppermute | solution.py:317
  33.5 22.8 %collective-permute-start.4 = (bf16[256,1024]{1,0:T(8,128)(2,1)S(1)}, bf16[256,1024]{1,0:T(8,128)(2,1)S(1)}, u32[]{:S(2)}, u32[]{:S(2)}) collective-permute-start(bf16[256,1024]{1,0:T(8,128)(2,1)S(1)} %copy-done.5), channel_id=1, source_target_pairs={{0,12},{4,0},{8,4},{12,8},{1,13},{5,1},{9,5},{13,9},{2,14},{6,2},{... | collective-permute-start | bytes 1572872 | tf_op jit(solution)/shard_map/ppermute | solution.py:317
  45.6 21.9 %all-to-all-start.1 = ((bf16[32,8,1024]{2,1,0:T(8,128)(2,1)}), bf16[32,8,1024]{2,1,0:T(8,128)(2,1)S(1)}, u32[]{:S(2)}, u32[]{:S(2)}) async-start(bf16[32,8,1024]{2,1,0:T(8,128)(2,1)} %bitcast.10), calls=%async_computation.1 | async-start | bytes 1048576 | tf_op jit(solution)/shard_map/all_to_all | solution.py:349
  56.3 28.7 %copy-start = (bf16[256,1024]{1,0:T(8,128)(2,1)}, bf16[256,1024]{1,0:T(8,128)(2,1)S(1)}, u32[]{:S(2)}) copy-start(bf16[256,1024]{1,0:T(8,128)(2,1)S(1)} %get-tuple-element.85.refs_0_) | copy-start | bytes 1572868
  56.3 28.7 %copy-start.1 = (bf16[256,1024]{1,0:T(8,128)(2,1)}, bf16[256,1024]{1,0:T(8,128)(2,1)S(1)}, u32[]{:S(2)}) copy-start(bf16[256,1024]{1,0:T(8,128)(2,1)S(1)} %get-tuple-element.86.refs_1_) | copy-start | bytes 1572868
  56.3 28.7 %copy-start.2 = (bf16[256,1024]{1,0:T(8,128)(2,1)}, bf16[256,1024]{1,0:T(8,128)(2,1)S(1)}, u32[]{:S(2)}) copy-start(bf16[256,1024]{1,0:T(8,128)(2,1)S(1)} %get-tuple-element.87.refs_2_) | copy-start | bytes 1572868
  56.3 6.3 %collective-permute-start.5 = (bf16[256,1024]{1,0:T(8,128)(2,1)S(1)}, bf16[256,1024]{1,0:T(8,128)(2,1)S(1)}, u32[]{:S(2)}, u32[]{:S(2)}) collective-permute-start(bf16[256,1024]{1,0:T(8,128)(2,1)S(1)} %get-tuple-element.85.refs_0_), channel_id=1, source_target_pairs={{0,16},{16,0},{1,17},{17,1},{2,18},{18,2},{3,19},{19,3},{4,20},{20... | collective-permute-start | bytes 1572872 | tf_op jit(solution)/shard_map/ppermute | solution.py:320
  58.3 4.4 %collective-permute-start.6 = (bf16[256,1024]{1,0:T(8,128)(2,1)S(1)}, bf16[256,1024]{1,0:T(8,128)(2,1)S(1)}, u32[]{:S(2)}, u32[]{:S(2)}) collective-permute-start(bf16[256,1024]{1,0:T(8,128)(2,1)S(1)} %get-tuple-element.86.refs_1_), channel_id=1, source_target_pairs={{0,16},{16,0},{1,17},{17,1},{2,18},{18,2},{3,19},{19,3},{4,20},{20... | collective-permute-start | bytes 1572872 | tf_op jit(solution)/shard_map/ppermute | solution.py:320
  60.7 3.9 %collective-permute-start.7 = (bf16[256,1024]{1,0:T(8,128)(2,1)S(1)}, bf16[256,1024]{1,0:T(8,128)(2,1)}, u32[]{:S(2)}, u32[]{:S(2)}) collective-permute-start(bf16[256,1024]{1,0:T(8,128)(2,1)S(1)} %get-tuple-element.87.refs_2_), channel_id=1, source_target_pairs={{0,16},{16,0},{1,17},{17,1},{2,18},{18,2},{3,19},{19,3},{4,20},{20... | collective-permute-start | bytes 1572872 | tf_op jit(solution)/shard_map/ppermute | solution.py:320
  62.6 22.5 %copy-start.3 = (bf16[256,1024]{1,0:T(8,128)(2,1)}, bf16[256,1024]{1,0:T(8,128)(2,1)S(1)}, u32[]{:S(2)}) copy-start(bf16[256,1024]{1,0:T(8,128)(2,1)S(1)} %collective-permute-done.5.refs_3_) | copy-start | bytes 1572868
  62.6 22.5 %copy-start.4 = (bf16[256,1024]{1,0:T(8,128)(2,1)}, bf16[256,1024]{1,0:T(8,128)(2,1)S(1)}, u32[]{:S(2)}) copy-start(bf16[256,1024]{1,0:T(8,128)(2,1)S(1)} %collective-permute-done.6.refs_4_) | copy-start | bytes 1572868
  69.0 18.9 %collective-permute-start.10 = (bf16[256,512]{1,0:T(8,128)(2,1)S(1)}, bf16[256,512]{1,0:T(8,128)(2,1)S(1)}, u32[]{:S(2)}, u32[]{:S(2)}) collective-permute-start(bf16[256,512]{1,0:T(8,128)(2,1)S(1)} %shard_map.99.refs_0_), channel_id=1, source_target_pairs={{0,12},{4,0},{8,4},{12,8},{1,13},{5,1},{9,5},{13,9},{2,14},{6,2},{... | collective-permute-start | bytes 786440 | tf_op jit(solution)/shard_map/ppermute | solution.py:317
  73.7 16.3 %collective-permute-start.8 = (bf16[256,512]{1,0:T(8,128)(2,1)S(1)}, bf16[256,512]{1,0:T(8,128)(2,1)S(1)}, u32[]{:S(2)}, u32[]{:S(2)}) collective-permute-start(bf16[256,512]{1,0:T(8,128)(2,1)S(1)} %shard_map.99.refs_0_), channel_id=1, source_target_pairs={{0,4},{4,8},{8,12},{12,0},{1,5},{5,9},{9,13},{13,1},{2,6},{6,10},{... | collective-permute-start | bytes 786440 | tf_op jit(solution)/shard_map/ppermute | solution.py:317
  75.6 14.4 %collective-permute-start.9 = (bf16[256,512]{1,0:T(8,128)(2,1)S(1)}, bf16[256,512]{1,0:T(8,128)(2,1)S(1)}, u32[]{:S(2)}, u32[]{:S(2)}) collective-permute-start(bf16[256,512]{1,0:T(8,128)(2,1)S(1)} %shard_map.99.refs_0_), channel_id=1, source_target_pairs={{0,8},{4,12},{8,0},{12,4},{1,9},{5,13},{9,1},{13,5},{2,10},{6,14},... | collective-permute-start | bytes 786440 | tf_op jit(solution)/shard_map/ppermute | solution.py:317
  81.4 16.0 %collective-permute-start.11 = (bf16[256,256]{1,0:T(8,128)(2,1)S(1)}, bf16[256,256]{1,0:T(8,128)(2,1)S(1)}, u32[]{:S(2)}, u32[]{:S(2)}) collective-permute-start(bf16[256,256]{1,0:T(8,128)(2,1)S(1)} %get-tuple-element.100), channel_id=1, source_target_pairs={{0,1},{1,0},{2,3},{3,2},{4,5},{5,4},{6,7},{7,6},{8,9},{9,8},{10,11... | collective-permute-start | bytes 393224 | tf_op jit(solution)/shard_map/ppermute | solution.py:364
  92.0 18.2 %all-to-all-start.2 = ((bf16[4,256,256]{2,1,0:T(8,128)(2,1)}), bf16[4,256,256]{2,1,0:T(8,128)(2,1)S(1)}, u32[]{:S(2)}, u32[]{:S(2)}) async-start(bf16[4,256,256]{2,1,0:T(8,128)(2,1)} %shard_map.101), calls=%async_computation.2 | async-start | bytes 1048576 | tf_op jit(solution)/shard_map/all_to_all | solution.py:374

commit v5 on v4

--- a/solution.py
+++ b/solution.py
@@ -6,6 +6,7 @@
 from jax.sharding import Mesh, PartitionSpec as P
 
 CONTEXT = ("z", "yl", "core")
+EXCHANGE = ("yl", "z", "core")
 TENSOR = ("x", "yh")
 F32 = jnp.float32
 BF16 = jnp.bfloat16
@@ -179,9 +180,14 @@
     copies = [pltpu.make_async_copy(out_ref.at[:, at], out_hbm.at[:, at], sems.at[i]) for i, at in enumerate(halves)]
     decay_ref[...] = expanded(got_ref[:, 2 * COLS :])
     two = 2 * LINES
+
+    def place(chip):
+        row = chip % 2 * (BLOCKS // 4) + chip // 2
+        return slice(row * two, (row + 1) * two)
+
     state = jnp.zeros((LINES, COLS), F32)
     for c in range(BLOCKS // 2):
-        at = slice(c * two, (c + 1) * two)
+        at = place(c)
         term, decay = got_ref[at, :COLS].astype(F32), decay_ref[at, :]
         after = state * decay[:LINES] + term[:LINES]
         out_ref[at, :COLS] = jnp.concatenate([state, after], axis=0).astype(BF16)
@@ -189,7 +195,7 @@
     copies[0].start()
     state = jnp.zeros((LINES, COLS), F32)
     for c in range(BLOCKS // 2 - 1, -1, -1):
-        at = slice(c * two, (c + 1) * two)
+        at = place(c)
         term, decay = got_ref[at, COLS : 2 * COLS].astype(F32), decay_ref[at, :]
         before = state * decay[LINES:] + term[LINES:]
         out_ref[at, COLS:] = jnp.concatenate([before, state], axis=0).astype(BF16)
@@ -337,7 +343,7 @@
     ends = ((STATE, 2 * COLS + 128), BF16)
     (send,) = call(ends_body, "vvvvvvv", [ends], [ends], copies=2, out_spaces="h")(b_own, c_own, *bc, wx, wdy, ext)
 
-    terms = lax.all_to_all(send, CONTEXT, 0, 0, tiled=True)
+    terms = lax.all_to_all(send, EXCHANGE, 0, 0, tiled=True)
     w_next, w_prev, w_far, bc, _ = hold((w_next, w_prev, w_far, bc, send))
     w_prev, w_next, w_far = ahead_on_x(w_next, 1), ahead_on_x(w_prev, 3), ahead_on_x(w_far, 2)
     local_x, b_rows, mixed = call(
@@ -346,7 +352,7 @@
     terms, local_x, b_rows, mixed = hold((terms, local_x, b_rows, mixed))
     both = ((STATE, 2 * COLS), BF16)
     (scanned,) = call(scan_body, "v", [both], [both, ((STATE, COLS), F32)], copies=2, out_spaces="h")(terms)
-    states = lax.all_to_all(scanned, CONTEXT, 0, 0, tiled=True)
+    states = lax.all_to_all(scanned, EXCHANGE, 0, 0, tiled=True)
     w_prev, w_far, w_next, _ = hold((w_prev, w_far, w_next, scanned))
     w_mine = passed(w_prev, w_far, w_next)
     w_theirs = [other_core(w) for w in w_mine]

time: 112 us -> 111 us (level)
  the two profiles are of different devices: /device:TPU:8 before, /device:TPU:72 now
where the time goes in v5:
time: 111 us; the launch traced here: 110 us
  starting transfers between devices  59.8 us (54%)
  waiting for transfers between devices  31 us (28%)
  Pallas kernels  18 us (16%)
    ppermute x6, starting transfers between devices, ahead_on_x(): return lax.ppermute(shard, 'x', [(i, (i + ahead) % 4) for i in range(4)])  22 us
    pallas_call x10, Pallas kernels, pinned(): run(*(pltpu.with_memory_space_constraint(a, PLACES[k]) if k in PLACES els...  18 us
    all_to_all x1, waiting for transfers between devices, per_device(): over_y = lax.all_to_all(partial, 'yh', 0, 0, tiled=True)  13.5 us
    all_to_all x1, starting transfers between devices, per_device(): terms = lax.all_to_all(send, EXCHANGE, 0, 0, tiled=True)  11 us
    ppermute x6, waiting for transfers between devices, ahead_on_x(): return lax.ppermute(shard, 'x', [(i, (i + ahead) % 4) for i in range(4)])  9.51 us
    ppermute x2, starting transfers between devices, per_device(): bc = (lax.ppermute(b_proj, 'yh', flip), lax.ppermute(c_proj, 'yh', flip))  6.75 us
    ppermute x3, starting transfers between devices, other_core(): return lax.ppermute(shard, 'core', [(0, 1), (1, 0)])  6.24 us
    all_to_all x1, starting transfers between devices, per_device(): over_y = lax.all_to_all(partial, 'yh', 0, 0, tiled=True)  5.37 us
  transfers between devices with their start and end apart: 15, of which 8 were waited for; matrix products, arithmetic and copies ran while one was open for 0% of the time, Pallas kernels for 13%

profile of v5, /device:TPU:72, one launch (start us, length us, event | category | flops | bytes accessed | tf_op | source)
XLA Modules:
  0.0 109.9 jit_solution(11630389998769039589)
XLA Ops:
  0.6 4.5 %collective-permute-start = (bf16[128,256]{1,0:T(8,128)(2,1)}, bf16[128,256]{1,0:T(8,128)(2,1)S(1)}, u32[]{:S(2)}, u32[]{:S(2)}) collective-permute-start(bf16[128,256]{1,0:T(8,128)(2,1)} %b_ref.3), channel_id=1, source_target_pairs={{0,1},{1,0},{2,3},{3,2},{4,5},{5,4},{6,7},{7,6},{8,9},{9,8},{10,11... | collective-permute-start | bytes 196616 | tf_op jit(solution)/shard_map/ppermute | solution.py:329
  5.1 2.2 %collective-permute-start.1 = (bf16[128,256]{1,0:T(8,128)(2,1)}, bf16[128,256]{1,0:T(8,128)(2,1)S(1)}, u32[]{:S(2)}, u32[]{:S(2)}) collective-permute-start(bf16[128,256]{1,0:T(8,128)(2,1)} %c_ref.3), channel_id=1, source_target_pairs={{0,1},{1,0},{2,3},{3,2},{4,5},{5,4},{6,7},{7,6},{8,9},{9,8},{10,11... | collective-permute-start | bytes 196616 | tf_op jit(solution)/shard_map/ppermute | solution.py:329
  7.4 0.1 pad_add_fusion.where_ref
  7.5 3.7 %shard_map.94 = (bf16[256,512]{1,0:T(8,128)(2,1)S(1)}, bf16[256,512]{1,0:T(8,128)(2,1)S(1)}, f32[8,256]{1,0:T(8,128)S(1)}, f32[256,128]{1,0:T(8,128)}, f32[1,128...) custom-call(s32[2]{0:T(128)S(1)} %pad_add_fusion.where_ref, ...), custom_call_target="tpu_custom_call" | custom-call | flops 1000000000 | bytes 1048576 | tf_op jit(solution)/shard_map/pallas_call | solution.py:53
  11.1 0.0 copy-start.6
  11.1 0.0 copy-start.5
  11.2 0.0 collective-permute-done.other_b
  11.2 1.2 %collective-permute-done.1.other_c = bf16[128,256]{1,0:T(8,128)(2,1)S(1)} collective-permute-done((bf16[128,256]{1,0:T(8,128)(2,1)}, bf16[128,256]{1,0:T(8,128)(2,1)S(1)}, u32[]{:S(2)}, u32[]{:S(2)}) %collective-permute-start.1) | collective-permute-done | bytes 65568 | tf_op jit(solution)/shard_map/ppermute | solution.py:329
  12.4 1.1 %shard_map.95 = bf16[256,1152]{1,0:T(8,128)(2,1)} custom-call(bf16[128,256]{1,0:T(8,128)(2,1)S(1)} %get-tuple-element.53.b_ref, bf16[128,256]{1,0:T(8,128)(2,1)S(1)} %get-tuple-element.54.c_ref, bf16[128,256]{1,0:T(8,128)(2,1)S(1)} %collective-permute-done.other_b, bf16[128,256]{1,0:T(8,128)(2,1)S(1)} %collective-permute-done.1.other_c, ...), custom_call_target="tpu_custom_call" | custom-call | flops 1000000000 | bytes 1048576 | tf_op jit(solution)/shard_map/pallas_call | solution.py:53
  13.5 11.0 %all-to-all-start = ((bf16[32,8,1152]{2,1,0:T(8,128)(2,1)}), bf16[32,8,1152]{2,1,0:T(8,128)(2,1)S(1)}, u32[]{:S(2)}, u32[]{:S(2)}) async-start(bf16[32,8,1152]{2,1,0:T(8,128)(2,1)} %bitcast.9), calls=%async_computation | async-start | bytes 1179648 | tf_op jit(solution)/shard_map/all_to_all | solution.py:346
  24.6 3.4 %collective-permute-start.2 = (bf16[256,1024]{1,0:T(8,128)(2,1)}, bf16[256,1024]{1,0:T(8,128)(2,1)S(1)}, u32[]{:S(2)}, u32[]{:S(2)}) collective-permute-start(bf16[256,1024]{1,0:T(8,128)(2,1)} %get-tuple-element.72), channel_id=1, source_target_pairs={{0,4},{4,8},{8,12},{12,0},{1,5},{5,9},{9,13},{13,1},{2,6},{6,10},{... | collective-permute-start | bytes 1572872 | tf_op jit(solution)/shard_map/ppermute | solution.py:323
  28.0 0.0 copy-done.6
  28.0 4.6 %collective-permute-start.3 = (bf16[256,1024]{1,0:T(8,128)(2,1)S(1)}, bf16[256,1024]{1,0:T(8,128)(2,1)S(1)}, u32[]{:S(2)}, u32[]{:S(2)}) collective-permute-start(bf16[256,1024]{1,0:T(8,128)(2,1)S(1)} %copy-done.6), channel_id=1, source_target_pairs={{0,8},{4,12},{8,0},{12,4},{1,9},{5,13},{9,1},{13,5},{2,10},{6,14},... | collective-permute-start | bytes 1572872 | tf_op jit(solution)/shard_map/ppermute | solution.py:323
  32.6 0.0 copy-done.5
  32.6 3.3 %collective-permute-start.4 = (bf16[256,1024]{1,0:T(8,128)(2,1)S(1)}, bf16[256,1024]{1,0:T(8,128)(2,1)S(1)}, u32[]{:S(2)}, u32[]{:S(2)}) collective-permute-start(bf16[256,1024]{1,0:T(8,128)(2,1)S(1)} %copy-done.5), channel_id=1, source_target_pairs={{0,12},{4,0},{8,4},{12,8},{1,13},{5,1},{9,5},{13,9},{2,14},{6,2},{... | collective-permute-start | bytes 1572872 | tf_op jit(solution)/shard_map/ppermute | solution.py:323
  36.0 3.0 %shard_map.96 = (bf16[256,512]{1,0:T(8,128)(2,1)}, bf16[256,256]{1,0:T(8,128)(2,1)}, bf16[256,256]{1,0:T(8,128)(2,1)}) custom-call(bf16[256,512]{1,0:T(8,128)(2,1)} %x_ref.1, bf16[256,512]{1,0:T(8,128)(2,1)} %dy_ref.1, bf16[128,256]{1,0:T(8,128)(2,1)} %b_ref.3, bf16[128,256]{1,0:T(8,128)(2,1)} %c_ref.3, bf16[128,256]{1,0:T(8,128)(2,1)S(1)} %collective-permute-done.other_b, ...), custom_call_target="tpu_custom_call" | custom-call | flops 1000000000 | bytes 1048576 | tf_op jit(solution)/shard_map/pallas_call | solution.py:53
  39.0 3.6 %all-to-all-done = bf16[32,8,1152]{2,1,0:T(8,128)(2,1)S(1)} async-done(((bf16[32,8,1152]{2,1,0:T(8,128)(2,1)}), bf16[32,8,1152]{2,1,0:T(8,128)(2,1)S(1)}, u32[]{:S(2)}, u32[]{:S(2)}) %all-to-all-start) | async-done | bytes 589856 | tf_op jit(solution)/shard_map/all_to_all | solution.py:346
  42.5 1.1 shard_map.97
  43.6 4.8 %all-to-all-start.1 = ((bf16[32,8,1024]{2,1,0:T(8,128)(2,1)}), bf16[32,8,1024]{2,1,0:T(8,128)(2,1)S(1)}, u32[]{:S(2)}, u32[]{:S(2)}) async-start(bf16[32,8,1024]{2,1,0:T(8,128)(2,1)} %bitcast.10), calls=%async_computation.1 | async-start | bytes 1048576 | tf_op jit(solution)/shard_map/all_to_all | solution.py:355
  48.4 0.0 collective-permute-done.2.refs_0_
  48.4 5.7 %collective-permute-done.3.refs_1_ = bf16[256,1024]{1,0:T(8,128)(2,1)S(1)} collective-permute-done((bf16[256,1024]{1,0:T(8,128)(2,1)S(1)}, bf16[256,1024]{1,0:T(8,128)(2,1)S(1)}, u32[]{:S(2)}, u32[]{:S(2)}) %collective-permute-start.3) | collective-permute-done | bytes 524320 | tf_op jit(solution)/shard_map/ppermute | solution.py:323
  54.1 1.4 %collective-permute-done.4.refs_2_ = bf16[256,1024]{1,0:T(8,128)(2,1)S(1)} collective-permute-done((bf16[256,1024]{1,0:T(8,128)(2,1)S(1)}, bf16[256,1024]{1,0:T(8,128)(2,1)S(1)}, u32[]{:S(2)}, u32[]{:S(2)}) %collective-permute-start.4) | collective-permute-done | bytes 524320 | tf_op jit(solution)/shard_map/ppermute | solution.py:323
  55.4 0.0 copy-start
  55.4 0.0 copy-start.1
  55.4 0.0 copy-start.2
  55.4 1.9 %collective-permute-start.5 = (bf16[256,1024]{1,0:T(8,128)(2,1)S(1)}, bf16[256,1024]{1,0:T(8,128)(2,1)S(1)}, u32[]{:S(2)}, u32[]{:S(2)}) collective-permute-start(bf16[256,1024]{1,0:T(8,128)(2,1)S(1)} %get-tuple-element.85.refs_0_), channel_id=1, source_target_pairs={{0,16},{16,0},{1,17},{17,1},{2,18},{18,2},{3,19},{19,3},{4,20},{20... | collective-permute-start | bytes 1572872 | tf_op jit(solution)/shard_map/ppermute | solution.py:326
  57.4 2.4 %collective-permute-start.6 = (bf16[256,1024]{1,0:T(8,128)(2,1)S(1)}, bf16[256,1024]{1,0:T(8,128)(2,1)S(1)}, u32[]{:S(2)}, u32[]{:S(2)}) collective-permute-start(bf16[256,1024]{1,0:T(8,128)(2,1)S(1)} %get-tuple-element.86.refs_1_), channel_id=1, source_target_pairs={{0,16},{16,0},{1,17},{17,1},{2,18},{18,2},{3,19},{19,3},{4,20},{20... | collective-permute-start | bytes 1572872 | tf_op jit(solution)/shard_map/ppermute | solution.py:326
  59.8 1.9 %collective-permute-start.7 = (bf16[256,1024]{1,0:T(8,128)(2,1)S(1)}, bf16[256,1024]{1,0:T(8,128)(2,1)}, u32[]{:S(2)}, u32[]{:S(2)}) collective-permute-start(bf16[256,1024]{1,0:T(8,128)(2,1)S(1)} %get-tuple-element.87.refs_2_), channel_id=1, source_target_pairs={{0,16},{16,0},{1,17},{17,1},{2,18},{18,2},{3,19},{19,3},{4,20},{20... | collective-permute-start | bytes 1572872 | tf_op jit(solution)/shard_map/ppermute | solution.py:326
  61.7 0.0 collective-permute-done.5.refs_3_
  61.7 0.0 copy-start.3
  61.7 0.0 collective-permute-done.6.refs_4_
  61.7 0.0 copy-start.4
  61.8 2.0 %collective-permute-done.7.refs_5_ = bf16[256,1024]{1,0:T(8,128)(2,1)} collective-permute-done((bf16[256,1024]{1,0:T(8,128)(2,1)S(1)}, bf16[256,1024]{1,0:T(8,128)(2,1)}, u32[]{:S(2)}, u32[]{:S(2)}) %collective-permute-start.7) | collective-permute-done | bytes 524320 | tf_op jit(solution)/shard_map/ppermute | solution.py:326
  63.7 1.3 %all-to-all-done.1 = bf16[32,8,1024]{2,1,0:T(8,128)(2,1)S(1)} async-done(((bf16[32,8,1024]{2,1,0:T(8,128)(2,1)}), bf16[32,8,1024]{2,1,0:T(8,128)(2,1)S(1)}, u32[]{:S(2)}, u32[]{:S(2)}) %all-to-all-start.1) | async-done | bytes 524320 | tf_op jit(solution)/shard_map/all_to_all | solution.py:355
  65.0 1.4 %shard_map.99.refs_0_ = bf16[256,512]{1,0:T(8,128)(2,1)S(1)} custom-call(bf16[256,256]{1,0:T(8,128)(2,1)} %get-tuple-element.68.bt_hbm, f32[8,256]{1,0:T(8,128)} %get-tuple-element.69.fwd_hbm, bf16[256,512]{1,0:T(8,128)(2,1)} %get-tuple-element.70.loc_hbm, bf16[256,1024]{1,0:T(8,128)(2,1)S(1)} %bitcast.7), custom_call_target="tpu_custom_call" | custom-call | flops 1000000000 | bytes 1048576 | tf_op jit(solution)/shard_map/pallas_call | solution.py:53
  66.5 4.5 %collective-permute-start.10 = (bf16[256,512]{1,0:T(8,128)(2,1)S(1)}, bf16[256,512]{1,0:T(8,128)(2,1)S(1)}, u32[]{:S(2)}, u32[]{:S(2)}) collective-permute-start(bf16[256,512]{1,0:T(8,128)(2,1)S(1)} %shard_map.99.refs_0_), channel_id=1, source_target_pairs={{0,12},{4,0},{8,4},{12,8},{1,13},{5,1},{9,5},{13,9},{2,14},{6,2},{... | collective-permute-start | bytes 786440 | tf_op jit(solution)/shard_map/ppermute | solution.py:323
  71.0 1.9 %collective-permute-start.8 = (bf16[256,512]{1,0:T(8,128)(2,1)S(1)}, bf16[256,512]{1,0:T(8,128)(2,1)S(1)}, u32[]{:S(2)}, u32[]{:S(2)}) collective-permute-start(bf16[256,512]{1,0:T(8,128)(2,1)S(1)} %shard_map.99.refs_0_), channel_id=1, source_target_pairs={{0,4},{4,8},{8,12},{12,0},{1,5},{5,9},{9,13},{13,1},{2,6},{6,10},{... | collective-permute-start | bytes 786440 | tf_op jit(solution)/shard_map/ppermute | solution.py:323
  72.9 4.2 %collective-permute-start.9 = (bf16[256,512]{1,0:T(8,128)(2,1)S(1)}, bf16[256,512]{1,0:T(8,128)(2,1)S(1)}, u32[]{:S(2)}, u32[]{:S(2)}) collective-permute-start(bf16[256,512]{1,0:T(8,128)(2,1)S(1)} %shard_map.99.refs_0_), channel_id=1, source_target_pairs={{0,8},{4,12},{8,0},{12,4},{1,9},{5,13},{9,1},{13,5},{2,10},{6,14},... | collective-permute-start | bytes 786440 | tf_op jit(solution)/shard_map/ppermute | solution.py:323
  77.1 1.6 %shard_map.103 = (bf16[256,256]{1,0:T(8,128)(2,1)S(1)}, bf16[256,256]{1,0:T(8,128)(2,1)S(1)}) custom-call(bf16[128,256]{1,0:T(8,128)(2,1)} %b_ref.3, bf16[128,256]{1,0:T(8,128)(2,1)} %c_ref.3, bf16[128,256]{1,0:T(8,128)(2,1)S(1)} %collective-permute-done.other_b, bf16[128,256]{1,0:T(8,128)(2,1)S(1)} %collective-permute-done.1.other_c, ...), custom_call_target="tpu_custom_call" | custom-call | flops 1000000000 | bytes 1048576 | tf_op jit(solution)/shard_map/pallas_call | solution.py:53
  78.7 3.7 %collective-permute-start.11 = (bf16[256,256]{1,0:T(8,128)(2,1)S(1)}, bf16[256,256]{1,0:T(8,128)(2,1)S(1)}, u32[]{:S(2)}, u32[]{:S(2)}) collective-permute-start(bf16[256,256]{1,0:T(8,128)(2,1)S(1)} %get-tuple-element.100), channel_id=1, source_target_pairs={{0,1},{1,0},{2,3},{3,2},{4,5},{5,4},{6,7},{7,6},{8,9},{9,8},{10,11... | collective-permute-start | bytes 393224 | tf_op jit(solution)/shard_map/ppermute | solution.py:370
  82.4 0.0 copy-done
  82.4 0.0 copy-done.1
  82.4 0.0 copy-done.2
  82.4 0.0 copy-done.3
  82.4 0.0 copy-done.4
  82.4 2.8 %shard_map.100.w_ref = bf16[2048,1024]{1,0:T(8,128)(2,1)S(1)} custom-call(s32[2]{0:T(128)S(1)} %pad_add_fusion.where_ref, bf16[512,4096]{1,0:T(8,128)(2,1)} %w_hbm.3, bf16[256,1024]{1,0:T(8,128)(2,1)} %copy-done, bf16[256,1024]{1,0:T(8,128)(2,1)} %copy-done.1, bf16[256,1024]{1,0:T(8,128)(2,1)} %copy-done.2, bf16[256,1024]{1,0:T(8,128)(2,1)} %copy-done.3, ...), custom_call_target="tpu_custom_call" | custom-call | flops 1000000000 | bytes 1048576 | tf_op jit(solution)/shard_map/pallas_call | solution.py:53
  85.2 0.0 collective-permute-done.10.refs_3_
  85.2 2.5 %collective-permute-done.8.refs_1_ = bf16[256,512]{1,0:T(8,128)(2,1)S(1)} collective-permute-done((bf16[256,512]{1,0:T(8,128)(2,1)S(1)}, bf16[256,512]{1,0:T(8,128)(2,1)S(1)}, u32[]{:S(2)}, u32[]{:S(2)}) %collective-permute-start.8) | collective-permute-done | bytes 262176 | tf_op jit(solution)/shard_map/ppermute | solution.py:323
  87.7 0.0 collective-permute-done.9.refs_2_
  87.7 2.0 %shard_map.101 = bf16[4,256,256]{2,1,0:T(8,128)(2,1)} custom-call(bf16[2048,1024]{1,0:T(8,128)(2,1)S(1)} %shard_map.100.w_ref, bf16[256,512]{1,0:T(8,128)(2,1)S(1)} %shard_map.99.refs_0_, bf16[256,512]{1,0:T(8,128)(2,1)S(1)} %collective-permute-done.8.refs_1_, bf16[256,512]{1,0:T(8,128)(2,1)S(1)} %collective-permute-done.9.refs_2_, ...), custom_call_target="tpu_custom_call" | custom-call | flops 1000000000 | bytes 1048576 | tf_op jit(solution)/shard_map/pallas_call | solution.py:53
  89.7 5.4 %all-to-all-start.2 = ((bf16[4,256,256]{2,1,0:T(8,128)(2,1)}), bf16[4,256,256]{2,1,0:T(8,128)(2,1)S(1)}, u32[]{:S(2)}, u32[]{:S(2)}) async-start(bf16[4,256,256]{2,1,0:T(8,128)(2,1)} %shard_map.101), calls=%async_computation.2 | async-start | bytes 1048576 | tf_op jit(solution)/shard_map/all_to_all | solution.py:380
  95.0 0.0 collective-permute-done.11.got_ref
  95.0 0.7 shard_map.104
  95.7 13.5 %all-to-all-done.2.got_ref = bf16[4,256,256]{2,1,0:T(8,128)(2,1)S(1)} async-done(((bf16[4,256,256]{2,1,0:T(8,128)(2,1)}), bf16[4,256,256]{2,1,0:T(8,128)(2,1)S(1)}, u32[]{:S(2)}, u32[]{:S(2)}) %all-to-all-start.2) | async-done | bytes 524320 | tf_op jit(solution)/shard_map/all_to_all | solution.py:380
  109.2 0.8 shard_map.102
  (1 shorter events, 0.0 us)
Async XLA Ops:
  0.6 10.5 %collective-permute-start = (bf16[128,256]{1,0:T(8,128)(2,1)}, bf16[128,256]{1,0:T(8,128)(2,1)S(1)}, u32[]{:S(2)}, u32[]{:S(2)}) collective-permute-start(bf16[128,256]{1,0:T(8,128)(2,1)} %b_ref.3), channel_id=1, source_target_pairs={{0,1},{1,0},{2,3},{3,2},{4,5},{5,4},{6,7},{7,6},{8,9},{9,8},{10,11... | collective-permute-start | bytes 196616 | tf_op jit(solution)/shard_map/ppermute | solution.py:329
  5.1 7.3 %collective-permute-start.1 = (bf16[128,256]{1,0:T(8,128)(2,1)}, bf16[128,256]{1,0:T(8,128)(2,1)S(1)}, u32[]{:S(2)}, u32[]{:S(2)}) collective-permute-start(bf16[128,256]{1,0:T(8,128)(2,1)} %c_ref.3), channel_id=1, source_target_pairs={{0,1},{1,0},{2,3},{3,2},{4,5},{5,4},{6,7},{7,6},{8,9},{9,8},{10,11... | collective-permute-start | bytes 196616 | tf_op jit(solution)/shard_map/ppermute | solution.py:329
  11.1 16.8 %copy-start.6 = (bf16[256,1024]{1,0:T(8,128)(2,1)S(1)}, bf16[256,1024]{1,0:T(8,128)(2,1)}, u32[]{:S(2)}) copy-start(bf16[256,1024]{1,0:T(8,128)(2,1)} %get-tuple-element.73) | copy-start | bytes 1572868
  11.1 21.5 %copy-start.5 = (bf16[256,1024]{1,0:T(8,128)(2,1)S(1)}, bf16[256,1024]{1,0:T(8,128)(2,1)}, u32[]{:S(2)}) copy-start(bf16[256,1024]{1,0:T(8,128)(2,1)} %get-tuple-element.74) | copy-start | bytes 1572868
  13.5 29.0 %all-to-all-start = ((bf16[32,8,1152]{2,1,0:T(8,128)(2,1)}), bf16[32,8,1152]{2,1,0:T(8,128)(2,1)S(1)}, u32[]{:S(2)}, u32[]{:S(2)}) async-start(bf16[32,8,1152]{2,1,0:T(8,128)(2,1)} %bitcast.9), calls=%async_computation | async-start | bytes 1179648 | tf_op jit(solution)/shard_map/all_to_all | solution.py:346
  24.6 23.8 %collective-permute-start.2 = (bf16[256,1024]{1,0:T(8,128)(2,1)}, bf16[256,1024]{1,0:T(8,128)(2,1)S(1)}, u32[]{:S(2)}, u32[]{:S(2)}) collective-permute-start(bf16[256,1024]{1,0:T(8,128)(2,1)} %get-tuple-element.72), channel_id=1, source_target_pairs={{0,4},{4,8},{8,12},{12,0},{1,5},{5,9},{9,13},{13,1},{2,6},{6,10},{... | collective-permute-start | bytes 1572872 | tf_op jit(solution)/shard_map/ppermute | solution.py:323
  28.0 26.1 %collective-permute-start.3 = (bf16[256,1024]{1,0:T(8,128)(2,1)S(1)}, bf16[256,1024]{1,0:T(8,128)(2,1)S(1)}, u32[]{:S(2)}, u32[]{:S(2)}) collective-permute-start(bf16[256,1024]{1,0:T(8,128)(2,1)S(1)} %copy-done.6), channel_id=1, source_target_pairs={{0,8},{4,12},{8,0},{12,4},{1,9},{5,13},{9,1},{13,5},{2,10},{6,14},... | collective-permute-start | bytes 1572872 | tf_op jit(solution)/shard_map/ppermute | solution.py:323
  32.6 22.8 %collective-permute-start.4 = (bf16[256,1024]{1,0:T(8,128)(2,1)S(1)}, bf16[256,1024]{1,0:T(8,128)(2,1)S(1)}, u32[]{:S(2)}, u32[]{:S(2)}) collective-permute-start(bf16[256,1024]{1,0:T(8,128)(2,1)S(1)} %copy-done.5), channel_id=1, source_target_pairs={{0,12},{4,0},{8,4},{12,8},{1,13},{5,1},{9,5},{13,9},{2,14},{6,2},{... | collective-permute-start | bytes 1572872 | tf_op jit(solution)/shard_map/ppermute | solution.py:323
  43.6 21.4 %all-to-all-start.1 = ((bf16[32,8,1024]{2,1,0:T(8,128)(2,1)}), bf16[32,8,1024]{2,1,0:T(8,128)(2,1)S(1)}, u32[]{:S(2)}, u32[]{:S(2)}) async-start(bf16[32,8,1024]{2,1,0:T(8,128)(2,1)} %bitcast.10), calls=%async_computation.1 | async-start | bytes 1048576 | tf_op jit(solution)/shard_map/all_to_all | solution.py:355
  55.4 26.9 %copy-start = (bf16[256,1024]{1,0:T(8,128)(2,1)}, bf16[256,1024]{1,0:T(8,128)(2,1)S(1)}, u32[]{:S(2)}) copy-start(bf16[256,1024]{1,0:T(8,128)(2,1)S(1)} %get-tuple-element.85.refs_0_) | copy-start | bytes 1572868
  55.4 26.9 %copy-start.1 = (bf16[256,1024]{1,0:T(8,128)(2,1)}, bf16[256,1024]{1,0:T(8,128)(2,1)S(1)}, u32[]{:S(2)}) copy-start(bf16[256,1024]{1,0:T(8,128)(2,1)S(1)} %get-tuple-element.86.refs_1_) | copy-start | bytes 1572868
  55.4 26.9 %copy-start.2 = (bf16[256,1024]{1,0:T(8,128)(2,1)}, bf16[256,1024]{1,0:T(8,128)(2,1)S(1)}, u32[]{:S(2)}) copy-start(bf16[256,1024]{1,0:T(8,128)(2,1)S(1)} %get-tuple-element.87.refs_2_) | copy-start | bytes 1572868
  55.4 6.3 %collective-permute-start.5 = (bf16[256,1024]{1,0:T(8,128)(2,1)S(1)}, bf16[256,1024]{1,0:T(8,128)(2,1)S(1)}, u32[]{:S(2)}, u32[]{:S(2)}) collective-permute-start(bf16[256,1024]{1,0:T(8,128)(2,1)S(1)} %get-tuple-element.85.refs_0_), channel_id=1, source_target_pairs={{0,16},{16,0},{1,17},{17,1},{2,18},{18,2},{3,19},{19,3},{4,20},{20... | collective-permute-start | bytes 1572872 | tf_op jit(solution)/shard_map/ppermute | solution.py:326
  57.4 4.4 %collective-permute-start.6 = (bf16[256,1024]{1,0:T(8,128)(2,1)S(1)}, bf16[256,1024]{1,0:T(8,128)(2,1)S(1)}, u32[]{:S(2)}, u32[]{:S(2)}) collective-permute-start(bf16[256,1024]{1,0:T(8,128)(2,1)S(1)} %get-tuple-element.86.refs_1_), channel_id=1, source_target_pairs={{0,16},{16,0},{1,17},{17,1},{2,18},{18,2},{3,19},{19,3},{4,20},{20... | collective-permute-start | bytes 1572872 | tf_op jit(solution)/shard_map/ppermute | solution.py:326
  59.8 3.9 %collective-permute-start.7 = (bf16[256,1024]{1,0:T(8,128)(2,1)S(1)}, bf16[256,1024]{1,0:T(8,128)(2,1)}, u32[]{:S(2)}, u32[]{:S(2)}) collective-permute-start(bf16[256,1024]{1,0:T(8,128)(2,1)S(1)} %get-tuple-element.87.refs_2_), channel_id=1, source_target_pairs={{0,16},{16,0},{1,17},{17,1},{2,18},{18,2},{3,19},{19,3},{4,20},{20... | collective-permute-start | bytes 1572872 | tf_op jit(solution)/shard_map/ppermute | solution.py:326
  61.7 20.7 %copy-start.3 = (bf16[256,1024]{1,0:T(8,128)(2,1)}, bf16[256,1024]{1,0:T(8,128)(2,1)S(1)}, u32[]{:S(2)}) copy-start(bf16[256,1024]{1,0:T(8,128)(2,1)S(1)} %collective-permute-done.5.refs_3_) | copy-start | bytes 1572868
  61.7 20.7 %copy-start.4 = (bf16[256,1024]{1,0:T(8,128)(2,1)}, bf16[256,1024]{1,0:T(8,128)(2,1)S(1)}, u32[]{:S(2)}) copy-start(bf16[256,1024]{1,0:T(8,128)(2,1)S(1)} %collective-permute-done.6.refs_4_) | copy-start | bytes 1572868
  66.5 18.7 %collective-permute-start.10 = (bf16[256,512]{1,0:T(8,128)(2,1)S(1)}, bf16[256,512]{1,0:T(8,128)(2,1)S(1)}, u32[]{:S(2)}, u32[]{:S(2)}) collective-permute-start(bf16[256,512]{1,0:T(8,128)(2,1)S(1)} %shard_map.99.refs_0_), channel_id=1, source_target_pairs={{0,12},{4,0},{8,4},{12,8},{1,13},{5,1},{9,5},{13,9},{2,14},{6,2},{... | collective-permute-start | bytes 786440 | tf_op jit(solution)/shard_map/ppermute | solution.py:323
  71.0 16.7 %collective-permute-start.8 = (bf16[256,512]{1,0:T(8,128)(2,1)S(1)}, bf16[256,512]{1,0:T(8,128)(2,1)S(1)}, u32[]{:S(2)}, u32[]{:S(2)}) collective-permute-start(bf16[256,512]{1,0:T(8,128)(2,1)S(1)} %shard_map.99.refs_0_), channel_id=1, source_target_pairs={{0,4},{4,8},{8,12},{12,0},{1,5},{5,9},{9,13},{13,1},{2,6},{6,10},{... | collective-permute-start | bytes 786440 | tf_op jit(solution)/shard_map/ppermute | solution.py:323
  72.9 14.7 %collective-permute-start.9 = (bf16[256,512]{1,0:T(8,128)(2,1)S(1)}, bf16[256,512]{1,0:T(8,128)(2,1)S(1)}, u32[]{:S(2)}, u32[]{:S(2)}) collective-permute-start(bf16[256,512]{1,0:T(8,128)(2,1)S(1)} %shard_map.99.refs_0_), channel_id=1, source_target_pairs={{0,8},{4,12},{8,0},{12,4},{1,9},{5,13},{9,1},{13,5},{2,10},{6,14},... | collective-permute-start | bytes 786440 | tf_op jit(solution)/shard_map/ppermute | solution.py:323
  78.7 16.3 %collective-permute-start.11 = (bf16[256,256]{1,0:T(8,128)(2,1)S(1)}, bf16[256,256]{1,0:T(8,128)(2,1)S(1)}, u32[]{:S(2)}, u32[]{:S(2)}) collective-permute-start(bf16[256,256]{1,0:T(8,128)(2,1)S(1)} %get-tuple-element.100), channel_id=1, source_target_pairs={{0,1},{1,0},{2,3},{3,2},{4,5},{5,4},{6,7},{7,6},{8,9},{9,8},{10,11... | collective-permute-start | bytes 393224 | tf_op jit(solution)/shard_map/ppermute | solution.py:370
  89.7 19.5 %all-to-all-start.2 = ((bf16[4,256,256]{2,1,0:T(8,128)(2,1)}), bf16[4,256,256]{2,1,0:T(8,128)(2,1)S(1)}, u32[]{:S(2)}, u32[]{:S(2)}) async-start(bf16[4,256,256]{2,1,0:T(8,128)(2,1)} %shard_map.101), calls=%async_computation.2 | async-start | bytes 1048576 | tf_op jit(solution)/shard_map/all_to_all | solution.py:380

commit v6 on v5

--- a/solution.py
+++ b/solution.py
@@ -163,21 +163,29 @@
     return jnp.concatenate([own_ref[...], other], axis=0)
 
 
+def pieces_out(source, target, at, sems, first):
+    rows = source.shape[0] // 4
+    parts = [slice(k * rows, (k + 1) * rows) for k in range(4)]
+    return [pltpu.make_async_copy(source.at[r, at], target.at[r, at], sems.at[first + k]) for k, r in enumerate(parts)]
+
+
 def ends_body(b_ref, c_ref, other_b, other_c, wx_ref, wdy_ref, ext_ref, send_hbm, send_ref, sems):
-    parts = [slice(0, COLS), slice(COLS, 2 * COLS + 128)]
-    copies = [pltpu.make_async_copy(send_ref.at[:, at], send_hbm.at[:, at], sems.at[i]) for i, at in enumerate(parts)]
+    early = pieces_out(send_ref, send_hbm, slice(0, COLS), sems, 0)
+    late = pieces_out(send_ref, send_hbm, slice(COLS, 2 * COLS + 128), sems, 4)
     send_ref[:, :COLS] = dot(whole(b_ref, other_b[...]), wx_ref[...], 1, 0).astype(BF16)
-    copies[0].start()
+    for copy in early:
+        copy.start()
     send_ref[:, COLS : 2 * COLS] = dot(whole(c_ref, other_c[...]), wdy_ref[...], 1, 0).astype(BF16)
     send_ref[:, 2 * COLS :] = jnp.broadcast_to(ext_ref[...], (STATE, 128)).astype(BF16)
-    copies[1].start()
-    for copy in copies:
+    for copy in late:
+        copy.start()
+    for copy in early + late:
         copy.wait()
 
 
 def scan_body(got_ref, out_hbm, out_ref, decay_ref, sems):
-    halves = [slice(0, COLS), slice(COLS, 2 * COLS)]
-    copies = [pltpu.make_async_copy(out_ref.at[:, at], out_hbm.at[:, at], sems.at[i]) for i, at in enumerate(halves)]
+    early = pieces_out(out_ref, out_hbm, slice(0, COLS), sems, 0)
+    late = pieces_out(out_ref, out_hbm, slice(COLS, 2 * COLS), sems, 4)
     decay_ref[...] = expanded(got_ref[:, 2 * COLS :])
     two = 2 * LINES
 
@@ -192,7 +200,8 @@
         after = state * decay[:LINES] + term[:LINES]
         out_ref[at, :COLS] = jnp.concatenate([state, after], axis=0).astype(BF16)
         state = after * decay[LINES:] + term[LINES:]
-    copies[0].start()
+    for copy in early:
+        copy.start()
     state = jnp.zeros((LINES, COLS), F32)
     for c in range(BLOCKS // 2 - 1, -1, -1):
         at = place(c)
@@ -200,8 +209,9 @@
         before = state * decay[LINES:] + term[LINES:]
         out_ref[at, COLS:] = jnp.concatenate([before, state], axis=0).astype(BF16)
         state = before * decay[:LINES] + term[:LINES]
-    copies[1].start()
-    for copy in copies:
+    for copy in late:
+        copy.start()
+    for copy in early + late:
         copy.wait()
 
 
@@ -341,7 +351,7 @@
         out_spaces="vvvhvvvhhhhhh",
     )(where, x_in, grad_out, step_size, log_decay, b_proj, c_proj, w_in)
     ends = ((STATE, 2 * COLS + 128), BF16)
-    (send,) = call(ends_body, "vvvvvvv", [ends], [ends], copies=2, out_spaces="h")(b_own, c_own, *bc, wx, wdy, ext)
+    (send,) = call(ends_body, "vvvvvvv", [ends], [ends], copies=8, out_spaces="h")(b_own, c_own, *bc, wx, wdy, ext)
 
     terms = lax.all_to_all(send, EXCHANGE, 0, 0, tiled=True)
     w_next, w_prev, w_far, bc, _ = hold((w_next, w_prev, w_far, bc, send))
@@ -351,7 +361,7 @@
     )(x_in, grad_out, b_proj, c_proj, *bc, run, cols)
     terms, local_x, b_rows, mixed = hold((terms, local_x, b_rows, mixed))
     both = ((STATE, 2 * COLS), BF16)
-    (scanned,) = call(scan_body, "v", [both], [both, ((STATE, COLS), F32)], copies=2, out_spaces="h")(terms)
+    (scanned,) = call(scan_body, "v", [both], [both, ((STATE, COLS), F32)], copies=8, out_spaces="h")(terms)
     states = lax.all_to_all(scanned, EXCHANGE, 0, 0, tiled=True)
     w_prev, w_far, w_next, _ = hold((w_prev, w_far, w_next, scanned))
     w_mine = passed(w_prev, w_far, w_next)

time: 111 us -> 111 us (level)
  no operation moved by 1% of the time
where the time goes in v6:
time: 111 us; the launch traced here: 110 us
  starting transfers between devices  59.8 us (54%)
  waiting for transfers between devices  31.1 us (28%)
  Pallas kernels  18.2 us (16%)
    ppermute x6, starting transfers between devices, ahead_on_x(): return lax.ppermute(shard, 'x', [(i, (i + ahead) % 4) for i in range(4)])  22 us
    pallas_call x10, Pallas kernels, pinned(): run(*(pltpu.with_memory_space_constraint(a, PLACES[k]) if k in PLACES els...  18.2 us
    all_to_all x1, waiting for transfers between devices, per_device(): over_y = lax.all_to_all(partial, 'yh', 0, 0, tiled=True)  13.5 us
    all_to_all x1, starting transfers between devices, per_device(): terms = lax.all_to_all(send, EXCHANGE, 0, 0, tiled=True)  11 us
    ppermute x6, waiting for transfers between devices, ahead_on_x(): return lax.ppermute(shard, 'x', [(i, (i + ahead) % 4) for i in range(4)])  9.46 us
    ppermute x2, starting transfers between devices, per_device(): bc = (lax.ppermute(b_proj, 'yh', flip), lax.ppermute(c_proj, 'yh', flip))  6.75 us
    ppermute x3, starting transfers between devices, other_core(): return lax.ppermute(shard, 'core', [(0, 1), (1, 0)])  6.24 us
    all_to_all x1, starting transfers between devices, per_device(): over_y = lax.all_to_all(partial, 'yh', 0, 0, tiled=True)  5.36 us
  transfers between devices with their start and end apart: 15, of which 8 were waited for; matrix products, arithmetic and copies ran while one was open for 0% of the time, Pallas kernels for 13%

profile of v6, /device:TPU:72, one launch (start us, length us, event | category | flops | bytes accessed | tf_op | source)
XLA Modules:
  0.0 110.1 jit_solution(4985256380942312539)
XLA Ops:
  0.6 4.5 %collective-permute-start = (bf16[128,256]{1,0:T(8,128)(2,1)}, bf16[128,256]{1,0:T(8,128)(2,1)S(1)}, u32[]{:S(2)}, u32[]{:S(2)}) collective-permute-start(bf16[128,256]{1,0:T(8,128)(2,1)} %b_ref.3), channel_id=1, source_target_pairs={{0,1},{1,0},{2,3},{3,2},{4,5},{5,4},{6,7},{7,6},{8,9},{9,8},{10,11... | collective-permute-start | bytes 196616 | tf_op jit(solution)/shard_map/ppermute | solution.py:339
  5.1 2.2 %collective-permute-start.1 = (bf16[128,256]{1,0:T(8,128)(2,1)}, bf16[128,256]{1,0:T(8,128)(2,1)S(1)}, u32[]{:S(2)}, u32[]{:S(2)}) collective-permute-start(bf16[128,256]{1,0:T(8,128)(2,1)} %c_ref.3), channel_id=1, source_target_pairs={{0,1},{1,0},{2,3},{3,2},{4,5},{5,4},{6,7},{7,6},{8,9},{9,8},{10,11... | collective-permute-start | bytes 196616 | tf_op jit(solution)/shard_map/ppermute | solution.py:339
  7.4 0.1 pad_add_fusion.where_ref
  7.5 3.7 %shard_map.94 = (bf16[256,512]{1,0:T(8,128)(2,1)S(1)}, bf16[256,512]{1,0:T(8,128)(2,1)S(1)}, f32[8,256]{1,0:T(8,128)S(1)}, f32[256,128]{1,0:T(8,128)}, f32[1,128...) custom-call(s32[2]{0:T(128)S(1)} %pad_add_fusion.where_ref, ...), custom_call_target="tpu_custom_call" | custom-call | flops 1000000000 | bytes 1048576 | tf_op jit(solution)/shard_map/pallas_call | solution.py:53
  11.1 0.0 copy-start.6
  11.1 0.0 copy-start.5
  11.2 0.0 collective-permute-done.other_b
  11.2 1.2 %collective-permute-done.1.other_c = bf16[128,256]{1,0:T(8,128)(2,1)S(1)} collective-permute-done((bf16[128,256]{1,0:T(8,128)(2,1)}, bf16[128,256]{1,0:T(8,128)(2,1)S(1)}, u32[]{:S(2)}, u32[]{:S(2)}) %collective-permute-start.1) | collective-permute-done | bytes 65568 | tf_op jit(solution)/shard_map/ppermute | solution.py:339
  12.4 1.2 %shard_map.95 = bf16[256,1152]{1,0:T(8,128)(2,1)} custom-call(bf16[128,256]{1,0:T(8,128)(2,1)S(1)} %get-tuple-element.53.b_ref, bf16[128,256]{1,0:T(8,128)(2,1)S(1)} %get-tuple-element.54.c_ref, bf16[128,256]{1,0:T(8,128)(2,1)S(1)} %collective-permute-done.other_b, bf16[128,256]{1,0:T(8,128)(2,1)S(1)} %collective-permute-done.1.other_c, ...), custom_call_target="tpu_custom_call" | custom-call | flops 1000000000 | bytes 1048576 | tf_op jit(solution)/shard_map/pallas_call | solution.py:53
  13.6 11.0 %all-to-all-start = ((bf16[32,8,1152]{2,1,0:T(8,128)(2,1)}), bf16[32,8,1152]{2,1,0:T(8,128)(2,1)S(1)}, u32[]{:S(2)}, u32[]{:S(2)}) async-start(bf16[32,8,1152]{2,1,0:T(8,128)(2,1)} %bitcast.9), calls=%async_computation | async-start | bytes 1179648 | tf_op jit(solution)/shard_map/all_to_all | solution.py:356
  24.6 3.4 %collective-permute-start.2 = (bf16[256,1024]{1,0:T(8,128)(2,1)}, bf16[256,1024]{1,0:T(8,128)(2,1)S(1)}, u32[]{:S(2)}, u32[]{:S(2)}) collective-permute-start(bf16[256,1024]{1,0:T(8,128)(2,1)} %get-tuple-element.72), channel_id=1, source_target_pairs={{0,4},{4,8},{8,12},{12,0},{1,5},{5,9},{9,13},{13,1},{2,6},{6,10},{... | collective-permute-start | bytes 1572872 | tf_op jit(solution)/shard_map/ppermute | solution.py:333
  28.0 0.0 copy-done.6
  28.0 4.6 %collective-permute-start.3 = (bf16[256,1024]{1,0:T(8,128)(2,1)S(1)}, bf16[256,1024]{1,0:T(8,128)(2,1)S(1)}, u32[]{:S(2)}, u32[]{:S(2)}) collective-permute-start(bf16[256,1024]{1,0:T(8,128)(2,1)S(1)} %copy-done.6), channel_id=1, source_target_pairs={{0,8},{4,12},{8,0},{12,4},{1,9},{5,13},{9,1},{13,5},{2,10},{6,14},... | collective-permute-start | bytes 1572872 | tf_op jit(solution)/shard_map/ppermute | solution.py:333
  32.7 0.0 copy-done.5
  32.7 3.3 %collective-permute-start.4 = (bf16[256,1024]{1,0:T(8,128)(2,1)S(1)}, bf16[256,1024]{1,0:T(8,128)(2,1)S(1)}, u32[]{:S(2)}, u32[]{:S(2)}) collective-permute-start(bf16[256,1024]{1,0:T(8,128)(2,1)S(1)} %copy-done.5), channel_id=1, source_target_pairs={{0,12},{4,0},{8,4},{12,8},{1,13},{5,1},{9,5},{13,9},{2,14},{6,2},{... | collective-permute-start | bytes 1572872 | tf_op jit(solution)/shard_map/ppermute | solution.py:333
  36.0 3.0 %shard_map.96 = (bf16[256,512]{1,0:T(8,128)(2,1)}, bf16[256,256]{1,0:T(8,128)(2,1)}, bf16[256,256]{1,0:T(8,128)(2,1)}) custom-call(bf16[256,512]{1,0:T(8,128)(2,1)} %x_ref.1, bf16[256,512]{1,0:T(8,128)(2,1)} %dy_ref.1, bf16[128,256]{1,0:T(8,128)(2,1)} %b_ref.3, bf16[128,256]{1,0:T(8,128)(2,1)} %c_ref.3, bf16[128,256]{1,0:T(8,128)(2,1)S(1)} %collective-permute-done.other_b, ...), custom_call_target="tpu_custom_call" | custom-call | flops 1000000000 | bytes 1048576 | tf_op jit(solution)/shard_map/pallas_call | solution.py:53
  39.0 3.6 %all-to-all-done = bf16[32,8,1152]{2,1,0:T(8,128)(2,1)S(1)} async-done(((bf16[32,8,1152]{2,1,0:T(8,128)(2,1)}), bf16[32,8,1152]{2,1,0:T(8,128)(2,1)S(1)}, u32[]{:S(2)}, u32[]{:S(2)}) %all-to-all-start) | async-done | bytes 589856 | tf_op jit(solution)/shard_map/all_to_all | solution.py:356
  42.6 1.1 %shard_map.97 = bf16[256,1024]{1,0:T(8,128)(2,1)} custom-call(bf16[256,1152]{1,0:T(8,128)(2,1)S(1)} %bitcast.6), custom_call_target="tpu_custom_call" | custom-call | flops 1000000000 | bytes 1048576 | tf_op jit(solution)/shard_map/pallas_call | solution.py:53
  43.7 4.8 %all-to-all-start.1 = ((bf16[32,8,1024]{2,1,0:T(8,128)(2,1)}), bf16[32,8,1024]{2,1,0:T(8,128)(2,1)S(1)}, u32[]{:S(2)}, u32[]{:S(2)}) async-start(bf16[32,8,1024]{2,1,0:T(8,128)(2,1)} %bitcast.10), calls=%async_computation.1 | async-start | bytes 1048576 | tf_op jit(solution)/shard_map/all_to_all | solution.py:365
  48.5 0.0 collective-permute-done.2.refs_0_
  48.5 5.6 %collective-permute-done.3.refs_1_ = bf16[256,1024]{1,0:T(8,128)(2,1)S(1)} collective-permute-done((bf16[256,1024]{1,0:T(8,128)(2,1)S(1)}, bf16[256,1024]{1,0:T(8,128)(2,1)S(1)}, u32[]{:S(2)}, u32[]{:S(2)}) %collective-permute-start.3) | collective-permute-done | bytes 524320 | tf_op jit(solution)/shard_map/ppermute | solution.py:333
  54.1 1.4 %collective-permute-done.4.refs_2_ = bf16[256,1024]{1,0:T(8,128)(2,1)S(1)} collective-permute-done((bf16[256,1024]{1,0:T(8,128)(2,1)S(1)}, bf16[256,1024]{1,0:T(8,128)(2,1)S(1)}, u32[]{:S(2)}, u32[]{:S(2)}) %collective-permute-start.4) | collective-permute-done | bytes 524320 | tf_op jit(solution)/shard_map/ppermute | solution.py:333
  55.5 0.0 copy-start
  55.5 0.0 copy-start.1
  55.5 0.0 copy-start.2
  55.5 1.9 %collective-permute-start.5 = (bf16[256,1024]{1,0:T(8,128)(2,1)S(1)}, bf16[256,1024]{1,0:T(8,128)(2,1)S(1)}, u32[]{:S(2)}, u32[]{:S(2)}) collective-permute-start(bf16[256,1024]{1,0:T(8,128)(2,1)S(1)} %get-tuple-element.85.refs_0_), channel_id=1, source_target_pairs={{0,16},{16,0},{1,17},{17,1},{2,18},{18,2},{3,19},{19,3},{4,20},{20... | collective-permute-start | bytes 1572872 | tf_op jit(solution)/shard_map/ppermute | solution.py:336
  57.4 2.4 %collective-permute-start.6 = (bf16[256,1024]{1,0:T(8,128)(2,1)S(1)}, bf16[256,1024]{1,0:T(8,128)(2,1)S(1)}, u32[]{:S(2)}, u32[]{:S(2)}) collective-permute-start(bf16[256,1024]{1,0:T(8,128)(2,1)S(1)} %get-tuple-element.86.refs_1_), channel_id=1, source_target_pairs={{0,16},{16,0},{1,17},{17,1},{2,18},{18,2},{3,19},{19,3},{4,20},{20... | collective-permute-start | bytes 1572872 | tf_op jit(solution)/shard_map/ppermute | solution.py:336
  59.8 1.9 %collective-permute-start.7 = (bf16[256,1024]{1,0:T(8,128)(2,1)S(1)}, bf16[256,1024]{1,0:T(8,128)(2,1)}, u32[]{:S(2)}, u32[]{:S(2)}) collective-permute-start(bf16[256,1024]{1,0:T(8,128)(2,1)S(1)} %get-tuple-element.87.refs_2_), channel_id=1, source_target_pairs={{0,16},{16,0},{1,17},{17,1},{2,18},{18,2},{3,19},{19,3},{4,20},{20... | collective-permute-start | bytes 1572872 | tf_op jit(solution)/shard_map/ppermute | solution.py:336
  61.8 0.0 collective-permute-done.5.refs_3_
  61.8 0.0 copy-start.3
  61.8 0.0 collective-permute-done.6.refs_4_
  61.8 0.0 copy-start.4
  61.8 2.0 %collective-permute-done.7.refs_5_ = bf16[256,1024]{1,0:T(8,128)(2,1)} collective-permute-done((bf16[256,1024]{1,0:T(8,128)(2,1)S(1)}, bf16[256,1024]{1,0:T(8,128)(2,1)}, u32[]{:S(2)}, u32[]{:S(2)}) %collective-permute-start.7) | collective-permute-done | bytes 524320 | tf_op jit(solution)/shard_map/ppermute | solution.py:336
  63.8 1.3 %all-to-all-done.1 = bf16[32,8,1024]{2,1,0:T(8,128)(2,1)S(1)} async-done(((bf16[32,8,1024]{2,1,0:T(8,128)(2,1)}), bf16[32,8,1024]{2,1,0:T(8,128)(2,1)S(1)}, u32[]{:S(2)}, u32[]{:S(2)}) %all-to-all-start.1) | async-done | bytes 524320 | tf_op jit(solution)/shard_map/all_to_all | solution.py:365
  65.1 1.4 %shard_map.99.refs_0_ = bf16[256,512]{1,0:T(8,128)(2,1)S(1)} custom-call(bf16[256,256]{1,0:T(8,128)(2,1)} %get-tuple-element.68.bt_hbm, f32[8,256]{1,0:T(8,128)} %get-tuple-element.69.fwd_hbm, bf16[256,512]{1,0:T(8,128)(2,1)} %get-tuple-element.70.loc_hbm, bf16[256,1024]{1,0:T(8,128)(2,1)S(1)} %bitcast.7), custom_call_target="tpu_custom_call" | custom-call | flops 1000000000 | bytes 1048576 | tf_op jit(solution)/shard_map/pallas_call | solution.py:53
  66.6 4.5 %collective-permute-start.10 = (bf16[256,512]{1,0:T(8,128)(2,1)S(1)}, bf16[256,512]{1,0:T(8,128)(2,1)S(1)}, u32[]{:S(2)}, u32[]{:S(2)}) collective-permute-start(bf16[256,512]{1,0:T(8,128)(2,1)S(1)} %shard_map.99.refs_0_), channel_id=1, source_target_pairs={{0,12},{4,0},{8,4},{12,8},{1,13},{5,1},{9,5},{13,9},{2,14},{6,2},{... | collective-permute-start | bytes 786440 | tf_op jit(solution)/shard_map/ppermute | solution.py:333
  71.1 1.9 %collective-permute-start.8 = (bf16[256,512]{1,0:T(8,128)(2,1)S(1)}, bf16[256,512]{1,0:T(8,128)(2,1)S(1)}, u32[]{:S(2)}, u32[]{:S(2)}) collective-permute-start(bf16[256,512]{1,0:T(8,128)(2,1)S(1)} %shard_map.99.refs_0_), channel_id=1, source_target_pairs={{0,4},{4,8},{8,12},{12,0},{1,5},{5,9},{9,13},{13,1},{2,6},{6,10},{... | collective-permute-start | bytes 786440 | tf_op jit(solution)/shard_map/ppermute | solution.py:333
  73.0 4.2 %collective-permute-start.9 = (bf16[256,512]{1,0:T(8,128)(2,1)S(1)}, bf16[256,512]{1,0:T(8,128)(2,1)S(1)}, u32[]{:S(2)}, u32[]{:S(2)}) collective-permute-start(bf16[256,512]{1,0:T(8,128)(2,1)S(1)} %shard_map.99.refs_0_), channel_id=1, source_target_pairs={{0,8},{4,12},{8,0},{12,4},{1,9},{5,13},{9,1},{13,5},{2,10},{6,14},... | collective-permute-start | bytes 786440 | tf_op jit(solution)/shard_map/ppermute | solution.py:333
  77.2 1.6 %shard_map.103 = (bf16[256,256]{1,0:T(8,128)(2,1)S(1)}, bf16[256,256]{1,0:T(8,128)(2,1)S(1)}) custom-call(bf16[128,256]{1,0:T(8,128)(2,1)} %b_ref.3, bf16[128,256]{1,0:T(8,128)(2,1)} %c_ref.3, bf16[128,256]{1,0:T(8,128)(2,1)S(1)} %collective-permute-done.other_b, bf16[128,256]{1,0:T(8,128)(2,1)S(1)} %collective-permute-done.1.other_c, ...), custom_call_target="tpu_custom_call" | custom-call | flops 1000000000 | bytes 1048576 | tf_op jit(solution)/shard_map/pallas_call | solution.py:53
  78.8 3.7 %collective-permute-start.11 = (bf16[256,256]{1,0:T(8,128)(2,1)S(1)}, bf16[256,256]{1,0:T(8,128)(2,1)S(1)}, u32[]{:S(2)}, u32[]{:S(2)}) collective-permute-start(bf16[256,256]{1,0:T(8,128)(2,1)S(1)} %get-tuple-element.100), channel_id=1, source_target_pairs={{0,1},{1,0},{2,3},{3,2},{4,5},{5,4},{6,7},{7,6},{8,9},{9,8},{10,11... | collective-permute-start | bytes 393224 | tf_op jit(solution)/shard_map/ppermute | solution.py:380
  82.5 0.0 copy-done
  82.5 0.0 copy-done.1
  82.5 0.0 copy-done.2
  82.5 0.0 copy-done.3
  82.5 0.0 copy-done.4
  82.5 2.8 %shard_map.100.w_ref = bf16[2048,1024]{1,0:T(8,128)(2,1)S(1)} custom-call(s32[2]{0:T(128)S(1)} %pad_add_fusion.where_ref, bf16[512,4096]{1,0:T(8,128)(2,1)} %w_hbm.3, bf16[256,1024]{1,0:T(8,128)(2,1)} %copy-done, bf16[256,1024]{1,0:T(8,128)(2,1)} %copy-done.1, bf16[256,1024]{1,0:T(8,128)(2,1)} %copy-done.2, bf16[256,1024]{1,0:T(8,128)(2,1)} %copy-done.3, ...), custom_call_target="tpu_custom_call" | custom-call | flops 1000000000 | bytes 1048576 | tf_op jit(solution)/shard_map/pallas_call | solution.py:53
  85.3 0.0 collective-permute-done.10.refs_3_
  85.3 2.5 %collective-permute-done.8.refs_1_ = bf16[256,512]{1,0:T(8,128)(2,1)S(1)} collective-permute-done((bf16[256,512]{1,0:T(8,128)(2,1)S(1)}, bf16[256,512]{1,0:T(8,128)(2,1)S(1)}, u32[]{:S(2)}, u32[]{:S(2)}) %collective-permute-start.8) | collective-permute-done | bytes 262176 | tf_op jit(solution)/shard_map/ppermute | solution.py:333
  87.8 0.0 collective-permute-done.9.refs_2_
  87.8 2.0 %shard_map.101 = bf16[4,256,256]{2,1,0:T(8,128)(2,1)} custom-call(bf16[2048,1024]{1,0:T(8,128)(2,1)S(1)} %shard_map.100.w_ref, bf16[256,512]{1,0:T(8,128)(2,1)S(1)} %shard_map.99.refs_0_, bf16[256,512]{1,0:T(8,128)(2,1)S(1)} %collective-permute-done.8.refs_1_, bf16[256,512]{1,0:T(8,128)(2,1)S(1)} %collective-permute-done.9.refs_2_, ...), custom_call_target="tpu_custom_call" | custom-call | flops 1000000000 | bytes 1048576 | tf_op jit(solution)/shard_map/pallas_call | solution.py:53
  89.8 5.4 %all-to-all-start.2 = ((bf16[4,256,256]{2,1,0:T(8,128)(2,1)}), bf16[4,256,256]{2,1,0:T(8,128)(2,1)S(1)}, u32[]{:S(2)}, u32[]{:S(2)}) async-start(bf16[4,256,256]{2,1,0:T(8,128)(2,1)} %shard_map.101), calls=%async_computation.2 | async-start | bytes 1048576 | tf_op jit(solution)/shard_map/all_to_all | solution.py:390
  95.1 0.0 collective-permute-done.11.got_ref
  95.1 0.7 shard_map.104
  95.8 13.5 %all-to-all-done.2.got_ref = bf16[4,256,256]{2,1,0:T(8,128)(2,1)S(1)} async-done(((bf16[4,256,256]{2,1,0:T(8,128)(2,1)}), bf16[4,256,256]{2,1,0:T(8,128)(2,1)S(1)}, u32[]{:S(2)}, u32[]{:S(2)}) %all-to-all-start.2) | async-done | bytes 524320 | tf_op jit(solution)/shard_map/all_to_all | solution.py:390
  109.3 0.8 shard_map.102
  (1 shorter events, 0.0 us)
Async XLA Ops:
  0.6 10.5 %collective-permute-start = (bf16[128,256]{1,0:T(8,128)(2,1)}, bf16[128,256]{1,0:T(8,128)(2,1)S(1)}, u32[]{:S(2)}, u32[]{:S(2)}) collective-permute-start(bf16[128,256]{1,0:T(8,128)(2,1)} %b_ref.3), channel_id=1, source_target_pairs={{0,1},{1,0},{2,3},{3,2},{4,5},{5,4},{6,7},{7,6},{8,9},{9,8},{10,11... | collective-permute-start | bytes 196616 | tf_op jit(solution)/shard_map/ppermute | solution.py:339
  5.1 7.3 %collective-permute-start.1 = (bf16[128,256]{1,0:T(8,128)(2,1)}, bf16[128,256]{1,0:T(8,128)(2,1)S(1)}, u32[]{:S(2)}, u32[]{:S(2)}) collective-permute-start(bf16[128,256]{1,0:T(8,128)(2,1)} %c_ref.3), channel_id=1, source_target_pairs={{0,1},{1,0},{2,3},{3,2},{4,5},{5,4},{6,7},{7,6},{8,9},{9,8},{10,11... | collective-permute-start | bytes 196616 | tf_op jit(solution)/shard_map/ppermute | solution.py:339
  11.1 16.9 %copy-start.6 = (bf16[256,1024]{1,0:T(8,128)(2,1)S(1)}, bf16[256,1024]{1,0:T(8,128)(2,1)}, u32[]{:S(2)}) copy-start(bf16[256,1024]{1,0:T(8,128)(2,1)} %get-tuple-element.73) | copy-start | bytes 1572868
  11.1 21.5 %copy-start.5 = (bf16[256,1024]{1,0:T(8,128)(2,1)S(1)}, bf16[256,1024]{1,0:T(8,128)(2,1)}, u32[]{:S(2)}) copy-start(bf16[256,1024]{1,0:T(8,128)(2,1)} %get-tuple-element.74) | copy-start | bytes 1572868
  13.6 29.0 %all-to-all-start = ((bf16[32,8,1152]{2,1,0:T(8,128)(2,1)}), bf16[32,8,1152]{2,1,0:T(8,128)(2,1)S(1)}, u32[]{:S(2)}, u32[]{:S(2)}) async-start(bf16[32,8,1152]{2,1,0:T(8,128)(2,1)} %bitcast.9), calls=%async_computation | async-start | bytes 1179648 | tf_op jit(solution)/shard_map/all_to_all | solution.py:356
  24.6 23.9 %collective-permute-start.2 = (bf16[256,1024]{1,0:T(8,128)(2,1)}, bf16[256,1024]{1,0:T(8,128)(2,1)S(1)}, u32[]{:S(2)}, u32[]{:S(2)}) collective-permute-start(bf16[256,1024]{1,0:T(8,128)(2,1)} %get-tuple-element.72), channel_id=1, source_target_pairs={{0,4},{4,8},{8,12},{12,0},{1,5},{5,9},{9,13},{13,1},{2,6},{6,10},{... | collective-permute-start | bytes 1572872 | tf_op jit(solution)/shard_map/ppermute | solution.py:333
  28.0 26.1 %collective-permute-start.3 = (bf16[256,1024]{1,0:T(8,128)(2,1)S(1)}, bf16[256,1024]{1,0:T(8,128)(2,1)S(1)}, u32[]{:S(2)}, u32[]{:S(2)}) collective-permute-start(bf16[256,1024]{1,0:T(8,128)(2,1)S(1)} %copy-done.6), channel_id=1, source_target_pairs={{0,8},{4,12},{8,0},{12,4},{1,9},{5,13},{9,1},{13,5},{2,10},{6,14},... | collective-permute-start | bytes 1572872 | tf_op jit(solution)/shard_map/ppermute | solution.py:333
  32.7 22.8 %collective-permute-start.4 = (bf16[256,1024]{1,0:T(8,128)(2,1)S(1)}, bf16[256,1024]{1,0:T(8,128)(2,1)S(1)}, u32[]{:S(2)}, u32[]{:S(2)}) collective-permute-start(bf16[256,1024]{1,0:T(8,128)(2,1)S(1)} %copy-done.5), channel_id=1, source_target_pairs={{0,12},{4,0},{8,4},{12,8},{1,13},{5,1},{9,5},{13,9},{2,14},{6,2},{... | collective-permute-start | bytes 1572872 | tf_op jit(solution)/shard_map/ppermute | solution.py:333
  43.7 21.4 %all-to-all-start.1 = ((bf16[32,8,1024]{2,1,0:T(8,128)(2,1)}), bf16[32,8,1024]{2,1,0:T(8,128)(2,1)S(1)}, u32[]{:S(2)}, u32[]{:S(2)}) async-start(bf16[32,8,1024]{2,1,0:T(8,128)(2,1)} %bitcast.10), calls=%async_computation.1 | async-start | bytes 1048576 | tf_op jit(solution)/shard_map/all_to_all | solution.py:365
  55.5 27.0 %copy-start = (bf16[256,1024]{1,0:T(8,128)(2,1)}, bf16[256,1024]{1,0:T(8,128)(2,1)S(1)}, u32[]{:S(2)}) copy-start(bf16[256,1024]{1,0:T(8,128)(2,1)S(1)} %get-tuple-element.85.refs_0_) | copy-start | bytes 1572868
  55.5 27.0 %copy-start.1 = (bf16[256,1024]{1,0:T(8,128)(2,1)}, bf16[256,1024]{1,0:T(8,128)(2,1)S(1)}, u32[]{:S(2)}) copy-start(bf16[256,1024]{1,0:T(8,128)(2,1)S(1)} %get-tuple-element.86.refs_1_) | copy-start | bytes 1572868
  55.5 27.0 %copy-start.2 = (bf16[256,1024]{1,0:T(8,128)(2,1)}, bf16[256,1024]{1,0:T(8,128)(2,1)S(1)}, u32[]{:S(2)}) copy-start(bf16[256,1024]{1,0:T(8,128)(2,1)S(1)} %get-tuple-element.87.refs_2_) | copy-start | bytes 1572868
  55.5 6.3 %collective-permute-start.5 = (bf16[256,1024]{1,0:T(8,128)(2,1)S(1)}, bf16[256,1024]{1,0:T(8,128)(2,1)S(1)}, u32[]{:S(2)}, u32[]{:S(2)}) collective-permute-start(bf16[256,1024]{1,0:T(8,128)(2,1)S(1)} %get-tuple-element.85.refs_0_), channel_id=1, source_target_pairs={{0,16},{16,0},{1,17},{17,1},{2,18},{18,2},{3,19},{19,3},{4,20},{20... | collective-permute-start | bytes 1572872 | tf_op jit(solution)/shard_map/ppermute | solution.py:336
  57.4 4.4 %collective-permute-start.6 = (bf16[256,1024]{1,0:T(8,128)(2,1)S(1)}, bf16[256,1024]{1,0:T(8,128)(2,1)S(1)}, u32[]{:S(2)}, u32[]{:S(2)}) collective-permute-start(bf16[256,1024]{1,0:T(8,128)(2,1)S(1)} %get-tuple-element.86.refs_1_), channel_id=1, source_target_pairs={{0,16},{16,0},{1,17},{17,1},{2,18},{18,2},{3,19},{19,3},{4,20},{20... | collective-permute-start | bytes 1572872 | tf_op jit(solution)/shard_map/ppermute | solution.py:336
  59.8 3.9 %collective-permute-start.7 = (bf16[256,1024]{1,0:T(8,128)(2,1)S(1)}, bf16[256,1024]{1,0:T(8,128)(2,1)}, u32[]{:S(2)}, u32[]{:S(2)}) collective-permute-start(bf16[256,1024]{1,0:T(8,128)(2,1)S(1)} %get-tuple-element.87.refs_2_), channel_id=1, source_target_pairs={{0,16},{16,0},{1,17},{17,1},{2,18},{18,2},{3,19},{19,3},{4,20},{20... | collective-permute-start | bytes 1572872 | tf_op jit(solution)/shard_map/ppermute | solution.py:336
  61.8 20.7 %copy-start.3 = (bf16[256,1024]{1,0:T(8,128)(2,1)}, bf16[256,1024]{1,0:T(8,128)(2,1)S(1)}, u32[]{:S(2)}) copy-start(bf16[256,1024]{1,0:T(8,128)(2,1)S(1)} %collective-permute-done.5.refs_3_) | copy-start | bytes 1572868
  61.8 20.7 %copy-start.4 = (bf16[256,1024]{1,0:T(8,128)(2,1)}, bf16[256,1024]{1,0:T(8,128)(2,1)S(1)}, u32[]{:S(2)}) copy-start(bf16[256,1024]{1,0:T(8,128)(2,1)S(1)} %collective-permute-done.6.refs_4_) | copy-start | bytes 1572868
  66.6 18.7 %collective-permute-start.10 = (bf16[256,512]{1,0:T(8,128)(2,1)S(1)}, bf16[256,512]{1,0:T(8,128)(2,1)S(1)}, u32[]{:S(2)}, u32[]{:S(2)}) collective-permute-start(bf16[256,512]{1,0:T(8,128)(2,1)S(1)} %shard_map.99.refs_0_), channel_id=1, source_target_pairs={{0,12},{4,0},{8,4},{12,8},{1,13},{5,1},{9,5},{13,9},{2,14},{6,2},{... | collective-permute-start | bytes 786440 | tf_op jit(solution)/shard_map/ppermute | solution.py:333
  71.1 16.7 %collective-permute-start.8 = (bf16[256,512]{1,0:T(8,128)(2,1)S(1)}, bf16[256,512]{1,0:T(8,128)(2,1)S(1)}, u32[]{:S(2)}, u32[]{:S(2)}) collective-permute-start(bf16[256,512]{1,0:T(8,128)(2,1)S(1)} %shard_map.99.refs_0_), channel_id=1, source_target_pairs={{0,4},{4,8},{8,12},{12,0},{1,5},{5,9},{9,13},{13,1},{2,6},{6,10},{... | collective-permute-start | bytes 786440 | tf_op jit(solution)/shard_map/ppermute | solution.py:333
  73.0 14.7 %collective-permute-start.9 = (bf16[256,512]{1,0:T(8,128)(2,1)S(1)}, bf16[256,512]{1,0:T(8,128)(2,1)S(1)}, u32[]{:S(2)}, u32[]{:S(2)}) collective-permute-start(bf16[256,512]{1,0:T(8,128)(2,1)S(1)} %shard_map.99.refs_0_), channel_id=1, source_target_pairs={{0,8},{4,12},{8,0},{12,4},{1,9},{5,13},{9,1},{13,5},{2,10},{6,14},... | collective-permute-start | bytes 786440 | tf_op jit(solution)/shard_map/ppermute | solution.py:333
  78.8 16.3 %collective-permute-start.11 = (bf16[256,256]{1,0:T(8,128)(2,1)S(1)}, bf16[256,256]{1,0:T(8,128)(2,1)S(1)}, u32[]{:S(2)}, u32[]{:S(2)}) collective-permute-start(bf16[256,256]{1,0:T(8,128)(2,1)S(1)} %get-tuple-element.100), channel_id=1, source_target_pairs={{0,1},{1,0},{2,3},{3,2},{4,5},{5,4},{6,7},{7,6},{8,9},{9,8},{10,11... | collective-permute-start | bytes 393224 | tf_op jit(solution)/shard_map/ppermute | solution.py:380
  89.8 19.5 %all-to-all-start.2 = ((bf16[4,256,256]{2,1,0:T(8,128)(2,1)}), bf16[4,256,256]{2,1,0:T(8,128)(2,1)S(1)}, u32[]{:S(2)}, u32[]{:S(2)}) async-start(bf16[4,256,256]{2,1,0:T(8,128)(2,1)} %shard_map.101), calls=%async_computation.2 | async-start | bytes 1048576 | tf_op jit(solution)/shard_map/all_to_all | solution.py:390

commit v7 on v5

--- a/solution.py
+++ b/solution.py
@@ -354,7 +354,8 @@
     (scanned,) = call(scan_body, "v", [both], [both, ((STATE, COLS), F32)], copies=2, out_spaces="h")(terms)
     states = lax.all_to_all(scanned, EXCHANGE, 0, 0, tiled=True)
     w_prev, w_far, w_next, _ = hold((w_prev, w_far, w_next, scanned))
-    w_mine = passed(w_prev, w_far, w_next)
+    w_prev, w_next, w_far = passed(w_prev, w_next, w_far)
+    w_mine = [w_prev, w_far, w_next]
     w_theirs = [other_core(w) for w in w_mine]
     states, w_mine, w_theirs = hold((states, w_mine, w_theirs))
 

time: 111 us -> 111 us (level)
  no operation moved by 1% of the time
where the time goes in v7:
time: 111 us; the launch traced here: 110 us
  starting transfers between devices  59.8 us (54%)
  waiting for transfers between devices  31 us (28%)
  Pallas kernels  18 us (16%)
    ppermute x6, starting transfers between devices, ahead_on_x(): return lax.ppermute(shard, 'x', [(i, (i + ahead) % 4) for i in range(4)])  22 us
    pallas_call x10, Pallas kernels, pinned(): run(*(pltpu.with_memory_space_constraint(a, PLACES[k]) if k in PLACES els...  18 us
    all_to_all x1, waiting for transfers between devices, per_device(): over_y = lax.all_to_all(partial, 'yh', 0, 0, tiled=True)  13.5 us
    all_to_all x1, starting transfers between devices, per_device(): terms = lax.all_to_all(send, EXCHANGE, 0, 0, tiled=True)  11 us
    ppermute x6, waiting for transfers between devices, ahead_on_x(): return lax.ppermute(shard, 'x', [(i, (i + ahead) % 4) for i in range(4)])  9.51 us
    ppermute x2, starting transfers between devices, per_device(): bc = (lax.ppermute(b_proj, 'yh', flip), lax.ppermute(c_proj, 'yh', flip))  6.75 us
    ppermute x3, starting transfers between devices, other_core(): return lax.ppermute(shard, 'core', [(0, 1), (1, 0)])  6.24 us
    all_to_all x1, starting transfers between devices, per_device(): over_y = lax.all_to_all(partial, 'yh', 0, 0, tiled=True)  5.37 us
  transfers between devices with their start and end apart: 15, of which 8 were waited for; matrix products, arithmetic and copies ran while one was open for 0% of the time, Pallas kernels for 13%

profile of v7, /device:TPU:72, one launch (start us, length us, event | category | flops | bytes accessed | tf_op | source)
XLA Modules:
  0.0 109.9 jit_solution(16549696615832284091)
XLA Ops:
  0.6 4.5 %collective-permute-start = (bf16[128,256]{1,0:T(8,128)(2,1)}, bf16[128,256]{1,0:T(8,128)(2,1)S(1)}, u32[]{:S(2)}, u32[]{:S(2)}) collective-permute-start(bf16[128,256]{1,0:T(8,128)(2,1)} %b_ref.3), channel_id=1, source_target_pairs={{0,1},{1,0},{2,3},{3,2},{4,5},{5,4},{6,7},{7,6},{8,9},{9,8},{10,11... | collective-permute-start | bytes 196616 | tf_op jit(solution)/shard_map/ppermute | solution.py:329
  5.1 2.2 %collective-permute-start.1 = (bf16[128,256]{1,0:T(8,128)(2,1)}, bf16[128,256]{1,0:T(8,128)(2,1)S(1)}, u32[]{:S(2)}, u32[]{:S(2)}) collective-permute-start(bf16[128,256]{1,0:T(8,128)(2,1)} %c_ref.3), channel_id=1, source_target_pairs={{0,1},{1,0},{2,3},{3,2},{4,5},{5,4},{6,7},{7,6},{8,9},{9,8},{10,11... | collective-permute-start | bytes 196616 | tf_op jit(solution)/shard_map/ppermute | solution.py:329
  7.4 0.1 pad_add_fusion.where_ref
  7.5 3.7 %shard_map.94 = (bf16[256,512]{1,0:T(8,128)(2,1)S(1)}, bf16[256,512]{1,0:T(8,128)(2,1)S(1)}, f32[8,256]{1,0:T(8,128)S(1)}, f32[256,128]{1,0:T(8,128)}, f32[1,128...) custom-call(s32[2]{0:T(128)S(1)} %pad_add_fusion.where_ref, ...), custom_call_target="tpu_custom_call" | custom-call | flops 1000000000 | bytes 1048576 | tf_op jit(solution)/shard_map/pallas_call | solution.py:53
  11.1 0.0 copy-start.6
  11.1 0.0 copy-start.5
  11.2 0.0 collective-permute-done.other_b
  11.2 1.2 %collective-permute-done.1.other_c = bf16[128,256]{1,0:T(8,128)(2,1)S(1)} collective-permute-done((bf16[128,256]{1,0:T(8,128)(2,1)}, bf16[128,256]{1,0:T(8,128)(2,1)S(1)}, u32[]{:S(2)}, u32[]{:S(2)}) %collective-permute-start.1) | collective-permute-done | bytes 65568 | tf_op jit(solution)/shard_map/ppermute | solution.py:329
  12.4 1.1 %shard_map.95 = bf16[256,1152]{1,0:T(8,128)(2,1)} custom-call(bf16[128,256]{1,0:T(8,128)(2,1)S(1)} %get-tuple-element.53.b_ref, bf16[128,256]{1,0:T(8,128)(2,1)S(1)} %get-tuple-element.54.c_ref, bf16[128,256]{1,0:T(8,128)(2,1)S(1)} %collective-permute-done.other_b, bf16[128,256]{1,0:T(8,128)(2,1)S(1)} %collective-permute-done.1.other_c, ...), custom_call_target="tpu_custom_call" | custom-call | flops 1000000000 | bytes 1048576 | tf_op jit(solution)/shard_map/pallas_call | solution.py:53
  13.5 11.0 %all-to-all-start = ((bf16[32,8,1152]{2,1,0:T(8,128)(2,1)}), bf16[32,8,1152]{2,1,0:T(8,128)(2,1)S(1)}, u32[]{:S(2)}, u32[]{:S(2)}) async-start(bf16[32,8,1152]{2,1,0:T(8,128)(2,1)} %bitcast.9), calls=%async_computation | async-start | bytes 1179648 | tf_op jit(solution)/shard_map/all_to_all | solution.py:346
  24.6 3.4 %collective-permute-start.2 = (bf16[256,1024]{1,0:T(8,128)(2,1)}, bf16[256,1024]{1,0:T(8,128)(2,1)S(1)}, u32[]{:S(2)}, u32[]{:S(2)}) collective-permute-start(bf16[256,1024]{1,0:T(8,128)(2,1)} %get-tuple-element.72), channel_id=1, source_target_pairs={{0,4},{4,8},{8,12},{12,0},{1,5},{5,9},{9,13},{13,1},{2,6},{6,10},{... | collective-permute-start | bytes 1572872 | tf_op jit(solution)/shard_map/ppermute | solution.py:323
  28.0 0.0 copy-done.6
  28.0 4.6 %collective-permute-start.3 = (bf16[256,1024]{1,0:T(8,128)(2,1)S(1)}, bf16[256,1024]{1,0:T(8,128)(2,1)S(1)}, u32[]{:S(2)}, u32[]{:S(2)}) collective-permute-start(bf16[256,1024]{1,0:T(8,128)(2,1)S(1)} %copy-done.6), channel_id=1, source_target_pairs={{0,8},{4,12},{8,0},{12,4},{1,9},{5,13},{9,1},{13,5},{2,10},{6,14},... | collective-permute-start | bytes 1572872 | tf_op jit(solution)/shard_map/ppermute | solution.py:323
  32.6 0.0 copy-done.5
  32.6 3.3 %collective-permute-start.4 = (bf16[256,1024]{1,0:T(8,128)(2,1)S(1)}, bf16[256,1024]{1,0:T(8,128)(2,1)S(1)}, u32[]{:S(2)}, u32[]{:S(2)}) collective-permute-start(bf16[256,1024]{1,0:T(8,128)(2,1)S(1)} %copy-done.5), channel_id=1, source_target_pairs={{0,12},{4,0},{8,4},{12,8},{1,13},{5,1},{9,5},{13,9},{2,14},{6,2},{... | collective-permute-start | bytes 1572872 | tf_op jit(solution)/shard_map/ppermute | solution.py:323
  36.0 3.0 %shard_map.96 = (bf16[256,512]{1,0:T(8,128)(2,1)}, bf16[256,256]{1,0:T(8,128)(2,1)}, bf16[256,256]{1,0:T(8,128)(2,1)}) custom-call(bf16[256,512]{1,0:T(8,128)(2,1)} %x_ref.1, bf16[256,512]{1,0:T(8,128)(2,1)} %dy_ref.1, bf16[128,256]{1,0:T(8,128)(2,1)} %b_ref.3, bf16[128,256]{1,0:T(8,128)(2,1)} %c_ref.3, bf16[128,256]{1,0:T(8,128)(2,1)S(1)} %collective-permute-done.other_b, ...), custom_call_target="tpu_custom_call" | custom-call | flops 1000000000 | bytes 1048576 | tf_op jit(solution)/shard_map/pallas_call | solution.py:53
  39.0 3.6 %all-to-all-done = bf16[32,8,1152]{2,1,0:T(8,128)(2,1)S(1)} async-done(((bf16[32,8,1152]{2,1,0:T(8,128)(2,1)}), bf16[32,8,1152]{2,1,0:T(8,128)(2,1)S(1)}, u32[]{:S(2)}, u32[]{:S(2)}) %all-to-all-start) | async-done | bytes 589856 | tf_op jit(solution)/shard_map/all_to_all | solution.py:346
  42.5 1.1 shard_map.97
  43.6 4.8 %all-to-all-start.1 = ((bf16[32,8,1024]{2,1,0:T(8,128)(2,1)}), bf16[32,8,1024]{2,1,0:T(8,128)(2,1)S(1)}, u32[]{:S(2)}, u32[]{:S(2)}) async-start(bf16[32,8,1024]{2,1,0:T(8,128)(2,1)} %bitcast.10), calls=%async_computation.1 | async-start | bytes 1048576 | tf_op jit(solution)/shard_map/all_to_all | solution.py:355
  48.4 0.0 collective-permute-done.2.refs_0_
  48.4 5.7 %collective-permute-done.3.refs_2_ = bf16[256,1024]{1,0:T(8,128)(2,1)S(1)} collective-permute-done((bf16[256,1024]{1,0:T(8,128)(2,1)S(1)}, bf16[256,1024]{1,0:T(8,128)(2,1)S(1)}, u32[]{:S(2)}, u32[]{:S(2)}) %collective-permute-start.3) | collective-permute-done | bytes 524320 | tf_op jit(solution)/shard_map/ppermute | solution.py:323
  54.1 1.4 %collective-permute-done.4.refs_1_ = bf16[256,1024]{1,0:T(8,128)(2,1)S(1)} collective-permute-done((bf16[256,1024]{1,0:T(8,128)(2,1)S(1)}, bf16[256,1024]{1,0:T(8,128)(2,1)S(1)}, u32[]{:S(2)}, u32[]{:S(2)}) %collective-permute-start.4) | collective-permute-done | bytes 524320 | tf_op jit(solution)/shard_map/ppermute | solution.py:323
  55.4 0.0 copy-start
  55.4 0.0 copy-start.1
  55.4 0.0 copy-start.2
  55.4 1.9 %collective-permute-start.5 = (bf16[256,1024]{1,0:T(8,128)(2,1)S(1)}, bf16[256,1024]{1,0:T(8,128)(2,1)S(1)}, u32[]{:S(2)}, u32[]{:S(2)}) collective-permute-start(bf16[256,1024]{1,0:T(8,128)(2,1)S(1)} %get-tuple-element.85.refs_0_), channel_id=1, source_target_pairs={{0,16},{16,0},{1,17},{17,1},{2,18},{18,2},{3,19},{19,3},{4,20},{20... | collective-permute-start | bytes 1572872 | tf_op jit(solution)/shard_map/ppermute | solution.py:326
  57.4 2.4 %collective-permute-start.6 = (bf16[256,1024]{1,0:T(8,128)(2,1)S(1)}, bf16[256,1024]{1,0:T(8,128)(2,1)S(1)}, u32[]{:S(2)}, u32[]{:S(2)}) collective-permute-start(bf16[256,1024]{1,0:T(8,128)(2,1)S(1)} %get-tuple-element.86.refs_1_), channel_id=1, source_target_pairs={{0,16},{16,0},{1,17},{17,1},{2,18},{18,2},{3,19},{19,3},{4,20},{20... | collective-permute-start | bytes 1572872 | tf_op jit(solution)/shard_map/ppermute | solution.py:326
  59.8 1.9 %collective-permute-start.7 = (bf16[256,1024]{1,0:T(8,128)(2,1)S(1)}, bf16[256,1024]{1,0:T(8,128)(2,1)}, u32[]{:S(2)}, u32[]{:S(2)}) collective-permute-start(bf16[256,1024]{1,0:T(8,128)(2,1)S(1)} %get-tuple-element.87.refs_2_), channel_id=1, source_target_pairs={{0,16},{16,0},{1,17},{17,1},{2,18},{18,2},{3,19},{19,3},{4,20},{20... | collective-permute-start | bytes 1572872 | tf_op jit(solution)/shard_map/ppermute | solution.py:326
  61.7 0.0 collective-permute-done.5.refs_3_
  61.7 0.0 copy-start.3
  61.7 0.0 collective-permute-done.6.refs_4_
  61.7 0.0 copy-start.4
  61.8 2.0 %collective-permute-done.7.refs_5_ = bf16[256,1024]{1,0:T(8,128)(2,1)} collective-permute-done((bf16[256,1024]{1,0:T(8,128)(2,1)S(1)}, bf16[256,1024]{1,0:T(8,128)(2,1)}, u32[]{:S(2)}, u32[]{:S(2)}) %collective-permute-start.7) | collective-permute-done | bytes 524320 | tf_op jit(solution)/shard_map/ppermute | solution.py:326
  63.7 1.3 %all-to-all-done.1 = bf16[32,8,1024]{2,1,0:T(8,128)(2,1)S(1)} async-done(((bf16[32,8,1024]{2,1,0:T(8,128)(2,1)}), bf16[32,8,1024]{2,1,0:T(8,128)(2,1)S(1)}, u32[]{:S(2)}, u32[]{:S(2)}) %all-to-all-start.1) | async-done | bytes 524320 | tf_op jit(solution)/shard_map/all_to_all | solution.py:355
  65.0 1.4 %shard_map.99.refs_0_ = bf16[256,512]{1,0:T(8,128)(2,1)S(1)} custom-call(bf16[256,256]{1,0:T(8,128)(2,1)} %get-tuple-element.68.bt_hbm, f32[8,256]{1,0:T(8,128)} %get-tuple-element.69.fwd_hbm, bf16[256,512]{1,0:T(8,128)(2,1)} %get-tuple-element.70.loc_hbm, bf16[256,1024]{1,0:T(8,128)(2,1)S(1)} %bitcast.7), custom_call_target="tpu_custom_call" | custom-call | flops 1000000000 | bytes 1048576 | tf_op jit(solution)/shard_map/pallas_call | solution.py:53
  66.5 4.5 %collective-permute-start.10 = (bf16[256,512]{1,0:T(8,128)(2,1)S(1)}, bf16[256,512]{1,0:T(8,128)(2,1)S(1)}, u32[]{:S(2)}, u32[]{:S(2)}) collective-permute-start(bf16[256,512]{1,0:T(8,128)(2,1)S(1)} %shard_map.99.refs_0_), channel_id=1, source_target_pairs={{0,12},{4,0},{8,4},{12,8},{1,13},{5,1},{9,5},{13,9},{2,14},{6,2},{... | collective-permute-start | bytes 786440 | tf_op jit(solution)/shard_map/ppermute | solution.py:323
  71.0 1.9 %collective-permute-start.8 = (bf16[256,512]{1,0:T(8,128)(2,1)S(1)}, bf16[256,512]{1,0:T(8,128)(2,1)S(1)}, u32[]{:S(2)}, u32[]{:S(2)}) collective-permute-start(bf16[256,512]{1,0:T(8,128)(2,1)S(1)} %shard_map.99.refs_0_), channel_id=1, source_target_pairs={{0,4},{4,8},{8,12},{12,0},{1,5},{5,9},{9,13},{13,1},{2,6},{6,10},{... | collective-permute-start | bytes 786440 | tf_op jit(solution)/shard_map/ppermute | solution.py:323
  72.9 4.2 %collective-permute-start.9 = (bf16[256,512]{1,0:T(8,128)(2,1)S(1)}, bf16[256,512]{1,0:T(8,128)(2,1)S(1)}, u32[]{:S(2)}, u32[]{:S(2)}) collective-permute-start(bf16[256,512]{1,0:T(8,128)(2,1)S(1)} %shard_map.99.refs_0_), channel_id=1, source_target_pairs={{0,8},{4,12},{8,0},{12,4},{1,9},{5,13},{9,1},{13,5},{2,10},{6,14},... | collective-permute-start | bytes 786440 | tf_op jit(solution)/shard_map/ppermute | solution.py:323
  77.1 1.6 %shard_map.103 = (bf16[256,256]{1,0:T(8,128)(2,1)S(1)}, bf16[256,256]{1,0:T(8,128)(2,1)S(1)}) custom-call(bf16[128,256]{1,0:T(8,128)(2,1)} %b_ref.3, bf16[128,256]{1,0:T(8,128)(2,1)} %c_ref.3, bf16[128,256]{1,0:T(8,128)(2,1)S(1)} %collective-permute-done.other_b, bf16[128,256]{1,0:T(8,128)(2,1)S(1)} %collective-permute-done.1.other_c, ...), custom_call_target="tpu_custom_call" | custom-call | flops 1000000000 | bytes 1048576 | tf_op jit(solution)/shard_map/pallas_call | solution.py:53
  78.7 3.7 %collective-permute-start.11 = (bf16[256,256]{1,0:T(8,128)(2,1)S(1)}, bf16[256,256]{1,0:T(8,128)(2,1)S(1)}, u32[]{:S(2)}, u32[]{:S(2)}) collective-permute-start(bf16[256,256]{1,0:T(8,128)(2,1)S(1)} %get-tuple-element.100), channel_id=1, source_target_pairs={{0,1},{1,0},{2,3},{3,2},{4,5},{5,4},{6,7},{7,6},{8,9},{9,8},{10,11... | collective-permute-start | bytes 393224 | tf_op jit(solution)/shard_map/ppermute | solution.py:371
  82.4 0.0 copy-done
  82.4 0.0 copy-done.1
  82.4 0.0 copy-done.2
  82.4 0.0 copy-done.3
  82.4 0.0 copy-done.4
  82.4 2.8 %shard_map.100.w_ref = bf16[2048,1024]{1,0:T(8,128)(2,1)S(1)} custom-call(s32[2]{0:T(128)S(1)} %pad_add_fusion.where_ref, bf16[512,4096]{1,0:T(8,128)(2,1)} %w_hbm.3, bf16[256,1024]{1,0:T(8,128)(2,1)} %copy-done, bf16[256,1024]{1,0:T(8,128)(2,1)} %copy-done.1, bf16[256,1024]{1,0:T(8,128)(2,1)} %copy-done.2, bf16[256,1024]{1,0:T(8,128)(2,1)} %copy-done.3, ...), custom_call_target="tpu_custom_call" | custom-call | flops 1000000000 | bytes 1048576 | tf_op jit(solution)/shard_map/pallas_call | solution.py:53
  85.2 0.0 collective-permute-done.10.refs_3_
  85.2 2.5 %collective-permute-done.8.refs_1_ = bf16[256,512]{1,0:T(8,128)(2,1)S(1)} collective-permute-done((bf16[256,512]{1,0:T(8,128)(2,1)S(1)}, bf16[256,512]{1,0:T(8,128)(2,1)S(1)}, u32[]{:S(2)}, u32[]{:S(2)}) %collective-permute-start.8) | collective-permute-done | bytes 262176 | tf_op jit(solution)/shard_map/ppermute | solution.py:323
  87.7 0.0 collective-permute-done.9.refs_2_
  87.7 2.0 %shard_map.101 = bf16[4,256,256]{2,1,0:T(8,128)(2,1)} custom-call(bf16[2048,1024]{1,0:T(8,128)(2,1)S(1)} %shard_map.100.w_ref, bf16[256,512]{1,0:T(8,128)(2,1)S(1)} %shard_map.99.refs_0_, bf16[256,512]{1,0:T(8,128)(2,1)S(1)} %collective-permute-done.8.refs_1_, bf16[256,512]{1,0:T(8,128)(2,1)S(1)} %collective-permute-done.9.refs_2_, ...), custom_call_target="tpu_custom_call" | custom-call | flops 1000000000 | bytes 1048576 | tf_op jit(solution)/shard_map/pallas_call | solution.py:53
  89.7 5.4 %all-to-all-start.2 = ((bf16[4,256,256]{2,1,0:T(8,128)(2,1)}), bf16[4,256,256]{2,1,0:T(8,128)(2,1)S(1)}, u32[]{:S(2)}, u32[]{:S(2)}) async-start(bf16[4,256,256]{2,1,0:T(8,128)(2,1)} %shard_map.101), calls=%async_computation.2 | async-start | bytes 1048576 | tf_op jit(solution)/shard_map/all_to_all | solution.py:381
  95.0 0.0 collective-permute-done.11.got_ref
  95.0 0.7 shard_map.104
  95.7 13.5 %all-to-all-done.2.got_ref = bf16[4,256,256]{2,1,0:T(8,128)(2,1)S(1)} async-done(((bf16[4,256,256]{2,1,0:T(8,128)(2,1)}), bf16[4,256,256]{2,1,0:T(8,128)(2,1)S(1)}, u32[]{:S(2)}, u32[]{:S(2)}) %all-to-all-start.2) | async-done | bytes 524320 | tf_op jit(solution)/shard_map/all_to_all | solution.py:381
  109.2 0.8 shard_map.102
  (1 shorter events, 0.0 us)
Async XLA Ops:
  0.6 10.5 %collective-permute-start = (bf16[128,256]{1,0:T(8,128)(2,1)}, bf16[128,256]{1,0:T(8,128)(2,1)S(1)}, u32[]{:S(2)}, u32[]{:S(2)}) collective-permute-start(bf16[128,256]{1,0:T(8,128)(2,1)} %b_ref.3), channel_id=1, source_target_pairs={{0,1},{1,0},{2,3},{3,2},{4,5},{5,4},{6,7},{7,6},{8,9},{9,8},{10,11... | collective-permute-start | bytes 196616 | tf_op jit(solution)/shard_map/ppermute | solution.py:329
  5.1 7.3 %collective-permute-start.1 = (bf16[128,256]{1,0:T(8,128)(2,1)}, bf16[128,256]{1,0:T(8,128)(2,1)S(1)}, u32[]{:S(2)}, u32[]{:S(2)}) collective-permute-start(bf16[128,256]{1,0:T(8,128)(2,1)} %c_ref.3), channel_id=1, source_target_pairs={{0,1},{1,0},{2,3},{3,2},{4,5},{5,4},{6,7},{7,6},{8,9},{9,8},{10,11... | collective-permute-start | bytes 196616 | tf_op jit(solution)/shard_map/ppermute | solution.py:329
  11.1 16.8 %copy-start.6 = (bf16[256,1024]{1,0:T(8,128)(2,1)S(1)}, bf16[256,1024]{1,0:T(8,128)(2,1)}, u32[]{:S(2)}) copy-start(bf16[256,1024]{1,0:T(8,128)(2,1)} %get-tuple-element.73) | copy-start | bytes 1572868
  11.1 21.5 %copy-start.5 = (bf16[256,1024]{1,0:T(8,128)(2,1)S(1)}, bf16[256,1024]{1,0:T(8,128)(2,1)}, u32[]{:S(2)}) copy-start(bf16[256,1024]{1,0:T(8,128)(2,1)} %get-tuple-element.74) | copy-start | bytes 1572868
  13.5 29.0 %all-to-all-start = ((bf16[32,8,1152]{2,1,0:T(8,128)(2,1)}), bf16[32,8,1152]{2,1,0:T(8,128)(2,1)S(1)}, u32[]{:S(2)}, u32[]{:S(2)}) async-start(bf16[32,8,1152]{2,1,0:T(8,128)(2,1)} %bitcast.9), calls=%async_computation | async-start | bytes 1179648 | tf_op jit(solution)/shard_map/all_to_all | solution.py:346
  24.6 23.8 %collective-permute-start.2 = (bf16[256,1024]{1,0:T(8,128)(2,1)}, bf16[256,1024]{1,0:T(8,128)(2,1)S(1)}, u32[]{:S(2)}, u32[]{:S(2)}) collective-permute-start(bf16[256,1024]{1,0:T(8,128)(2,1)} %get-tuple-element.72), channel_id=1, source_target_pairs={{0,4},{4,8},{8,12},{12,0},{1,5},{5,9},{9,13},{13,1},{2,6},{6,10},{... | collective-permute-start | bytes 1572872 | tf_op jit(solution)/shard_map/ppermute | solution.py:323
  28.0 26.1 %collective-permute-start.3 = (bf16[256,1024]{1,0:T(8,128)(2,1)S(1)}, bf16[256,1024]{1,0:T(8,128)(2,1)S(1)}, u32[]{:S(2)}, u32[]{:S(2)}) collective-permute-start(bf16[256,1024]{1,0:T(8,128)(2,1)S(1)} %copy-done.6), channel_id=1, source_target_pairs={{0,8},{4,12},{8,0},{12,4},{1,9},{5,13},{9,1},{13,5},{2,10},{6,14},... | collective-permute-start | bytes 1572872 | tf_op jit(solution)/shard_map/ppermute | solution.py:323
  32.6 22.8 %collective-permute-start.4 = (bf16[256,1024]{1,0:T(8,128)(2,1)S(1)}, bf16[256,1024]{1,0:T(8,128)(2,1)S(1)}, u32[]{:S(2)}, u32[]{:S(2)}) collective-permute-start(bf16[256,1024]{1,0:T(8,128)(2,1)S(1)} %copy-done.5), channel_id=1, source_target_pairs={{0,12},{4,0},{8,4},{12,8},{1,13},{5,1},{9,5},{13,9},{2,14},{6,2},{... | collective-permute-start | bytes 1572872 | tf_op jit(solution)/shard_map/ppermute | solution.py:323
  43.6 21.4 %all-to-all-start.1 = ((bf16[32,8,1024]{2,1,0:T(8,128)(2,1)}), bf16[32,8,1024]{2,1,0:T(8,128)(2,1)S(1)}, u32[]{:S(2)}, u32[]{:S(2)}) async-start(bf16[32,8,1024]{2,1,0:T(8,128)(2,1)} %bitcast.10), calls=%async_computation.1 | async-start | bytes 1048576 | tf_op jit(solution)/shard_map/all_to_all | solution.py:355
  55.4 26.9 %copy-start = (bf16[256,1024]{1,0:T(8,128)(2,1)}, bf16[256,1024]{1,0:T(8,128)(2,1)S(1)}, u32[]{:S(2)}) copy-start(bf16[256,1024]{1,0:T(8,128)(2,1)S(1)} %get-tuple-element.85.refs_0_) | copy-start | bytes 1572868
  55.4 26.9 %copy-start.1 = (bf16[256,1024]{1,0:T(8,128)(2,1)}, bf16[256,1024]{1,0:T(8,128)(2,1)S(1)}, u32[]{:S(2)}) copy-start(bf16[256,1024]{1,0:T(8,128)(2,1)S(1)} %get-tuple-element.86.refs_1_) | copy-start | bytes 1572868
  55.4 26.9 %copy-start.2 = (bf16[256,1024]{1,0:T(8,128)(2,1)}, bf16[256,1024]{1,0:T(8,128)(2,1)S(1)}, u32[]{:S(2)}) copy-start(bf16[256,1024]{1,0:T(8,128)(2,1)S(1)} %get-tuple-element.87.refs_2_) | copy-start | bytes 1572868
  55.4 6.3 %collective-permute-start.5 = (bf16[256,1024]{1,0:T(8,128)(2,1)S(1)}, bf16[256,1024]{1,0:T(8,128)(2,1)S(1)}, u32[]{:S(2)}, u32[]{:S(2)}) collective-permute-start(bf16[256,1024]{1,0:T(8,128)(2,1)S(1)} %get-tuple-element.85.refs_0_), channel_id=1, source_target_pairs={{0,16},{16,0},{1,17},{17,1},{2,18},{18,2},{3,19},{19,3},{4,20},{20... | collective-permute-start | bytes 1572872 | tf_op jit(solution)/shard_map/ppermute | solution.py:326
  57.4 4.4 %collective-permute-start.6 = (bf16[256,1024]{1,0:T(8,128)(2,1)S(1)}, bf16[256,1024]{1,0:T(8,128)(2,1)S(1)}, u32[]{:S(2)}, u32[]{:S(2)}) collective-permute-start(bf16[256,1024]{1,0:T(8,128)(2,1)S(1)} %get-tuple-element.86.refs_1_), channel_id=1, source_target_pairs={{0,16},{16,0},{1,17},{17,1},{2,18},{18,2},{3,19},{19,3},{4,20},{20... | collective-permute-start | bytes 1572872 | tf_op jit(solution)/shard_map/ppermute | solution.py:326
  59.8 3.9 %collective-permute-start.7 = (bf16[256,1024]{1,0:T(8,128)(2,1)S(1)}, bf16[256,1024]{1,0:T(8,128)(2,1)}, u32[]{:S(2)}, u32[]{:S(2)}) collective-permute-start(bf16[256,1024]{1,0:T(8,128)(2,1)S(1)} %get-tuple-element.87.refs_2_), channel_id=1, source_target_pairs={{0,16},{16,0},{1,17},{17,1},{2,18},{18,2},{3,19},{19,3},{4,20},{20... | collective-permute-start | bytes 1572872 | tf_op jit(solution)/shard_map/ppermute | solution.py:326
  61.7 20.7 %copy-start.3 = (bf16[256,1024]{1,0:T(8,128)(2,1)}, bf16[256,1024]{1,0:T(8,128)(2,1)S(1)}, u32[]{:S(2)}) copy-start(bf16[256,1024]{1,0:T(8,128)(2,1)S(1)} %collective-permute-done.5.refs_3_) | copy-start | bytes 1572868
  61.7 20.7 %copy-start.4 = (bf16[256,1024]{1,0:T(8,128)(2,1)}, bf16[256,1024]{1,0:T(8,128)(2,1)S(1)}, u32[]{:S(2)}) copy-start(bf16[256,1024]{1,0:T(8,128)(2,1)S(1)} %collective-permute-done.6.refs_4_) | copy-start | bytes 1572868
  66.5 18.7 %collective-permute-start.10 = (bf16[256,512]{1,0:T(8,128)(2,1)S(1)}, bf16[256,512]{1,0:T(8,128)(2,1)S(1)}, u32[]{:S(2)}, u32[]{:S(2)}) collective-permute-start(bf16[256,512]{1,0:T(8,128)(2,1)S(1)} %shard_map.99.refs_0_), channel_id=1, source_target_pairs={{0,12},{4,0},{8,4},{12,8},{1,13},{5,1},{9,5},{13,9},{2,14},{6,2},{... | collective-permute-start | bytes 786440 | tf_op jit(solution)/shard_map/ppermute | solution.py:323
  71.0 16.7 %collective-permute-start.8 = (bf16[256,512]{1,0:T(8,128)(2,1)S(1)}, bf16[256,512]{1,0:T(8,128)(2,1)S(1)}, u32[]{:S(2)}, u32[]{:S(2)}) collective-permute-start(bf16[256,512]{1,0:T(8,128)(2,1)S(1)} %shard_map.99.refs_0_), channel_id=1, source_target_pairs={{0,4},{4,8},{8,12},{12,0},{1,5},{5,9},{9,13},{13,1},{2,6},{6,10},{... | collective-permute-start | bytes 786440 | tf_op jit(solution)/shard_map/ppermute | solution.py:323
  72.9 14.7 %collective-permute-start.9 = (bf16[256,512]{1,0:T(8,128)(2,1)S(1)}, bf16[256,512]{1,0:T(8,128)(2,1)S(1)}, u32[]{:S(2)}, u32[]{:S(2)}) collective-permute-start(bf16[256,512]{1,0:T(8,128)(2,1)S(1)} %shard_map.99.refs_0_), channel_id=1, source_target_pairs={{0,8},{4,12},{8,0},{12,4},{1,9},{5,13},{9,1},{13,5},{2,10},{6,14},... | collective-permute-start | bytes 786440 | tf_op jit(solution)/shard_map/ppermute | solution.py:323
  78.7 16.3 %collective-permute-start.11 = (bf16[256,256]{1,0:T(8,128)(2,1)S(1)}, bf16[256,256]{1,0:T(8,128)(2,1)S(1)}, u32[]{:S(2)}, u32[]{:S(2)}) collective-permute-start(bf16[256,256]{1,0:T(8,128)(2,1)S(1)} %get-tuple-element.100), channel_id=1, source_target_pairs={{0,1},{1,0},{2,3},{3,2},{4,5},{5,4},{6,7},{7,6},{8,9},{9,8},{10,11... | collective-permute-start | bytes 393224 | tf_op jit(solution)/shard_map/ppermute | solution.py:371
  89.7 19.5 %all-to-all-start.2 = ((bf16[4,256,256]{2,1,0:T(8,128)(2,1)}), bf16[4,256,256]{2,1,0:T(8,128)(2,1)S(1)}, u32[]{:S(2)}, u32[]{:S(2)}) async-start(bf16[4,256,256]{2,1,0:T(8,128)(2,1)} %shard_map.101), calls=%async_computation.2 | async-start | bytes 1048576 | tf_op jit(solution)/shard_map/all_to_all | solution.py:381
